TPU v7x, 32 devices: a whole 2x2x4 slice. The times are simulated.
32 devices in a mesh: row: 4 (over z), col: 2 (over x), depth: 4 (over y, core).
Axes of the slice: x: 2, y: 2, z: 4, core: 2. Of those that a mesh axis runs over, the one named last changes fastest.
Arguments:
- density: bfloat16 [2048, 2048], P('row', 'col'), as said below
Outputs:
- purified: float32 [2048, 2048], P('row', ('col', 'depth'))
Inputs may be any that keep to these rules, and one draw needn't show every extreme that they name: density is symmetric: density[i, j] == density[j, i] for every i and j, for any seed.
All inputs are finite; a program needn't handle non-finite values.
Results may differ from a plain program's by a relative error of at most 0.002.
Values may be sent and summed in bfloat16 or wider, within the bound.
No kernel may reach another device: no remote copies, remote signals or barrier semaphores. Data moves between devices by JAX's collectives and lax.ppermute only.
A program may use at most 64 MiB of HBM per device.

v0:
```python
import jax
import jax.numpy as jnp
from jax import lax
from jax.sharding import PartitionSpec as P


def on_device(density):
    rows_blk, cols_blk = density.shape
    depth_n = lax.axis_size("depth")
    strip_len = rows_blk // depth_n
    groups = cols_blk // rows_blk
    layer_idx = lax.axis_index("depth")
    col_strips = lax.dynamic_index_in_dim(
        density.reshape(rows_blk, groups, depth_n, strip_len), layer_idx, 2, keepdims=False
    ).reshape(rows_blk, groups * strip_len)
    row_strips = lax.dynamic_index_in_dim(
        density.reshape(depth_n, strip_len, cols_blk), layer_idx, 0, keepdims=False
    )

    def gather_slab(local_slab):
        return lax.all_gather(local_slab, "col", axis=1, tiled=True)

    def multiply(left_full):
        return jnp.dot(
            left_full,
            lax.all_gather(row_strips, "row", axis=0, tiled=True),
            preferred_element_type=jnp.float32,
        )

    partial_square = multiply(gather_slab(col_strips))
    square = lax.psum(partial_square, "depth").astype(jnp.bfloat16)
    square_strips = lax.dynamic_index_in_dim(
        square.reshape(rows_blk, groups, depth_n, strip_len), layer_idx, 2, keepdims=False
    ).reshape(rows_blk, groups * strip_len)
    partial_cube = multiply(gather_slab(square_strips))
    cube_sum = lax.psum_scatter(-2.0 * partial_cube, "depth", scatter_dimension=1, tiled=True)
    share_width = cols_blk // depth_n
    own_square = lax.dynamic_slice_in_dim(square, layer_idx * share_width, share_width, 1).astype(
        jnp.float32
    )
    return cube_sum + 3.0 * own_square


def solution(mesh):
    placed = (P("row", "col"),)
    return jax.shard_map(
        on_device, mesh=mesh, in_specs=placed, out_specs=P("row", ("col", "depth")), check_vma=False
    )
```

profile of v0, /device:TPU:17, one launch (start us, length us, event | category | flops | bytes accessed | tf_op | source)
XLA Modules:
  0.0 135.2 jit_solution(775658902013907812)
XLA Ops:
  6.5 0.0 all-gather.3.cloned.1.call-start
  6.5 1.7 %constant_dynamic-slice_fusion.1 = bf16[1,128,1024]{2,1,0:T(8,128)(2,1)} fusion(bf16[4,128,1024]{2,1,0:T(8,128)(2,1)} %bitcast.11, s32[]{:T(128)S(6)} %select_n.10), kind=kLoop, calls=%fused_computation.6 | loop fusion | bytes 524292 | tf_op jit(solution)/shard_map/jit(dynamic_index_in_dim)/dynamic_slice | solution.py:16
  8.2 0.0 all-gather.3.cloned.1.call-update
  8.2 0.0 reduce-scatter.2.cloned.1.call-start
  8.3 1.5 %copy.3 = bf16[512,1024]{0,1:T(8,128)(2,1)S(1)} copy(bf16[512,1024]{1,0:T(8,128)(2,1)} %param.1) | data formatting | bytes 2097152 | tf_op args[0]
  9.8 7.9 %all_gather.10 = bf16[512,512]{0,1:T(8,128)(2,1)S(1)} all-gather(bf16[512,256]{0,1:T(8,128)(2,1)S(1)} %bitcast.14), channel_id=1, replica_groups=mesh['row'=4,'col'=2,'depth'=4] {'col'}, dimensions={1}, use_global_device_ids=true | all-gather | bytes 786432 | tf_op jit(solution)/shard_map/all_gather | solution.py:21
  17.7 19.8 %all-gather.3.cloned.1.call-done = bf16[1,512,1024]{2,1,0:T(8,128)(2,1)} async-done(((bf16[1,128,1024]{2,1,0:T(8,128)(2,1)}), bf16[1,512,1024]{2,1,0:T(8,128)(2,1)}) %all-gather.3.cloned.1.call-update) | async-done | bytes 1048592 | tf_op jit(solution)/shard_map/all_gather | solution.py:26
  37.5 1.9 %fusion.1 = f32[512,1024]{1,0:T(8,128)S(1)} fusion(bf16[512,512]{0,1:T(8,128)(2,1)S(1)} %all_gather.10, bf16[1,512,1024]{2,1,0:T(8,128)(2,1)} %all-gather.3.cloned.1.call-done), kind=kOutput, calls=%fused_computation.2 | convolution fusion | flops 536870912 | bytes 3670016 | tf_op jit(solution)/shard_map/dot_general | solution.py:24
  39.4 42.1 %all-reduce.1 = bf16[512,1024]{1,0:T(8,128)(2,1)S(1)} all-reduce(f32[512,1024]{1,0:T(8,128)S(1)} %fusion.1), channel_id=1, replica_groups=mesh['row'=4,'col'=2,'depth'=4] {'depth'}, use_global_device_ids=true, to_apply=%region_0.1 | all-reduce | flops 524288 | bytes 3145728 | tf_op jit(solution)/shard_map/psum | solution.py:31
  81.5 0.0 copy-start
  81.6 0.8 reshape.20
  82.3 1.3 constant_dynamic-slice_fusion
  83.7 1.2 copy.5
  84.9 8.4 %all_gather.12 = bf16[512,512]{0,1:T(8,128)(2,1)S(1)} all-gather(bf16[512,256]{0,1:T(8,128)(2,1)S(1)} %bitcast.13), channel_id=1, replica_groups=mesh['row'=4,'col'=2,'depth'=4] {'col'}, dimensions={1}, use_global_device_ids=true | all-gather | bytes 786432 | tf_op jit(solution)/shard_map/all_gather | solution.py:21
  93.3 0.0 copy-done
  93.4 2.1 %convolution_multiply_fusion = f32[512,1024]{1,0:T(8,128)} fusion(bf16[512,512]{0,1:T(8,128)(2,1)S(1)} %all_gather.12, bf16[1,512,1024]{2,1,0:T(8,128)(2,1)S(1)} %copy-done), kind=kOutput, calls=%fused_computation | convolution fusion | flops 537395200 | bytes 3670016 | tf_op jit(solution)/shard_map/dot_general | solution.py:24
  95.4 0.0 reduce-scatter.2.cloned.1.call-update
  95.4 31.0 %reduce-scatter.2.cloned.1.call-done = f32[512,256]{1,0:T(8,128)} async-done(((f32[512,1024]{1,0:T(8,128)}), f32[512,256]{1,0:T(8,128)}) %reduce-scatter.2.cloned.1.call-update) | async-done | bytes 524304 | tf_op jit(solution)/shard_map/reduce_scatter | solution.py:36
  126.4 1.9 %multiply_add_fusion = f32[512,256]{1,0:T(8,128)} fusion(f32[512,256]{1,0:T(8,128)} %reduce-scatter.2.cloned.1.call-done, bf16[512,1024]{1,0:T(8,128)(2,1)S(1)} %all-reduce.1, s32[]{:T(128)S(6)} %select_n.11), kind=kLoop, calls=%fused_computation.4 | loop fusion | flops 393216 | bytes 1310724 | tf_op jit(solution)/shard_map/add | solution.py:41
  (1 shorter events, 0.0 us)
Async XLA Ops:
  6.5 30.9 %all-gather.3.cloned.1.call-start = ((), (), s32[]{:S(2)}) async-start(), calls=%async_computation.2 | async-start | bytes 1310720 | tf_op jit(solution)/shard_map/all_gather | solution.py:26
  8.2 118.2 %reduce-scatter.2.cloned.1.call-start = ((), (), s32[]{:S(2)}) async-start(), calls=%async_computation.1 | async-start | bytes 2621440 | tf_op jit(solution)/shard_map/reduce_scatter | solution.py:36
  81.5 11.8 %copy-start = (bf16[1,512,1024]{2,1,0:T(8,128)(2,1)S(1)}, bf16[1,512,1024]{2,1,0:T(8,128)(2,1)}, u32[]{:S(2)}) copy-start(bf16[1,512,1024]{2,1,0:T(8,128)(2,1)} %all-gather.3.cloned.1.call-done) | copy-start | bytes 3145732
Sparse Core Ops, SparseCore 0:
  8.9 28.4 all-gather.2
  95.6 30.7 reduce-scatter.1
where the time goes:
time: 137 us; the launch traced here: 135 us
  blocking collectives  58.4 us (43%)
  waiting for transfers between devices  50.8 us (37%)
  between operations  13.5 us (10%)
  local copies, waits for them, and re-layouts  6.54 us (5%)
  matrix products  4.01 us (3%)
  other arithmetic  1.91 us (1%)
    psum x1, blocking collectives, on_device(): square = lax.psum(partial_square, 'depth').astype(jnp.bfloat16)  42.1 us
    reduce_scatter x1, waiting for transfers between devices, on_device(): lax.psum_scatter(-2.0 * partial_cube, 'depth', scatter_dimension=1, tiled...  31 us
    all_gather x1, waiting for transfers between devices, multiply(): lax.all_gather(row_strips, 'row', axis=0, tiled=True)  19.8 us
    all_gather x2, blocking collectives, gather_slab(): return lax.all_gather(local_slab, 'col', axis=1, tiled=True)  16.3 us
    dot_general x2, matrix products, multiply(): jnp.dot(left_full, lax.all_gather(row_strips, 'row', axis=0, tiled=True),...  4.01 us
    unnamed x4, local copies, waits for them, and re-layouts  2.74 us
  transfers between devices with their start and end apart: 2, of which 2 were waited for; matrix products, arithmetic and copies ran while one was open for 1% of the time, Pallas kernels for 0%

commit v1 on v0

--- a/solution.py
+++ b/solution.py
@@ -1,10 +1,14 @@
+import functools
+
 import jax
 import jax.numpy as jnp
 from jax import lax
+from jax.experimental import pallas as pl
+from jax.experimental.pallas import tpu as pltpu
 from jax.sharding import PartitionSpec as P
 
 
-def on_device(density):
+def split_products(density):
     rows_blk, cols_blk = density.shape
     depth_n = lax.axis_size("depth")
     strip_len = rows_blk // depth_n
@@ -41,8 +45,165 @@
     return cube_sum + 3.0 * own_square
 
 
+def dot(a, b):
+    return jnp.dot(a, b, preferred_element_type=jnp.float32)
+
+
+def dot_t(a, b):
+    return lax.dot_general(a, b, (((1,), (1,)), ((), ())), preferred_element_type=jnp.float32)
+
+
+def place():
+    z, x, d = lax.axis_index("row"), lax.axis_index("col"), lax.axis_index("depth")
+    return z, x, d, lax.div(d, 2), lax.rem(d, 2)
+
+
+def picked(z, x):
+    return lax.rem(z, 2) ^ lax.div(z, 2) ^ x
+
+
+def purify_kernel(half, own, near, far, own0, own1, own2, own3, oth0, oth1, oth2a, oth2b, oth3a, oth3b, out, row, total, square):
+    z, x, d, y, c = place()
+    zr = z ^ (2 * x)
+    for s in range(4):
+        row[s] = own[:, s * half : (s + 1) * half]
+        row[4 + s, pl.ds(pl.multiple_of(c * half, half), half)] = near[:, s * half : (s + 1) * half]
+        row[4 + s, pl.ds(pl.multiple_of((1 - c) * half, half), half)] = far[:, s * half : (s + 1) * half]
+
+    def rows_of(s, h):
+        return row[s, pl.ds(pl.multiple_of(h * half, half), half)]
+
+    for s in range(8):
+        total[s] = dot(row[2 * zr], row[s, :half]) + dot(row[2 * zr + 1], row[s, half:])
+    for h in range(2):
+        acc = total[2 * zr + h]
+        for m in (1, 2, 3):
+            for g in range(2):
+                s = 2 * (zr ^ m) + g
+                acc += dot_t(row[s], row[s, h * half : (h + 1) * half])
+        total[2 * zr + h] = acc
+
+    def blocks():
+        for other in range(2):
+            xx = x ^ other
+            for slot, dist in enumerate((2, 1, 3)):
+                src = z ^ dist
+                if slot == 0:
+                    i, k = src, 2 * xx + picked(src, xx)
+                elif slot == 1:
+                    i = k = 2 * xx + (lax.rem(z, 2) ^ 1)
+                else:
+                    i, k = src, 2 * xx + (1 - picked(src, xx))
+                i, k = i ^ (2 * x), k ^ (2 * x)
+                if other:
+                    q = (
+                        lambda slot=slot: oth0[slot],
+                        lambda slot=slot: oth1[slot],
+                        lambda slot=slot: jnp.concatenate([oth2a[slot], oth2b[slot]], 0),
+                        lambda slot=slot: jnp.concatenate([oth3a[slot], oth3b[slot]], 0),
+                    )
+                else:
+                    q = tuple((lambda r=r, slot=slot: r[slot]) for r in (own0, own1, own2, own3))
+                yield slot, i, k, q
+
+    for slot, i, k, q in blocks():
+        for cc in range(2):
+            total[2 * k + (c ^ cc)] += dot(row[2 * i + y], q[cc]()) + dot(row[2 * i + (1 - y)], q[2 + cc]())
+        if slot != 1:
+
+            def mirrored(i=i, k=k, q=q):
+                for yy in range(2):
+                    total[2 * i + (y ^ yy)] += dot_t(row[2 * k + c], q[2 * yy]()) + dot_t(
+                        row[2 * k + (1 - c)], q[2 * yy + 1]()
+                    )
+
+            if slot == 0:
+                pl.when(i != k)(mirrored)
+            else:
+                mirrored()
+
+    for s in range(8):
+        square[s] = total[s].astype(jnp.bfloat16)
+
+    out[...] = 3.0 * square[d].astype(jnp.float32) - 2.0 * (
+        dot(square[2 * zr], row[d, :half]) + dot(square[2 * zr + 1], row[d, half:])
+    )
+
+    @pl.when(zr == y)
+    def _():
+        acc = out[...]
+        for m in (1, 2, 3):
+            for g in range(2):
+                s = 2 * (zr ^ m) + g
+                acc -= 2.0 * dot_t(square[s], rows_of(s, c))
+        out[...] = acc
+
+    for slot, i, k, q in blocks():
+
+        @pl.when(k == y)
+        def _(i=i, q=q):
+            out[...] -= 2.0 * (dot(square[2 * i + y], q[0]()) + dot(square[2 * i + (1 - y)], q[2]()))
+
+        if slot != 1:
+            for same in range(2):
+
+                @pl.when((i == y) & (i != k) & ((y == c) if same else (y != c)))
+                def _(k=k, q=q, same=same):
+                    a, b = (q[0], q[1]) if same else (q[2], q[3])
+                    out[...] -= 2.0 * (dot_t(square[2 * k + c], a()) + dot_t(square[2 * k + (1 - c)], b()))
+
+
+def gathered(density):
+    blk, half = density.shape[0], density.shape[0] // 2
+    z, x, d, y, c = place()
+
+    def by_z(v, m):
+        return lax.ppermute(v, "row", [(i, i ^ m) for i in range(lax.axis_size("row"))])
+
+    def by_x(v):
+        return lax.ppermute(v, "col", [(i, i ^ 1) for i in range(lax.axis_size("col"))])
+
+    def by_depth(v, m):
+        return lax.ppermute(v, "depth", [(i, i ^ m) for i in range(lax.axis_size("depth"))])
+
+    def quarter(k):
+        return lax.dynamic_slice(density, (y * half, k * blk + c * half), (half, half))
+
+    pick = picked(z, x)
+    sent = quarter(pick)
+    two_away = by_z(sent, 2)
+    three_away = by_z(quarter(1 - pick), 3)
+    near = by_x(lax.dynamic_slice(density, (c * half, 0), (half, 2 * blk)))
+    one_away = by_z(jnp.where(lax.div(z, 2) == x, sent, two_away), 1)
+    far = by_depth(near, 1)
+    own0 = jnp.stack([two_away, one_away, three_away])
+    oth0 = by_x(own0)
+    own2 = by_depth(own0, 2)
+    oth2a = by_depth(oth0[:, : half // 2], 2)
+    oth2b = by_x(own2[:, half // 2 :])
+    own1, oth1, own3, oth3a, oth3b = (by_depth(v, 1) for v in (own0, oth0, own2, oth2a, oth2b))
+    args = (density, near, far, own0, own1, own2, own3, oth0, oth1, oth2a, oth2b, oth3a, oth3b)
+    return pl.pallas_call(
+        functools.partial(purify_kernel, half),
+        out_shape=jax.ShapeDtypeStruct((blk, half), jnp.float32),
+        in_specs=[pl.BlockSpec(memory_space=pltpu.VMEM)] * len(args),
+        out_specs=pl.BlockSpec(memory_space=pltpu.VMEM),
+        scratch_shapes=[
+            pltpu.VMEM((8, blk, half), jnp.bfloat16),
+            pltpu.VMEM((8, blk, half), jnp.float32),
+            pltpu.VMEM((8, blk, half), jnp.bfloat16),
+        ],
+        compiler_params=pltpu.CompilerParams(vmem_limit_bytes=48 * 1024 * 1024),
+        name="purify",
+    )(*args)
+
+
 def solution(mesh):
-    placed = (P("row", "col"),)
+    four_by_two = mesh.shape["row"] == mesh.shape["depth"] == 2 * mesh.shape["col"] == 4
     return jax.shard_map(
-        on_device, mesh=mesh, in_specs=placed, out_specs=P("row", ("col", "depth")), check_vma=False
-    )
+        gathered if four_by_two else split_products,
+        mesh=mesh,
+        in_specs=(P("row", "col"),),
+        out_specs=P("row", ("col", "depth")),
+        check_vma=False,
+    )

time: 137 us -> 45.9 us (0.34); the launches traced: 135 us -> 45.7 us
  blocking collectives: 58.4 us -> 0 us
  waiting for transfers between devices: 50.8 us -> 13 us
  starting transfers between devices: 0.04 us -> 22.5 us
  between operations: 13.5 us -> 0.06 us
  Pallas kernels: 0 us -> 8.01 us
  local copies, waits for them, and re-layouts: 6.54 us -> 2.1 us
  matrix products: 4.01 us -> 0 us
  other arithmetic: 1.91 us -> 0.06 us
    psum x1 -> x0, blocking collectives: 42.1 us -> none  [on_device(): square = lax.psum(partial_square, 'depth').astype(jnp.bfloat16)]
    reduce_scatter x1 -> x0, waiting for transfers between devices: 31 us -> none  [on_device(): lax.psum_scatter(-2.0 * partial_cube, 'depth', scatter_dimension=1, tiled...]
    ppermute x0 -> x14, starting transfers between devices: none -> 22.5 us  [the longest x8 11 us: by_depth(): lax.ppermute(v, 'depth', [(i, i ^ m) for i in range(lax.axis_size('depth'...]
    all_gather x1 -> x0, waiting for transfers between devices: 19.8 us -> none  [multiply(): lax.all_gather(row_strips, 'row', axis=0, tiled=True)]
    all_gather x2 -> x0, blocking collectives: 16.3 us -> none  [gather_slab(): return lax.all_gather(local_slab, 'col', axis=1, tiled=True)]
    ppermute x0 -> x14, waiting for transfers between devices: none -> 13 us  [the longest x3 6.58 us: by_z(): lax.ppermute(v, 'row', [(i, i ^ m) for i in range(lax.axis_size('row'))])]
    pallas_call x0 -> x1, Pallas kernels: none -> 8.01 us  [gathered(): pl.pallas_call(functools.partial(purify_kernel, half), out_shape=jax.Shap...]
    dot_general x2 -> x0, matrix products: 4.01 us -> none  [multiply(): jnp.dot(left_full, lax.all_gather(row_strips, 'row', axis=0, tiled=True),...]
  transfers between devices with their start and end apart: 2 -> 14, of which waited for: 2 -> 5; matrix products, arithmetic and copies ran while one was open for 1% -> 3% of each run, Pallas kernels for 0% -> 0%
where the time goes in v1:
time: 45.9 us; the launch traced here: 45.7 us
  starting transfers between devices  22.5 us (49%)
  waiting for transfers between devices  13 us (28%)
  Pallas kernels  8.01 us (17%)
  local copies, waits for them, and re-layouts  2.1 us (5%)
    ppermute x8, starting transfers between devices, by_depth(): lax.ppermute(v, 'depth', [(i, i ^ m) for i in range(lax.axis_size('depth'...  11 us
    pallas_call x1, Pallas kernels, gathered(): pl.pallas_call(functools.partial(purify_kernel, half), out_shape=jax.Shap...  8.01 us
    ppermute x3, starting transfers between devices, by_z(): lax.ppermute(v, 'row', [(i, i ^ m) for i in range(lax.axis_size('row'))])  7.61 us
    ppermute x3, waiting for transfers between devices, by_z(): lax.ppermute(v, 'row', [(i, i ^ m) for i in range(lax.axis_size('row'))])  6.58 us
    ppermute x3, waiting for transfers between devices, by_x(): lax.ppermute(v, 'col', [(i, i ^ 1) for i in range(lax.axis_size('col'))])  5.33 us
    ppermute x3, starting transfers between devices, by_x(): lax.ppermute(v, 'col', [(i, i ^ 1) for i in range(lax.axis_size('col'))])  3.83 us
    ppermute x8, waiting for transfers between devices, by_depth(): lax.ppermute(v, 'depth', [(i, i ^ m) for i in range(lax.axis_size('depth'...  1.08 us
    dynamic_slice x1, local copies, waits for them, and re-layouts, gathered(): near = by_x(lax.dynamic_slice(density, (c * half, 0), (half, 2 * blk)))  1.08 us
  transfers between devices with their start and end apart: 14, of which 5 were waited for; matrix products, arithmetic and copies ran while one was open for 3% of the time, Pallas kernels for 0%

profile of v1, /device:TPU:17, one launch (start us, length us, event | category | flops | bytes accessed | tf_op | source)
XLA Modules:
  0.0 45.7 jit_solution(5392378234367574727)
XLA Ops:
  0.0 1.0 %fusion = (bf16[256,256]{1,0:T(8,128)(2,1)S(1)}, bf16[256,256]{1,0:T(8,128)(2,1)S(1)}) fusion(bf16[512,1024]{1,0:T(8,128)(2,1)} %own.1, s32[]{:T(128)S(6)} %select_n.22, s32[]{:T(128)S(6)} %select_n.23, s32[]{:T(128)S(6)} %select_n.26), kind=kLoop, calls=%fused_computation.3 | loop fusion | bytes 524300 | tf_op jit(solution)/shard_map/dynamic_slice | solution.py:170
  1.0 0.1 collective-permute-start.2
  1.1 2.5 %collective-permute-start.4 = (bf16[256,256]{1,0:T(8,128)(2,1)S(1)}, bf16[256,256]{1,0:T(8,128)(2,1)S(1)}, u32[]{:S(2)}, u32[]{:S(2)}) collective-permute-start(bf16[256,256]{1,0:T(8,128)(2,1)S(1)} %get-tuple-element.6), channel_id=1, source_target_pairs={{0,24},{8,16},{16,8},{24,0},{1,25},{9,17},{17,9},{25,1},{2,26},{10... | collective-permute-start | bytes 393224 | tf_op jit(solution)/shard_map/ppermute | solution.py:161
  3.5 1.1 %constant_dynamic-slice_fusion = bf16[256,1024]{1,0:T(8,128)(2,1)S(1)} fusion(bf16[512,1024]{1,0:T(8,128)(2,1)} %own.1, s32[]{:T(128)S(6)} %select_n.21), kind=kLoop, calls=%fused_computation.2 | loop fusion | bytes 1048580 | tf_op jit(solution)/shard_map/dynamic_slice | solution.py:176
  4.6 0.0 copy-start
  4.6 1.3 %collective-permute-start = (bf16[256,1024]{1,0:T(8,128)(2,1)S(1)}, bf16[256,1024]{1,0:T(8,128)(2,1)S(1)}, u32[]{:S(2)}, u32[]{:S(2)}) collective-permute-start(bf16[256,1024]{1,0:T(8,128)(2,1)S(1)} %constant_dynamic-slice_fusion), channel_id=1, source_target_pairs={{0,4},{4,0},{1,5},{5,1},{2,6},{6,2},{3,7},{7,3},{8,12},{12,8},{9,1... | collective-permute-start | bytes 1572872 | tf_op jit(solution)/shard_map/ppermute | solution.py:164
  5.9 3.3 %collective-permute-done.2 = bf16[256,256]{1,0:T(8,128)(2,1)S(1)} collective-permute-done((bf16[256,256]{1,0:T(8,128)(2,1)S(1)}, bf16[256,256]{1,0:T(8,128)(2,1)S(1)}, u32[]{:S(2)}, u32[]{:S(2)}) %collective-permute-start.2) | collective-permute-done | bytes 131104 | tf_op jit(solution)/shard_map/ppermute | solution.py:161
  9.2 5.1 %collective-permute-start.3 = (bf16[256,256]{1,0:T(8,128)(2,1)S(1)}, bf16[256,256]{1,0:T(8,128)(2,1)S(1)}, u32[]{:S(2)}, u32[]{:S(2)}) collective-permute-start(bf16[256,256]{1,0:T(8,128)(2,1)S(1)} %broadcast_select_fusion), channel_id=1, source_target_pairs={{0,8},{8,0},{16,24},{24,16},{1,9},{9,1},{17,25},{25,17},{2,10},{10... | collective-permute-start | bytes 393224 | tf_op jit(solution)/shard_map/ppermute | solution.py:161
  14.3 1.5 %collective-permute-done.4 = bf16[256,256]{1,0:T(8,128)(2,1)S(1)} collective-permute-done((bf16[256,256]{1,0:T(8,128)(2,1)S(1)}, bf16[256,256]{1,0:T(8,128)(2,1)S(1)}, u32[]{:S(2)}, u32[]{:S(2)}) %collective-permute-start.4) | collective-permute-done | bytes 131104 | tf_op jit(solution)/shard_map/ppermute | solution.py:161
  15.8 1.8 %collective-permute-done.3 = bf16[256,256]{1,0:T(8,128)(2,1)S(1)} collective-permute-done((bf16[256,256]{1,0:T(8,128)(2,1)S(1)}, bf16[256,256]{1,0:T(8,128)(2,1)S(1)}, u32[]{:S(2)}, u32[]{:S(2)}) %collective-permute-start.3) | collective-permute-done | bytes 131104 | tf_op jit(solution)/shard_map/ppermute | solution.py:161
  17.6 1.3 %collective-permute-start.8 = (bf16[3,256,256]{2,1,0:T(8,128)(2,1)S(1)}, bf16[3,256,256]{2,1,0:T(8,128)(2,1)S(1)}, u32[]{:S(2)}, u32[]{:S(2)}) collective-permute-start(bf16[3,256,256]{2,1,0:T(8,128)(2,1)S(1)} %pad_maximum_fusion.own0), channel_id=1, source_target_pairs={{0,4},{4,0},{1,5},{5,1},{2,6},{6,2},{3,7},{7,3},{8,12},{12,8},{9,1... | collective-permute-start | bytes 1179656 | tf_op jit(solution)/shard_map/ppermute | solution.py:164
  18.9 1.2 %collective-permute-start.6 = (bf16[3,256,256]{2,1,0:T(8,128)(2,1)S(1)}, bf16[3,256,256]{2,1,0:T(8,128)(2,1)S(1)}, u32[]{:S(2)}, u32[]{:S(2)}) collective-permute-start(bf16[3,256,256]{2,1,0:T(8,128)(2,1)S(1)} %pad_maximum_fusion.own0), channel_id=1, source_target_pairs={{0,2},{1,3},{2,0},{3,1},{4,6},{5,7},{6,4},{7,5},{8,10},{9,11},{10,... | collective-permute-start | bytes 1179656 | tf_op jit(solution)/shard_map/ppermute | solution.py:167
  20.1 1.7 %collective-permute-start.5 = (bf16[3,256,256]{2,1,0:T(8,128)(2,1)S(1)}, bf16[3,256,256]{2,1,0:T(8,128)(2,1)S(1)}, u32[]{:S(2)}, u32[]{:S(2)}) collective-permute-start(bf16[3,256,256]{2,1,0:T(8,128)(2,1)S(1)} %pad_maximum_fusion.own0), channel_id=1, source_target_pairs={{0,1},{1,0},{2,3},{3,2},{4,5},{5,4},{6,7},{7,6},{8,9},{9,8},{10,11... | collective-permute-start | bytes 1179656 | tf_op jit(solution)/shard_map/ppermute | solution.py:167
  21.8 0.0 collective-permute-done.near
  21.8 0.0 collective-permute-start.1
  21.8 5.3 %collective-permute-done.8.oth0 = bf16[3,256,256]{2,1,0:T(8,128)(2,1)S(1)} collective-permute-done((bf16[3,256,256]{2,1,0:T(8,128)(2,1)S(1)}, bf16[3,256,256]{2,1,0:T(8,128)(2,1)S(1)}, u32[]{:S(2)}, u32[]{:S(2)}) %collective-permute-start.8) | collective-permute-done | bytes 393248 | tf_op jit(solution)/shard_map/ppermute | solution.py:164
  27.2 1.3 %collective-permute-start.10 = (bf16[3,128,256]{2,1,0:T(8,128)(2,1)S(1)}, bf16[3,128,256]{2,1,0:T(8,128)(2,1)S(1)}, u32[]{:S(2)}, u32[]{:S(2)}) collective-permute-start(bf16[3,128,256]{2,1,0:T(8,128)(2,1)S(1)} %slice.8), channel_id=1, source_target_pairs={{0,2},{1,3},{2,0},{3,1},{4,6},{5,7},{6,4},{7,5},{8,10},{9,11},{10,... | collective-permute-start | bytes 589832 | tf_op jit(solution)/shard_map/ppermute | solution.py:167
  28.5 0.0 collective-permute-done.6.own2
  28.5 1.3 %collective-permute-start.11 = (bf16[3,128,256]{2,1,0:T(8,128)(2,1)S(1)}, bf16[3,128,256]{2,1,0:T(8,128)(2,1)S(1)}, u32[]{:S(2)}, u32[]{:S(2)}) collective-permute-start(bf16[3,128,256]{2,1,0:T(8,128)(2,1)S(1)} %slice.9), channel_id=1, source_target_pairs={{0,4},{4,0},{1,5},{5,1},{2,6},{6,2},{3,7},{7,3},{8,12},{12,8},{9,1... | collective-permute-start | bytes 589832 | tf_op jit(solution)/shard_map/ppermute | solution.py:164
  29.8 2.6 %collective-permute-start.9 = (bf16[3,256,256]{2,1,0:T(8,128)(2,1)S(1)}, bf16[3,256,256]{2,1,0:T(8,128)(2,1)S(1)}, u32[]{:S(2)}, u32[]{:S(2)}) collective-permute-start(bf16[3,256,256]{2,1,0:T(8,128)(2,1)S(1)} %collective-permute-done.8.oth0), channel_id=1, source_target_pairs={{0,1},{1,0},{2,3},{3,2},{4,5},{5,4},{6,7},{7,6},{8,9},{9,8},{10,11... | collective-permute-start | bytes 1179656 | tf_op jit(solution)/shard_map/ppermute | solution.py:167
  32.4 0.0 collective-permute-done.5.own1
  32.4 0.0 collective-permute-start.7
  32.4 0.0 collective-permute-done.10.oth2a
  32.4 2.6 %collective-permute-start.12 = (bf16[3,128,256]{2,1,0:T(8,128)(2,1)S(1)}, bf16[3,128,256]{2,1,0:T(8,128)(2,1)S(1)}, u32[]{:S(2)}, u32[]{:S(2)}) collective-permute-start(bf16[3,128,256]{2,1,0:T(8,128)(2,1)S(1)} %collective-permute-done.10.oth2a), channel_id=1, source_target_pairs={{0,1},{1,0},{2,3},{3,2},{4,5},{5,4},{6,7},{7,6},{8,9},{9,8},{10,11... | collective-permute-start | bytes 589832 | tf_op jit(solution)/shard_map/ppermute | solution.py:167
  35.0 0.0 collective-permute-done.11.oth2b
  35.0 1.6 %collective-permute-start.13 = (bf16[3,128,256]{2,1,0:T(8,128)(2,1)S(1)}, bf16[3,128,256]{2,1,0:T(8,128)(2,1)S(1)}, u32[]{:S(2)}, u32[]{:S(2)}) collective-permute-start(bf16[3,128,256]{2,1,0:T(8,128)(2,1)S(1)} %collective-permute-done.11.oth2b), channel_id=1, source_target_pairs={{0,1},{1,0},{2,3},{3,2},{4,5},{5,4},{6,7},{7,6},{8,9},{9,8},{10,11... | collective-permute-start | bytes 589832 | tf_op jit(solution)/shard_map/ppermute | solution.py:167
  36.6 0.0 collective-permute-done.12.oth3a
  36.6 0.0 collective-permute-done.9.oth1
  36.6 1.1 %collective-permute-done.13.oth3b = bf16[3,128,256]{2,1,0:T(8,128)(2,1)S(1)} collective-permute-done((bf16[3,128,256]{2,1,0:T(8,128)(2,1)S(1)}, bf16[3,128,256]{2,1,0:T(8,128)(2,1)S(1)}, u32[]{:S(2)}, u32[]{:S(2)}) %collective-permute-start.13) | collective-permute-done | bytes 196640 | tf_op jit(solution)/shard_map/ppermute | solution.py:167
  37.7 0.0 collective-permute-done.7.own3
  37.7 0.0 collective-permute-done.1.far
  37.7 8.0 %purify.1 = f32[512,256]{1,0:T(8,128)} custom-call(bf16[512,1024]{1,0:T(8,128)(2,1)S(1)} %copy-done, bf16[256,1024]{1,0:T(8,128)(2,1)S(1)} %collective-permute-done.near, bf16[256,1024]{1,0:T(8,128)(2,1)S(1)} %collective-permute-done.1.far, bf16[3,256,256]{2,1,0:T(8,128)(2,1)S(1)} %pad_maximum_fusion.own0, ...), custom_call_target="tpu_custom_call" | custom-call | tf_op jit(solution)/shard_map/purify/pallas_call | solution.py:186
  (5 shorter events, 0.1 us)
Async XLA Ops:
  1.0 8.2 %collective-permute-start.2 = (bf16[256,256]{1,0:T(8,128)(2,1)S(1)}, bf16[256,256]{1,0:T(8,128)(2,1)S(1)}, u32[]{:S(2)}, u32[]{:S(2)}) collective-permute-start(bf16[256,256]{1,0:T(8,128)(2,1)S(1)} %get-tuple-element.5), channel_id=1, source_target_pairs={{0,16},{8,24},{16,0},{24,8},{1,17},{9,25},{17,1},{25,9},{2,18},{10... | collective-permute-start | bytes 393224 | tf_op jit(solution)/shard_map/ppermute | solution.py:161
  1.1 14.7 %collective-permute-start.4 = (bf16[256,256]{1,0:T(8,128)(2,1)S(1)}, bf16[256,256]{1,0:T(8,128)(2,1)S(1)}, u32[]{:S(2)}, u32[]{:S(2)}) collective-permute-start(bf16[256,256]{1,0:T(8,128)(2,1)S(1)} %get-tuple-element.6), channel_id=1, source_target_pairs={{0,24},{8,16},{16,8},{24,0},{1,25},{9,17},{17,9},{25,1},{2,26},{10... | collective-permute-start | bytes 393224 | tf_op jit(solution)/shard_map/ppermute | solution.py:161
  4.6 33.1 %copy-start = (bf16[512,1024]{1,0:T(8,128)(2,1)S(1)}, bf16[512,1024]{1,0:T(8,128)(2,1)}, u32[]{:S(2)}) copy-start(bf16[512,1024]{1,0:T(8,128)(2,1)} %own.1) | copy-start | bytes 3145732
  4.6 17.2 %collective-permute-start = (bf16[256,1024]{1,0:T(8,128)(2,1)S(1)}, bf16[256,1024]{1,0:T(8,128)(2,1)S(1)}, u32[]{:S(2)}, u32[]{:S(2)}) collective-permute-start(bf16[256,1024]{1,0:T(8,128)(2,1)S(1)} %constant_dynamic-slice_fusion), channel_id=1, source_target_pairs={{0,4},{4,0},{1,5},{5,1},{2,6},{6,2},{3,7},{7,3},{8,12},{12,8},{9,1... | collective-permute-start | bytes 1572872 | tf_op jit(solution)/shard_map/ppermute | solution.py:164
  9.2 8.4 %collective-permute-start.3 = (bf16[256,256]{1,0:T(8,128)(2,1)S(1)}, bf16[256,256]{1,0:T(8,128)(2,1)S(1)}, u32[]{:S(2)}, u32[]{:S(2)}) collective-permute-start(bf16[256,256]{1,0:T(8,128)(2,1)S(1)} %broadcast_select_fusion), channel_id=1, source_target_pairs={{0,8},{8,0},{16,24},{24,16},{1,9},{9,1},{17,25},{25,17},{2,10},{10... | collective-permute-start | bytes 393224 | tf_op jit(solution)/shard_map/ppermute | solution.py:161
  17.6 9.5 %collective-permute-start.8 = (bf16[3,256,256]{2,1,0:T(8,128)(2,1)S(1)}, bf16[3,256,256]{2,1,0:T(8,128)(2,1)S(1)}, u32[]{:S(2)}, u32[]{:S(2)}) collective-permute-start(bf16[3,256,256]{2,1,0:T(8,128)(2,1)S(1)} %pad_maximum_fusion.own0), channel_id=1, source_target_pairs={{0,4},{4,0},{1,5},{5,1},{2,6},{6,2},{3,7},{7,3},{8,12},{12,8},{9,1... | collective-permute-start | bytes 1179656 | tf_op jit(solution)/shard_map/ppermute | solution.py:164
  18.9 9.6 %collective-permute-start.6 = (bf16[3,256,256]{2,1,0:T(8,128)(2,1)S(1)}, bf16[3,256,256]{2,1,0:T(8,128)(2,1)S(1)}, u32[]{:S(2)}, u32[]{:S(2)}) collective-permute-start(bf16[3,256,256]{2,1,0:T(8,128)(2,1)S(1)} %pad_maximum_fusion.own0), channel_id=1, source_target_pairs={{0,2},{1,3},{2,0},{3,1},{4,6},{5,7},{6,4},{7,5},{8,10},{9,11},{10,... | collective-permute-start | bytes 1179656 | tf_op jit(solution)/shard_map/ppermute | solution.py:167
  20.1 12.3 %collective-permute-start.5 = (bf16[3,256,256]{2,1,0:T(8,128)(2,1)S(1)}, bf16[3,256,256]{2,1,0:T(8,128)(2,1)S(1)}, u32[]{:S(2)}, u32[]{:S(2)}) collective-permute-start(bf16[3,256,256]{2,1,0:T(8,128)(2,1)S(1)} %pad_maximum_fusion.own0), channel_id=1, source_target_pairs={{0,1},{1,0},{2,3},{3,2},{4,5},{5,4},{6,7},{7,6},{8,9},{9,8},{10,11... | collective-permute-start | bytes 1179656 | tf_op jit(solution)/shard_map/ppermute | solution.py:167
  21.8 15.8 %collective-permute-start.1 = (bf16[256,1024]{1,0:T(8,128)(2,1)S(1)}, bf16[256,1024]{1,0:T(8,128)(2,1)S(1)}, u32[]{:S(2)}, u32[]{:S(2)}) collective-permute-start(bf16[256,1024]{1,0:T(8,128)(2,1)S(1)} %collective-permute-done.near), channel_id=1, source_target_pairs={{0,1},{1,0},{2,3},{3,2},{4,5},{5,4},{6,7},{7,6},{8,9},{9,8},{10,11... | collective-permute-start | bytes 1572872 | tf_op jit(solution)/shard_map/ppermute | solution.py:167
  27.2 5.2 %collective-permute-start.10 = (bf16[3,128,256]{2,1,0:T(8,128)(2,1)S(1)}, bf16[3,128,256]{2,1,0:T(8,128)(2,1)S(1)}, u32[]{:S(2)}, u32[]{:S(2)}) collective-permute-start(bf16[3,128,256]{2,1,0:T(8,128)(2,1)S(1)} %slice.8), channel_id=1, source_target_pairs={{0,2},{1,3},{2,0},{3,1},{4,6},{5,7},{6,4},{7,5},{8,10},{9,11},{10,... | collective-permute-start | bytes 589832 | tf_op jit(solution)/shard_map/ppermute | solution.py:167
  28.5 6.5 %collective-permute-start.11 = (bf16[3,128,256]{2,1,0:T(8,128)(2,1)S(1)}, bf16[3,128,256]{2,1,0:T(8,128)(2,1)S(1)}, u32[]{:S(2)}, u32[]{:S(2)}) collective-permute-start(bf16[3,128,256]{2,1,0:T(8,128)(2,1)S(1)} %slice.9), channel_id=1, source_target_pairs={{0,4},{4,0},{1,5},{5,1},{2,6},{6,2},{3,7},{7,3},{8,12},{12,8},{9,1... | collective-permute-start | bytes 589832 | tf_op jit(solution)/shard_map/ppermute | solution.py:164
  29.8 6.8 %collective-permute-start.9 = (bf16[3,256,256]{2,1,0:T(8,128)(2,1)S(1)}, bf16[3,256,256]{2,1,0:T(8,128)(2,1)S(1)}, u32[]{:S(2)}, u32[]{:S(2)}) collective-permute-start(bf16[3,256,256]{2,1,0:T(8,128)(2,1)S(1)} %collective-permute-done.8.oth0), channel_id=1, source_target_pairs={{0,1},{1,0},{2,3},{3,2},{4,5},{5,4},{6,7},{7,6},{8,9},{9,8},{10,11... | collective-permute-start | bytes 1179656 | tf_op jit(solution)/shard_map/ppermute | solution.py:167
  32.4 5.2 %collective-permute-start.7 = (bf16[3,256,256]{2,1,0:T(8,128)(2,1)S(1)}, bf16[3,256,256]{2,1,0:T(8,128)(2,1)S(1)}, u32[]{:S(2)}, u32[]{:S(2)}) collective-permute-start(bf16[3,256,256]{2,1,0:T(8,128)(2,1)S(1)} %collective-permute-done.6.own2), channel_id=1, source_target_pairs={{0,1},{1,0},{2,3},{3,2},{4,5},{5,4},{6,7},{7,6},{8,9},{9,8},{10,11... | collective-permute-start | bytes 1179656 | tf_op jit(solution)/shard_map/ppermute | solution.py:167
  32.4 4.2 %collective-permute-start.12 = (bf16[3,128,256]{2,1,0:T(8,128)(2,1)S(1)}, bf16[3,128,256]{2,1,0:T(8,128)(2,1)S(1)}, u32[]{:S(2)}, u32[]{:S(2)}) collective-permute-start(bf16[3,128,256]{2,1,0:T(8,128)(2,1)S(1)} %collective-permute-done.10.oth2a), channel_id=1, source_target_pairs={{0,1},{1,0},{2,3},{3,2},{4,5},{5,4},{6,7},{7,6},{8,9},{9,8},{10,11... | collective-permute-start | bytes 589832 | tf_op jit(solution)/shard_map/ppermute | solution.py:167
  35.0 2.7 %collective-permute-start.13 = (bf16[3,128,256]{2,1,0:T(8,128)(2,1)S(1)}, bf16[3,128,256]{2,1,0:T(8,128)(2,1)S(1)}, u32[]{:S(2)}, u32[]{:S(2)}) collective-permute-start(bf16[3,128,256]{2,1,0:T(8,128)(2,1)S(1)} %collective-permute-done.11.oth2b), channel_id=1, source_target_pairs={{0,1},{1,0},{2,3},{3,2},{4,5},{5,4},{6,7},{7,6},{8,9},{9,8},{10,11... | collective-permute-start | bytes 589832 | tf_op jit(solution)/shard_map/ppermute | solution.py:167

commit v2 on v0

--- a/solution.py
+++ b/solution.py
@@ -1,10 +1,16 @@
+import functools
+
 import jax
 import jax.numpy as jnp
 from jax import lax
+from jax.experimental import pallas as pl
+from jax.experimental.pallas import tpu as pltpu
 from jax.sharding import PartitionSpec as P
 
-
-def on_device(density):
+MIB = 1024 * 1024
+
+
+def split_products(density):
     rows_blk, cols_blk = density.shape
     depth_n = lax.axis_size("depth")
     strip_len = rows_blk // depth_n
@@ -41,8 +47,270 @@
     return cube_sum + 3.0 * own_square
 
 
+def dot(a, b):
+    return jnp.dot(a, b, preferred_element_type=jnp.float32)
+
+
+def turned(a):
+    n = a.shape[1]
+    unit = lax.broadcasted_iota(jnp.int32, (n, n), 0) == lax.broadcasted_iota(jnp.int32, (n, n), 1)
+    unit = unit.astype(jnp.float32).astype(a.dtype)
+    return lax.dot_general(unit, a, (((1,), (1,)), ((), ())), preferred_element_type=jnp.float32).astype(a.dtype)
+
+
+def place():
+    z, x, d = lax.axis_index("row"), lax.axis_index("col"), lax.axis_index("depth")
+    return z, x, d, lax.div(d, 2), lax.rem(d, 2)
+
+
+def picked(z, x):
+    return lax.rem(z, 2) ^ lax.div(z, 2) ^ x
+
+
+def received(slot, other):
+    z, x, _, _, _ = place()
+    away = x ^ other ^ lax.div(z, 2)
+    if slot == 0:
+        return 2, 1 + away
+    if slot == 1:
+        return 1 + 2 * away, 1 + 2 * away
+    return 3, 1 + away
+
+
+def lanes(s, half):
+    return pl.ds(pl.multiple_of(s * half, half), half)
+
+
+def put(columns, i, k, quarter):
+    half = quarter.shape[0]
+    columns[k, lanes(i, half)] = quarter
+    columns[i, lanes(k, half)] = turned(quarter)
+
+
+def put_strip(columns, other, y_dist, same_core, other_core):
+    _, _, _, y, c = place()
+    for slot in range(3):
+        i, k = received(slot, other)
+        for cc, quarter in ((c, same_core(slot)), (1 - c, other_core(slot))):
+            put(columns, 2 * i + (y ^ y_dist), 2 * k + cc, quarter)
+
+
+def put_row(row, columns, m, rows, piece):
+    half = columns.shape[2]
+    for h in range(2):
+        part = piece[:, h * half : (h + 1) * half]
+        s = 2 * m + h
+        if rows is None:
+            row[:, lanes(s, half)] = part
+            for g in range(2):
+                put(columns, g, s, part[g * half : (g + 1) * half])
+        else:
+            row[lanes(rows, half), lanes(s, half)] = part
+            put(columns, rows, s, part)
+
+
+def home():
+    z, x, _, _, _ = place()
+    return (x == lax.div(z, 2)).astype(jnp.int32)
+
+
+def early_halves():
+    _, _, _, y, _ = place()
+    at_home = home()
+    return 0, 1, (4 + y) * (1 - at_home) + 2 * at_home, (6 + y) * (1 - at_home) + 3 * at_home
+
+
+def late_halves():
+    _, _, _, y, _ = place()
+    at_home = home()
+    return (
+        2 + 2 * at_home,
+        3 + 2 * at_home,
+        (5 - y) * (1 - at_home) + (6 + y) * at_home,
+        (7 - y),
+    )
+
+
+def slices_kernel(density, sent, half_row, third, sems):
+    del sent
+    z, x, _, y, c = place()
+    half = third.shape[0]
+    copies = (
+        pltpu.make_async_copy(density.at[lanes(c, half)], half_row, sems.at[0]),
+        pltpu.make_async_copy(
+            density.at[lanes(y, half), lanes(2 * (1 - picked(z, x)) + c, half)], third, sems.at[1]
+        ),
+    )
+    for copy in copies:
+        copy.start()
+    for copy in copies:
+        copy.wait()
+
+
+def row_kernel(own0, own1, near, far, own, row, columns, square):
+    z, x, _, _, c = place()
+    blk, half = own.shape[0], columns.shape[2]
+    for b in range(2):
+        put_row(row, columns, (2 * x + b) ^ z, None, own[:, b * blk : (b + 1) * blk])
+    for b in range(2):
+        m = (2 * (1 - x) + b) ^ z
+        put_row(row, columns, m, c, near[:, b * blk : (b + 1) * blk])
+        put_row(row, columns, m, 1 - c, far[:, b * blk : (b + 1) * blk])
+    put_strip(columns, 0, 0, lambda s: own0[s], lambda s: own1[s])
+    for s in early_halves()[:2]:
+        square[:, lanes(s, half)] = dot(row[...], columns[s]).astype(square.dtype)
+
+
+def middle_kernel(row, columns_in, square_in, own2, own3, oth0, oth1, columns, square, partial):
+    del columns_in, square_in
+    _, _, _, y, c = place()
+    half = columns.shape[2]
+    put_strip(columns, 0, 1, lambda s: own2[s], lambda s: own3[s])
+    put_strip(columns, 1, 0, lambda s: oth0[s], lambda s: oth1[s])
+    nothing = jnp.zeros((half, half), columns.dtype)
+    for slot in range(3):
+        i, k = received(slot, 1)
+        for h in range(2):
+            columns[2 * k + h, lanes(2 * i + 1 - y, half)] = nothing
+
+            @pl.when(i != k)
+            def _(i=i, k=k, h=h):
+                columns[2 * i + 1 - y, lanes(2 * k + h, half)] = nothing
+
+    for s in early_halves()[2:]:
+        square[:, lanes(s, half)] = dot(row[...], columns[s]).astype(square.dtype)
+    for n, s in enumerate(late_halves()):
+        partial[n] = dot(row[...], columns[s])
+
+
+def last_kernel(row, columns_in, square_in, partial, oth2a, oth2b, oth3a, oth3b, out, columns, square):
+    del columns_in, square_in
+    z, x, _, y, c = place()
+    half = columns.shape[2]
+    put_strip(
+        columns,
+        1,
+        1,
+        lambda s: jnp.concatenate([oth2a[s], oth2b[s]], 0),
+        lambda s: jnp.concatenate([oth3a[s], oth3b[s]], 0),
+    )
+
+    def finish(missing):
+        for n, (s, halves) in enumerate(zip(late_halves(), missing, strict=True)):
+            acc = partial[n]
+            for h in halves:
+                acc += dot(row[:, lanes(h, half)], columns[s, lanes(h, half)])
+            square[:, lanes(s, half)] = acc.astype(square.dtype)
+
+    @pl.when(home() == 1)
+    def _():
+        below = (5 - y, 7 - y)
+        finish((below, below, (7 - y,), (4, 5, 7 - y)))
+
+    @pl.when(home() == 0)
+    def _():
+        below = (3 - y, 5 - y, 7 - y)
+        finish((below, below, (2, 3), (2, 3)))
+
+    s = 2 * ((2 * x + y) ^ z) + c
+    out[...] = 3.0 * square[:, lanes(s, half)].astype(jnp.float32) - 2.0 * dot(square[...], columns[s])
+
+
+def call(kernel, name, flops, args, outs, aliases=None, where=pltpu.VMEM, scratch=()):
+    return pl.pallas_call(
+        kernel,
+        out_shape=outs,
+        in_specs=[pl.BlockSpec(memory_space=where)] * len(args),
+        out_specs=[pl.BlockSpec(memory_space=pltpu.VMEM)] * len(outs),
+        scratch_shapes=scratch,
+        input_output_aliases=aliases or {},
+        compiler_params=pltpu.CompilerParams(vmem_limit_bytes=16 * MIB),
+        cost_estimate=pl.CostEstimate(flops=flops, bytes_accessed=0, transcendentals=0),
+        name=name,
+    )(*args)
+
+
+def after(value, *others):
+    return lax.optimization_barrier((value, *others))[0]
+
+
+def gathered(density):
+    blk, half = density.shape[0], density.shape[0] // 2
+    z, x, d, y, c = place()
+    cube = blk**3
+
+    def by_z(v, m):
+        return lax.ppermute(v, "row", [(i, i ^ m) for i in range(lax.axis_size("row"))])
+
+    def by_x(v):
+        return lax.ppermute(v, "col", [(i, i ^ 1) for i in range(lax.axis_size("col"))])
+
+    def by_depth(v, m):
+        return lax.ppermute(v, "depth", [(i, i ^ m) for i in range(lax.axis_size("depth"))])
+
+    def quarter(array, k):
+        return lax.dynamic_slice(array, (y * half, k * blk + c * half), (half, half))
+
+    def shape(*dims, dtype=jnp.bfloat16):
+        return jax.ShapeDtypeStruct(dims, dtype)
+
+    row_shape = shape(blk, 4 * blk)
+    columns_shape = shape(8, 4 * blk, half)
+    pick = picked(z, x)
+    sent = quarter(density, pick)
+    two_away = by_z(sent, 2)
+    half_row, third = call(
+        slices_kernel,
+        "slices",
+        40 * cube,
+        (density, sent),
+        (shape(half, 2 * blk), shape(half, half)),
+        where=pl.ANY,
+        scratch=[pltpu.SemaphoreType.DMA((2,))],
+    )
+    near = by_x(half_row)
+    three_away = by_z(third, 3)
+    one_away = by_z(jnp.where(lax.div(z, 2) == x, sent, two_away), 1)
+    far = by_depth(near, 1)
+    own0 = jnp.stack([two_away, one_away, three_away])
+    oth0, own2 = by_x(own0), by_depth(own0, 2)
+    own1 = by_depth(own0, 1)
+    row, columns, square = call(
+        row_kernel,
+        "row_blocks",
+        18 * cube,
+        (own0, own1, near, far, density),
+        (row_shape, columns_shape, row_shape),
+    )
+    oth2a = by_depth(oth0[:, : half // 2], 2)
+    oth2b = by_x(own2[:, half // 2 :])
+    own3, oth1 = by_depth(own2, 1), by_depth(oth0, 1)
+    columns, square, partial = call(
+        middle_kernel,
+        "middle_blocks",
+        30 * cube,
+        (row, columns, square, own2, own3, oth0, oth1),
+        (columns_shape, row_shape, shape(4, blk, half, dtype=jnp.float32)),
+        {1: 0, 2: 1},
+    )
+    oth2a, oth2b, partial = lax.optimization_barrier((oth2a, oth2b, partial))
+    oth3a, oth3b = by_depth(oth2a, 1), by_depth(oth2b, 1)
+    return call(
+        last_kernel,
+        "last_blocks",
+        10 * cube,
+        (row, columns, square, partial, oth2a, oth2b, oth3a, oth3b),
+        (shape(blk, half, dtype=jnp.float32), columns_shape, row_shape),
+        {1: 1, 2: 2},
+    )[0]
+
+
 def solution(mesh):
-    placed = (P("row", "col"),)
+    four_by_two = mesh.shape["row"] == mesh.shape["depth"] == 2 * mesh.shape["col"] == 4
     return jax.shard_map(
-        on_device, mesh=mesh, in_specs=placed, out_specs=P("row", ("col", "depth")), check_vma=False
-    )
+        gathered if four_by_two else split_products,
+        mesh=mesh,
+        in_specs=(P("row", "col"),),
+        out_specs=P("row", ("col", "depth")),
+        check_vma=False,
+    )

time: 137 us -> 44.5 us (0.32); the launches traced: 135 us -> 44.3 us
  blocking collectives: 58.4 us -> 0 us
  waiting for transfers between devices: 50.8 us -> 10.3 us
  starting transfers between devices: 0.04 us -> 21.7 us
  between operations: 13.5 us -> 0.11 us
  Pallas kernels: 0 us -> 9.92 us
  local copies, waits for them, and re-layouts: 6.54 us -> 2.16 us
  matrix products: 4.01 us -> 0 us
  other arithmetic: 1.91 us -> 0.09 us
    psum x1 -> x0, blocking collectives: 42.1 us -> none  [on_device(): square = lax.psum(partial_square, 'depth').astype(jnp.bfloat16)]
    reduce_scatter x1 -> x0, waiting for transfers between devices: 31 us -> none  [on_device(): lax.psum_scatter(-2.0 * partial_cube, 'depth', scatter_dimension=1, tiled...]
    ppermute x0 -> x14, starting transfers between devices: none -> 21.7 us  [the longest x3 10.4 us: by_z(): lax.ppermute(v, 'row', [(i, i ^ m) for i in range(lax.axis_size('row'))])]
    all_gather x1 -> x0, waiting for transfers between devices: 19.8 us -> none  [multiply(): lax.all_gather(row_strips, 'row', axis=0, tiled=True)]
    all_gather x2 -> x0, blocking collectives: 16.3 us -> none  [gather_slab(): return lax.all_gather(local_slab, 'col', axis=1, tiled=True)]
    ppermute x0 -> x14, waiting for transfers between devices: none -> 10.3 us  [the longest x8 6.71 us: by_depth(): lax.ppermute(v, 'depth', [(i, i ^ m) for i in range(lax.axis_size('depth'...]
    pallas_call x0 -> x4, Pallas kernels: none -> 9.92 us  [call(): pl.pallas_call(kernel, out_shape=outs, in_specs=[pl.BlockSpec(memory_spac...]
    dot_general x2 -> x0, matrix products: 4.01 us -> none  [multiply(): jnp.dot(left_full, lax.all_gather(row_strips, 'row', axis=0, tiled=True),...]
  transfers between devices with their start and end apart: 2 -> 14, of which waited for: 2 -> 6; matrix products, arithmetic and copies ran while one was open for 1% -> 0% of each run, Pallas kernels for 0% -> 16%
where the time goes in v2:
time: 44.5 us; the launch traced here: 44.3 us
  starting transfers between devices  21.7 us (49%)
  waiting for transfers between devices  10.3 us (23%)
  Pallas kernels  9.92 us (22%)
  local copies, waits for them, and re-layouts  2.16 us (5%)
    ppermute x3, starting transfers between devices, by_z(): lax.ppermute(v, 'row', [(i, i ^ m) for i in range(lax.axis_size('row'))])  10.4 us
    pallas_call x4, Pallas kernels, call(): pl.pallas_call(kernel, out_shape=outs, in_specs=[pl.BlockSpec(memory_spac...  9.92 us
    ppermute x8, starting transfers between devices, by_depth(): lax.ppermute(v, 'depth', [(i, i ^ m) for i in range(lax.axis_size('depth'...  7.56 us
    ppermute x8, waiting for transfers between devices, by_depth(): lax.ppermute(v, 'depth', [(i, i ^ m) for i in range(lax.axis_size('depth'...  6.71 us
    ppermute x3, starting transfers between devices, by_x(): lax.ppermute(v, 'col', [(i, i ^ 1) for i in range(lax.axis_size('col'))])  3.8 us
    ppermute x3, waiting for transfers between devices, by_z(): lax.ppermute(v, 'row', [(i, i ^ m) for i in range(lax.axis_size('row'))])  3.55 us
    unnamed x4, local copies, waits for them, and re-layouts  1.22 us
    dynamic_slice x1, local copies, waits for them, and re-layouts, quarter(): lax.dynamic_slice(array, (y * half, k * blk + c * half), (half, half))  0.91 us
  transfers between devices with their start and end apart: 14, of which 6 were waited for; matrix products, arithmetic and copies ran while one was open for 0% of the time, Pallas kernels for 16%

profile of v2, /device:TPU:17, one launch (start us, length us, event | category | flops | bytes accessed | tf_op | source)
XLA Modules:
  0.0 44.3 jit_solution(9863742764389941136)
XLA Ops:
  0.0 0.9 %dynamic_slice.3.sent = bf16[256,256]{1,0:T(8,128)(2,1)S(1)} dynamic-slice(bf16[512,1024]{1,0:T(8,128)(2,1)} %own.1, s32[]{:T(128)S(6)} %select_n.14, s32[]{:T(128)S(6)} %select_n.15), dynamic_slice_sizes={256,256} | dynamic-slice | bytes 262148 | tf_op jit(solution)/shard_map/dynamic_slice | solution.py:252
  0.9 0.1 collective-permute-start
  1.0 0.0 copy-start
  1.0 1.2 %copy-done = bf16[512,1024]{1,0:T(8,128)(2,1)S(1)} copy-done((bf16[512,1024]{1,0:T(8,128)(2,1)S(1)}, bf16[512,1024]{1,0:T(8,128)(2,1)}, u32[]{:S(2)}) %copy-start) | copy-done | bytes 1048600
  2.2 0.1 slices.1
  2.3 1.3 %collective-permute-start.4 = (bf16[256,1024]{1,0:T(8,128)(2,1)S(1)}, bf16[256,1024]{1,0:T(8,128)(2,1)S(1)}, u32[]{:S(2)}, u32[]{:S(2)}) collective-permute-start(bf16[256,1024]{1,0:T(8,128)(2,1)S(1)} %get-tuple-element.18), channel_id=1, source_target_pairs={{0,4},{4,0},{1,5},{5,1},{2,6},{6,2},{3,7},{7,3},{8,12},{12,8},{9,1... | collective-permute-start | bytes 1572872 | tf_op jit(solution)/shard_map/ppermute | solution.py:246
  3.6 2.4 %collective-permute-start.2 = (bf16[256,256]{1,0:T(8,128)(2,1)S(1)}, bf16[256,256]{1,0:T(8,128)(2,1)S(1)}, u32[]{:S(2)}, u32[]{:S(2)}) collective-permute-start(bf16[256,256]{1,0:T(8,128)(2,1)S(1)} %get-tuple-element.17), channel_id=1, source_target_pairs={{0,24},{8,16},{16,8},{24,0},{1,25},{9,17},{17,9},{25,1},{2,26},{10... | collective-permute-start | bytes 393224 | tf_op jit(solution)/shard_map/ppermute | solution.py:243
  6.0 0.2 collective-permute-done
  6.3 7.9 %collective-permute-start.1 = (bf16[256,256]{1,0:T(8,128)(2,1)S(1)}, bf16[256,256]{1,0:T(8,128)(2,1)S(1)}, u32[]{:S(2)}, u32[]{:S(2)}) collective-permute-start(bf16[256,256]{1,0:T(8,128)(2,1)S(1)} %broadcast_select_fusion), channel_id=1, source_target_pairs={{0,8},{8,0},{16,24},{24,16},{1,9},{9,1},{17,25},{25,17},{2,10},{10... | collective-permute-start | bytes 393224 | tf_op jit(solution)/shard_map/ppermute | solution.py:243
  14.2 1.5 %collective-permute-done.2 = bf16[256,256]{1,0:T(8,128)(2,1)S(1)} collective-permute-done((bf16[256,256]{1,0:T(8,128)(2,1)S(1)}, bf16[256,256]{1,0:T(8,128)(2,1)S(1)}, u32[]{:S(2)}, u32[]{:S(2)}) %collective-permute-start.2) | collective-permute-done | bytes 131104 | tf_op jit(solution)/shard_map/ppermute | solution.py:243
  15.7 1.8 %collective-permute-done.1 = bf16[256,256]{1,0:T(8,128)(2,1)S(1)} collective-permute-done((bf16[256,256]{1,0:T(8,128)(2,1)S(1)}, bf16[256,256]{1,0:T(8,128)(2,1)S(1)}, u32[]{:S(2)}, u32[]{:S(2)}) %collective-permute-start.1) | collective-permute-done | bytes 131104 | tf_op jit(solution)/shard_map/ppermute | solution.py:243
  17.6 1.3 %collective-permute-start.6 = (bf16[3,256,256]{2,1,0:T(8,128)(2,1)S(1)}, bf16[3,256,256]{2,1,0:T(8,128)(2,1)S(1)}, u32[]{:S(2)}, u32[]{:S(2)}) collective-permute-start(bf16[3,256,256]{2,1,0:T(8,128)(2,1)S(1)} %pad_maximum_fusion.own0), channel_id=1, source_target_pairs={{0,2},{1,3},{2,0},{3,1},{4,6},{5,7},{6,4},{7,5},{8,10},{9,11},{10,... | collective-permute-start | bytes 1179656 | tf_op jit(solution)/shard_map/ppermute | solution.py:249
  18.9 1.2 %collective-permute-start.8 = (bf16[3,256,256]{2,1,0:T(8,128)(2,1)S(1)}, bf16[3,256,256]{2,1,0:T(8,128)(2,1)S(1)}, u32[]{:S(2)}, u32[]{:S(2)}) collective-permute-start(bf16[3,256,256]{2,1,0:T(8,128)(2,1)S(1)} %pad_maximum_fusion.own0), channel_id=1, source_target_pairs={{0,4},{4,0},{1,5},{5,1},{2,6},{6,2},{3,7},{7,3},{8,12},{12,8},{9,1... | collective-permute-start | bytes 1179656 | tf_op jit(solution)/shard_map/ppermute | solution.py:246
  20.1 0.0 collective-permute-done.4.near
  20.1 1.7 %collective-permute-start.5 = (bf16[256,1024]{1,0:T(8,128)(2,1)S(1)}, bf16[256,1024]{1,0:T(8,128)(2,1)S(1)}, u32[]{:S(2)}, u32[]{:S(2)}) collective-permute-start(bf16[256,1024]{1,0:T(8,128)(2,1)S(1)} %collective-permute-done.4.near), channel_id=1, source_target_pairs={{0,1},{1,0},{2,3},{3,2},{4,5},{5,4},{6,7},{7,6},{8,9},{9,8},{10,11... | collective-permute-start | bytes 1572872 | tf_op jit(solution)/shard_map/ppermute | solution.py:249
  21.8 0.0 collective-permute-start.3
  21.8 5.3 %collective-permute-done.6.own2 = bf16[3,256,256]{2,1,0:T(8,128)(2,1)S(1)} collective-permute-done((bf16[3,256,256]{2,1,0:T(8,128)(2,1)S(1)}, bf16[3,256,256]{2,1,0:T(8,128)(2,1)S(1)}, u32[]{:S(2)}, u32[]{:S(2)}) %collective-permute-start.6) | collective-permute-done | bytes 393248 | tf_op jit(solution)/shard_map/ppermute | solution.py:249
  27.1 2.1 %collective-permute-start.7 = (bf16[3,256,256]{2,1,0:T(8,128)(2,1)S(1)}, bf16[3,256,256]{2,1,0:T(8,128)(2,1)S(1)}, u32[]{:S(2)}, u32[]{:S(2)}) collective-permute-start(bf16[3,256,256]{2,1,0:T(8,128)(2,1)S(1)} %collective-permute-done.6.own2), channel_id=1, source_target_pairs={{0,1},{1,0},{2,3},{3,2},{4,5},{5,4},{6,7},{7,6},{8,9},{9,8},{10,11... | collective-permute-start | bytes 1179656 | tf_op jit(solution)/shard_map/ppermute | solution.py:249
  29.2 0.0 collective-permute-done.8.oth0
  29.2 1.2 %collective-permute-start.9 = (bf16[3,256,256]{2,1,0:T(8,128)(2,1)S(1)}, bf16[3,256,256]{2,1,0:T(8,128)(2,1)S(1)}, u32[]{:S(2)}, u32[]{:S(2)}) collective-permute-start(bf16[3,256,256]{2,1,0:T(8,128)(2,1)S(1)} %collective-permute-done.8.oth0), channel_id=1, source_target_pairs={{0,1},{1,0},{2,3},{3,2},{4,5},{5,4},{6,7},{7,6},{8,9},{9,8},{10,11... | collective-permute-start | bytes 1179656 | tf_op jit(solution)/shard_map/ppermute | solution.py:249
  30.4 0.3 collective-permute-start.10
  30.8 0.0 collective-permute-done.3.own1
  30.8 1.3 %collective-permute-start.11 = (bf16[3,128,256]{2,1,0:T(8,128)(2,1)S(1)}, bf16[3,128,256]{2,1,0:T(8,128)(2,1)S(1)}, u32[]{:S(2)}, u32[]{:S(2)}) collective-permute-start(bf16[3,128,256]{2,1,0:T(8,128)(2,1)S(1)} %slice.9), channel_id=1, source_target_pairs={{0,4},{4,0},{1,5},{5,1},{2,6},{6,2},{3,7},{7,3},{8,12},{12,8},{9,1... | collective-permute-start | bytes 589832 | tf_op jit(solution)/shard_map/ppermute | solution.py:246
  32.0 0.0 collective-permute-done.5.far
  32.0 2.7 %row_blocks.1 = (bf16[512,2048]{1,0:T(8,128)(2,1)S(1)}, bf16[8,2048,256]{2,1,0:T(8,128)(2,1)S(1)}, bf16[512,2048]{1,0:T(8,128)(2,1)S(1)}) custom-call(bf16[3,256,256]{2,1,0:T(8,128)(2,1)S(1)} %pad_maximum_fusion.own0, bf16[3,256,256]{2,1,0:T(8,128)(2,1)S(1)} %collective-permute-done.3.own1, bf16[256,1024]{1,0:T(8,128)(2,1)S(1)} %collective-permute-done.4.near, ...), custom_call_target="tpu_custom_call" | custom-call | flops 2415919104 | tf_op jit(solution)/shard_map/row_blocks/pallas_call | solution.py:220
  34.8 0.0 collective-permute-done.9.oth1
  34.8 4.3 %middle_blocks.1 = (bf16[8,2048,256]{2,1,0:T(8,128)(2,1)S(1)}, bf16[512,2048]{1,0:T(8,128)(2,1)S(1)}, f32[4,512,256]{2,1,0:T(8,128)S(1)}) custom-call(bf16[512,2048]{1,0:T(8,128)(2,1)S(1)} %get-tuple-element.19.row, bf16[8,2048,256]{2,1,0:T(8,128)(2,1)S(1)} %get-tuple-element.20.columns_in, ...), custom_call_target="tpu_custom_call", output_to_operand_aliasing={{0}: (1, {}), {1}: (2, {})} | custom-call | flops 4026531840 | tf_op jit(solution)/shard_map/middle_blocks/pallas_call | solution.py:220
  39.1 0.9 %collective-permute-start.12 = (bf16[3,128,256]{2,1,0:T(8,128)(2,1)S(1)}, bf16[3,128,256]{2,1,0:T(8,128)(2,1)S(1)}, u32[]{:S(2)}, u32[]{:S(2)}) collective-permute-start(bf16[3,128,256]{2,1,0:T(8,128)(2,1)S(1)} %collective-permute-done.10.oth2a), channel_id=1, source_target_pairs={{0,1},{1,0},{2,3},{3,2},{4,5},{5,4},{6,7},{7,6},{8,9},{9,8},{10,11... | collective-permute-start | bytes 589832 | tf_op jit(solution)/shard_map/ppermute | solution.py:249
  40.0 0.1 collective-permute-start.13
  40.1 1.0 %collective-permute-done.12.oth3a = bf16[3,128,256]{2,1,0:T(8,128)(2,1)S(1)} collective-permute-done((bf16[3,128,256]{2,1,0:T(8,128)(2,1)S(1)}, bf16[3,128,256]{2,1,0:T(8,128)(2,1)S(1)}, u32[]{:S(2)}, u32[]{:S(2)}) %collective-permute-start.12) | collective-permute-done | bytes 196640 | tf_op jit(solution)/shard_map/ppermute | solution.py:249
  41.1 0.4 collective-permute-done.13.oth3b
  41.5 2.8 %last_blocks.1 = (f32[512,256]{1,0:T(8,128)}, bf16[8,2048,256]{2,1,0:T(8,128)(2,1)S(1)}, bf16[512,2048]{1,0:T(8,128)(2,1)S(1)}) custom-call(bf16[512,2048]{1,0:T(8,128)(2,1)S(1)} %get-tuple-element.19.row, bf16[8,2048,256]{2,1,0:T(8,128)(2,1)S(1)} %get-tuple-element.22.columns_in, ...), custom_call_target="tpu_custom_call", output_to_operand_aliasing={{1}: (1, {}), {2}: (2, {})} | custom-call | flops 1342177280 | tf_op jit(solution)/shard_map/last_blocks/pallas_call | solution.py:220
  (9 shorter events, 0.1 us)
Async XLA Ops:
  0.9 5.4 %collective-permute-start = (bf16[256,256]{1,0:T(8,128)(2,1)S(1)}, bf16[256,256]{1,0:T(8,128)(2,1)S(1)}, u32[]{:S(2)}, u32[]{:S(2)}) collective-permute-start(bf16[256,256]{1,0:T(8,128)(2,1)S(1)} %dynamic_slice.3.sent), channel_id=1, source_target_pairs={{0,16},{8,24},{16,0},{24,8},{1,17},{9,25},{17,1},{25,9},{2,18},{10... | collective-permute-start | bytes 393224 | tf_op jit(solution)/shard_map/ppermute | solution.py:243
  1.0 1.2 %copy-start = (bf16[512,1024]{1,0:T(8,128)(2,1)S(1)}, bf16[512,1024]{1,0:T(8,128)(2,1)}, u32[]{:S(2)}) copy-start(bf16[512,1024]{1,0:T(8,128)(2,1)} %own.1) | copy-start | bytes 3145732
  2.2 4.1 %copy-start.1 = (bf16[512,1024]{1,0:T(8,128)(2,1)S(1)}, bf16[512,1024]{1,0:T(8,128)(2,1)}, u32[]{:S(2)}) copy-start(bf16[512,1024]{1,0:T(8,128)(2,1)} %own.1) | copy-start | bytes 3145732
  2.3 17.8 %collective-permute-start.4 = (bf16[256,1024]{1,0:T(8,128)(2,1)S(1)}, bf16[256,1024]{1,0:T(8,128)(2,1)S(1)}, u32[]{:S(2)}, u32[]{:S(2)}) collective-permute-start(bf16[256,1024]{1,0:T(8,128)(2,1)S(1)} %get-tuple-element.18), channel_id=1, source_target_pairs={{0,4},{4,0},{1,5},{5,1},{2,6},{6,2},{3,7},{7,3},{8,12},{12,8},{9,1... | collective-permute-start | bytes 1572872 | tf_op jit(solution)/shard_map/ppermute | solution.py:246
  3.6 12.1 %collective-permute-start.2 = (bf16[256,256]{1,0:T(8,128)(2,1)S(1)}, bf16[256,256]{1,0:T(8,128)(2,1)S(1)}, u32[]{:S(2)}, u32[]{:S(2)}) collective-permute-start(bf16[256,256]{1,0:T(8,128)(2,1)S(1)} %get-tuple-element.17), channel_id=1, source_target_pairs={{0,24},{8,16},{16,8},{24,0},{1,25},{9,17},{17,9},{25,1},{2,26},{10... | collective-permute-start | bytes 393224 | tf_op jit(solution)/shard_map/ppermute | solution.py:243
  6.3 11.2 %collective-permute-start.1 = (bf16[256,256]{1,0:T(8,128)(2,1)S(1)}, bf16[256,256]{1,0:T(8,128)(2,1)S(1)}, u32[]{:S(2)}, u32[]{:S(2)}) collective-permute-start(bf16[256,256]{1,0:T(8,128)(2,1)S(1)} %broadcast_select_fusion), channel_id=1, source_target_pairs={{0,8},{8,0},{16,24},{24,16},{1,9},{9,1},{17,25},{25,17},{2,10},{10... | collective-permute-start | bytes 393224 | tf_op jit(solution)/shard_map/ppermute | solution.py:243
  17.6 9.5 %collective-permute-start.6 = (bf16[3,256,256]{2,1,0:T(8,128)(2,1)S(1)}, bf16[3,256,256]{2,1,0:T(8,128)(2,1)S(1)}, u32[]{:S(2)}, u32[]{:S(2)}) collective-permute-start(bf16[3,256,256]{2,1,0:T(8,128)(2,1)S(1)} %pad_maximum_fusion.own0), channel_id=1, source_target_pairs={{0,2},{1,3},{2,0},{3,1},{4,6},{5,7},{6,4},{7,5},{8,10},{9,11},{10,... | collective-permute-start | bytes 1179656 | tf_op jit(solution)/shard_map/ppermute | solution.py:249
  18.9 10.3 %collective-permute-start.8 = (bf16[3,256,256]{2,1,0:T(8,128)(2,1)S(1)}, bf16[3,256,256]{2,1,0:T(8,128)(2,1)S(1)}, u32[]{:S(2)}, u32[]{:S(2)}) collective-permute-start(bf16[3,256,256]{2,1,0:T(8,128)(2,1)S(1)} %pad_maximum_fusion.own0), channel_id=1, source_target_pairs={{0,4},{4,0},{1,5},{5,1},{2,6},{6,2},{3,7},{7,3},{8,12},{12,8},{9,1... | collective-permute-start | bytes 1179656 | tf_op jit(solution)/shard_map/ppermute | solution.py:246
  20.1 11.9 %collective-permute-start.5 = (bf16[256,1024]{1,0:T(8,128)(2,1)S(1)}, bf16[256,1024]{1,0:T(8,128)(2,1)S(1)}, u32[]{:S(2)}, u32[]{:S(2)}) collective-permute-start(bf16[256,1024]{1,0:T(8,128)(2,1)S(1)} %collective-permute-done.4.near), channel_id=1, source_target_pairs={{0,1},{1,0},{2,3},{3,2},{4,5},{5,4},{6,7},{7,6},{8,9},{9,8},{10,11... | collective-permute-start | bytes 1572872 | tf_op jit(solution)/shard_map/ppermute | solution.py:249
  21.8 9.0 %collective-permute-start.3 = (bf16[3,256,256]{2,1,0:T(8,128)(2,1)S(1)}, bf16[3,256,256]{2,1,0:T(8,128)(2,1)S(1)}, u32[]{:S(2)}, u32[]{:S(2)}) collective-permute-start(bf16[3,256,256]{2,1,0:T(8,128)(2,1)S(1)} %pad_maximum_fusion.own0), channel_id=1, source_target_pairs={{0,1},{1,0},{2,3},{3,2},{4,5},{5,4},{6,7},{7,6},{8,9},{9,8},{10,11... | collective-permute-start | bytes 1179656 | tf_op jit(solution)/shard_map/ppermute | solution.py:249
  27.1 7.6 %collective-permute-start.7 = (bf16[3,256,256]{2,1,0:T(8,128)(2,1)S(1)}, bf16[3,256,256]{2,1,0:T(8,128)(2,1)S(1)}, u32[]{:S(2)}, u32[]{:S(2)}) collective-permute-start(bf16[3,256,256]{2,1,0:T(8,128)(2,1)S(1)} %collective-permute-done.6.own2), channel_id=1, source_target_pairs={{0,1},{1,0},{2,3},{3,2},{4,5},{5,4},{6,7},{7,6},{8,9},{9,8},{10,11... | collective-permute-start | bytes 1179656 | tf_op jit(solution)/shard_map/ppermute | solution.py:249
  29.2 5.6 %collective-permute-start.9 = (bf16[3,256,256]{2,1,0:T(8,128)(2,1)S(1)}, bf16[3,256,256]{2,1,0:T(8,128)(2,1)S(1)}, u32[]{:S(2)}, u32[]{:S(2)}) collective-permute-start(bf16[3,256,256]{2,1,0:T(8,128)(2,1)S(1)} %collective-permute-done.8.oth0), channel_id=1, source_target_pairs={{0,1},{1,0},{2,3},{3,2},{4,5},{5,4},{6,7},{7,6},{8,9},{9,8},{10,11... | collective-permute-start | bytes 1179656 | tf_op jit(solution)/shard_map/ppermute | solution.py:249
  30.4 8.7 %collective-permute-start.10 = (bf16[3,128,256]{2,1,0:T(8,128)(2,1)S(1)}, bf16[3,128,256]{2,1,0:T(8,128)(2,1)S(1)}, u32[]{:S(2)}, u32[]{:S(2)}) collective-permute-start(bf16[3,128,256]{2,1,0:T(8,128)(2,1)S(1)} %slice.8), channel_id=1, source_target_pairs={{0,2},{1,3},{2,0},{3,1},{4,6},{5,7},{6,4},{7,5},{8,10},{9,11},{10,... | collective-permute-start | bytes 589832 | tf_op jit(solution)/shard_map/ppermute | solution.py:249
  30.8 8.3 %collective-permute-start.11 = (bf16[3,128,256]{2,1,0:T(8,128)(2,1)S(1)}, bf16[3,128,256]{2,1,0:T(8,128)(2,1)S(1)}, u32[]{:S(2)}, u32[]{:S(2)}) collective-permute-start(bf16[3,128,256]{2,1,0:T(8,128)(2,1)S(1)} %slice.9), channel_id=1, source_target_pairs={{0,4},{4,0},{1,5},{5,1},{2,6},{6,2},{3,7},{7,3},{8,12},{12,8},{9,1... | collective-permute-start | bytes 589832 | tf_op jit(solution)/shard_map/ppermute | solution.py:246
  39.1 2.0 %collective-permute-start.12 = (bf16[3,128,256]{2,1,0:T(8,128)(2,1)S(1)}, bf16[3,128,256]{2,1,0:T(8,128)(2,1)S(1)}, u32[]{:S(2)}, u32[]{:S(2)}) collective-permute-start(bf16[3,128,256]{2,1,0:T(8,128)(2,1)S(1)} %collective-permute-done.10.oth2a), channel_id=1, source_target_pairs={{0,1},{1,0},{2,3},{3,2},{4,5},{5,4},{6,7},{7,6},{8,9},{9,8},{10,11... | collective-permute-start | bytes 589832 | tf_op jit(solution)/shard_map/ppermute | solution.py:249
  40.0 1.4 %collective-permute-start.13 = (bf16[3,128,256]{2,1,0:T(8,128)(2,1)S(1)}, bf16[3,128,256]{2,1,0:T(8,128)(2,1)S(1)}, u32[]{:S(2)}, u32[]{:S(2)}) collective-permute-start(bf16[3,128,256]{2,1,0:T(8,128)(2,1)S(1)} %collective-permute-done.11.oth2b), channel_id=1, source_target_pairs={{0,1},{1,0},{2,3},{3,2},{4,5},{5,4},{6,7},{7,6},{8,9},{9,8},{10,11... | collective-permute-start | bytes 589832 | tf_op jit(solution)/shard_map/ppermute | solution.py:249

commit v3 on v2

--- a/solution.py
+++ b/solution.py
@@ -51,11 +51,12 @@
     return jnp.dot(a, b, preferred_element_type=jnp.float32)
 
 
+def dot_t(a, b):
+    return lax.dot_general(a, b, (((1,), (1,)), ((), ())), preferred_element_type=jnp.float32)
+
+
 def turned(a):
-    n = a.shape[1]
-    unit = lax.broadcasted_iota(jnp.int32, (n, n), 0) == lax.broadcasted_iota(jnp.int32, (n, n), 1)
-    unit = unit.astype(jnp.float32).astype(a.dtype)
-    return lax.dot_general(unit, a, (((1,), (1,)), ((), ())), preferred_element_type=jnp.float32).astype(a.dtype)
+    return jnp.transpose(a)
 
 
 def place():
@@ -99,14 +100,8 @@
     half = columns.shape[2]
     for h in range(2):
         part = piece[:, h * half : (h + 1) * half]
-        s = 2 * m + h
-        if rows is None:
-            row[:, lanes(s, half)] = part
-            for g in range(2):
-                put(columns, g, s, part[g * half : (g + 1) * half])
-        else:
-            row[lanes(rows, half), lanes(s, half)] = part
-            put(columns, rows, s, part)
+        row[lanes(rows, half), lanes(2 * m + h, half)] = part
+        put(columns, rows, 2 * m + h, part)
 
 
 def home():
@@ -131,40 +126,67 @@
     )
 
 
-def slices_kernel(density, sent, half_row, third, sems):
-    del sent
+def half_kernel(array, before, out, upper):
+    del before
+    out[...] = array[:, : out.shape[1]] if upper else array[:, out.shape[1] :]
+
+
+def join_kernel(a, b, before, out):
+    del before
+    out[: a.shape[0]] = a[...]
+    out[a.shape[0] :] = b[...]
+
+
+def stack_kernel(a, b, c, before, out):
+    del before
+    for n, ref in enumerate((a, b, c)):
+        out[n] = ref[...]
+
+
+def fetch(source, out, sem):
+    copy = pltpu.make_async_copy(source, out, sem)
+    copy.start()
+    copy.wait()
+
+
+def half_row_kernel(density, before, out, sem):
+    del before
+    _, _, _, _, c = place()
+    fetch(density.at[lanes(c, out.shape[0])], out, sem)
+
+
+def third_kernel(density, before, out, sem):
+    del before
     z, x, _, y, c = place()
-    half = third.shape[0]
-    copies = (
-        pltpu.make_async_copy(density.at[lanes(c, half)], half_row, sems.at[0]),
-        pltpu.make_async_copy(
-            density.at[lanes(y, half), lanes(2 * (1 - picked(z, x)) + c, half)], third, sems.at[1]
-        ),
-    )
-    for copy in copies:
-        copy.start()
-    for copy in copies:
-        copy.wait()
-
-
-def row_kernel(own0, own1, near, far, own, row, columns, square):
-    z, x, _, _, c = place()
-    blk, half = own.shape[0], columns.shape[2]
+    half = out.shape[0]
+    fetch(density.at[lanes(y, half), lanes(2 * (1 - picked(z, x)) + c, half)], out, sem)
+
+
+def own_kernel(own, own_turned, own_square):
+    half = own_turned.shape[2]
+    for h in range(2):
+        rows = own[h * half : (h + 1) * half, :]
+        own_square[h] = dot_t(own[...], rows)
+        for s in range(4):
+            own_turned[h, s * half : (s + 1) * half] = turned(rows[:, s * half : (s + 1) * half])
+
+
+def middle_kernel(
+    own, own_turned, own_square, near, far, own0, own1, own2, own3, oth0, oth1, row, columns, square, partial
+):
+    z, x, _, y, c = place()
+    blk, half = near.shape[1] // 2, columns.shape[2]
     for b in range(2):
-        put_row(row, columns, (2 * x + b) ^ z, None, own[:, b * blk : (b + 1) * blk])
-    for b in range(2):
+        m = (2 * x + b) ^ z
+        for h in range(2):
+            part = own[:, (2 * b + h) * half : (2 * b + h + 1) * half]
+            row[:, lanes(2 * m + h, half)] = part
+            columns[2 * m + h, :blk] = part
+            columns[h, pl.ds(pl.multiple_of(m * blk, blk), blk)] = own_turned[h, b * blk : (b + 1) * blk]
         m = (2 * (1 - x) + b) ^ z
         put_row(row, columns, m, c, near[:, b * blk : (b + 1) * blk])
         put_row(row, columns, m, 1 - c, far[:, b * blk : (b + 1) * blk])
     put_strip(columns, 0, 0, lambda s: own0[s], lambda s: own1[s])
-    for s in early_halves()[:2]:
-        square[:, lanes(s, half)] = dot(row[...], columns[s]).astype(square.dtype)
-
-
-def middle_kernel(row, columns_in, square_in, own2, own3, oth0, oth1, columns, square, partial):
-    del columns_in, square_in
-    _, _, _, y, c = place()
-    half = columns.shape[2]
     put_strip(columns, 0, 1, lambda s: own2[s], lambda s: own3[s])
     put_strip(columns, 1, 0, lambda s: oth0[s], lambda s: oth1[s])
     nothing = jnp.zeros((half, half), columns.dtype)
@@ -177,50 +199,63 @@
             def _(i=i, k=k, h=h):
                 columns[2 * i + 1 - y, lanes(2 * k + h, half)] = nothing
 
+    others = pl.ds(pl.multiple_of(2 * blk * home(), 2 * blk), 2 * blk)
+    for h in range(2):
+        acc = own_square[h] + dot(row[:, others], columns[h, others])
+        square[:, h * half : (h + 1) * half] = acc.astype(square.dtype)
     for s in early_halves()[2:]:
         square[:, lanes(s, half)] = dot(row[...], columns[s]).astype(square.dtype)
     for n, s in enumerate(late_halves()):
         partial[n] = dot(row[...], columns[s])
 
 
-def last_kernel(row, columns_in, square_in, partial, oth2a, oth2b, oth3a, oth3b, out, columns, square):
-    del columns_in, square_in
+def add_last(row, columns, partial, upper, lower, cc):
+    _, _, _, y, _ = place()
+    half = columns.shape[2]
+    quarters = [jnp.concatenate([upper[slot], lower[slot]], 0) for slot in range(3)]
+    for slot, q in enumerate(quarters):
+        i, k = received(slot, 1)
+        put(columns, 2 * i + 1 - y, 2 * k + cc, q)
+    two, one, three = quarters
+
+    def rows(s):
+        return row[:, lanes(s, half)]
+
+    @pl.when(home() == 1)
+    def _():
+        partial[cc] += dot(rows(5 - y), two) + dot(rows(7 - y), three)
+        partial[3 - (cc ^ y ^ 1)] += dot(rows(7 - y), one)
+        partial[3] += dot_t(rows(4 + cc), three)
+
+    @pl.when(home() == 0)
+    def _():
+        partial[cc] += dot(rows(5 - y), two) + dot(rows(3 - y), one) + dot(rows(7 - y), three)
+        partial[2] += dot_t(rows(2 + cc), two)
+        partial[3] += dot_t(rows(2 + cc), three)
+
+
+def finish_kernel(row, columns_in, partial_in, oth2a, oth2b, columns, partial):
+    del columns_in, partial_in
+    add_last(row, columns, partial, oth2a, oth2b, place()[4])
+
+
+def last_kernel(row, columns_in, square_in, partial_in, oth3a, oth3b, out, columns, square, partial):
+    del columns_in, square_in, partial_in
     z, x, _, y, c = place()
     half = columns.shape[2]
-    put_strip(
-        columns,
-        1,
-        1,
-        lambda s: jnp.concatenate([oth2a[s], oth2b[s]], 0),
-        lambda s: jnp.concatenate([oth3a[s], oth3b[s]], 0),
-    )
-
-    def finish(missing):
-        for n, (s, halves) in enumerate(zip(late_halves(), missing, strict=True)):
-            acc = partial[n]
-            for h in halves:
-                acc += dot(row[:, lanes(h, half)], columns[s, lanes(h, half)])
-            square[:, lanes(s, half)] = acc.astype(square.dtype)
-
-    @pl.when(home() == 1)
-    def _():
-        below = (5 - y, 7 - y)
-        finish((below, below, (7 - y,), (4, 5, 7 - y)))
-
-    @pl.when(home() == 0)
-    def _():
-        below = (3 - y, 5 - y, 7 - y)
-        finish((below, below, (2, 3), (2, 3)))
-
+    add_last(row, columns, partial, oth3a, oth3b, 1 - c)
+    for n, s in enumerate(late_halves()):
+        square[:, lanes(s, half)] = partial[n].astype(square.dtype)
     s = 2 * ((2 * x + y) ^ z) + c
     out[...] = 3.0 * square[:, lanes(s, half)].astype(jnp.float32) - 2.0 * dot(square[...], columns[s])
 
 
-def call(kernel, name, flops, args, outs, aliases=None, where=pltpu.VMEM, scratch=()):
+def call(kernel, name, flops, args, outs, aliases=None, order_only=0, scratch=()):
     return pl.pallas_call(
         kernel,
         out_shape=outs,
-        in_specs=[pl.BlockSpec(memory_space=where)] * len(args),
+        in_specs=[pl.BlockSpec(memory_space=pltpu.VMEM)] * (len(args) - order_only)
+        + [pl.BlockSpec(memory_space=pl.ANY)] * order_only,
         out_specs=[pl.BlockSpec(memory_space=pltpu.VMEM)] * len(outs),
         scratch_shapes=scratch,
         input_output_aliases=aliases or {},
@@ -259,49 +294,73 @@
     pick = picked(z, x)
     sent = quarter(density, pick)
     two_away = by_z(sent, 2)
-    half_row, third = call(
-        slices_kernel,
-        "slices",
+    half_row = call(
+        half_row_kernel,
+        "half_row",
         40 * cube,
         (density, sent),
-        (shape(half, 2 * blk), shape(half, half)),
-        where=pl.ANY,
-        scratch=[pltpu.SemaphoreType.DMA((2,))],
-    )
+        (shape(half, 2 * blk),),
+        order_only=2,
+        scratch=[pltpu.SemaphoreType.DMA],
+    )[0]
+    third = call(
+        third_kernel,
+        "third",
+        20 * cube,
+        (density, half_row),
+        (shape(half, half),),
+        order_only=2,
+        scratch=[pltpu.SemaphoreType.DMA],
+    )[0]
     near = by_x(half_row)
     three_away = by_z(third, 3)
     one_away = by_z(jnp.where(lax.div(z, 2) == x, sent, two_away), 1)
     far = by_depth(near, 1)
-    own0 = jnp.stack([two_away, one_away, three_away])
+    own_turned, own_square = call(
+        own_kernel,
+        "own_blocks",
+        8 * cube,
+        (density,),
+        (shape(2, 2 * blk, half), shape(2, blk, half, dtype=jnp.float32)),
+    )
+    own0 = call(
+        stack_kernel,
+        "stack",
+        0,
+        (two_away, one_away, three_away, own_turned),
+        (shape(3, half, half),),
+        order_only=1,
+    )[0]
     oth0, own2 = by_x(own0), by_depth(own0, 2)
     own1 = by_depth(own0, 1)
-    row, columns, square = call(
-        row_kernel,
-        "row_blocks",
-        18 * cube,
-        (own0, own1, near, far, density),
-        (row_shape, columns_shape, row_shape),
-    )
     oth2a = by_depth(oth0[:, : half // 2], 2)
     oth2b = by_x(own2[:, half // 2 :])
     own3, oth1 = by_depth(own2, 1), by_depth(oth0, 1)
-    columns, square, partial = call(
+    row, columns, square, partial = call(
         middle_kernel,
         "middle_blocks",
         30 * cube,
-        (row, columns, square, own2, own3, oth0, oth1),
-        (columns_shape, row_shape, shape(4, blk, half, dtype=jnp.float32)),
-        {1: 0, 2: 1},
+        (density, own_turned, own_square, near, far, own0, own1, own2, own3, oth0, oth1),
+        (row_shape, columns_shape, row_shape, shape(4, blk, half, dtype=jnp.float32)),
     )
     oth2a, oth2b, partial = lax.optimization_barrier((oth2a, oth2b, partial))
     oth3a, oth3b = by_depth(oth2a, 1), by_depth(oth2b, 1)
+    partial_shape = shape(4, blk, half, dtype=jnp.float32)
+    columns, partial = call(
+        finish_kernel,
+        "finish_blocks",
+        4 * cube,
+        (row, columns, partial, oth2a, oth2b),
+        (columns_shape, partial_shape),
+        {1: 0, 2: 1},
+    )
     return call(
         last_kernel,
         "last_blocks",
-        10 * cube,
-        (row, columns, square, partial, oth2a, oth2b, oth3a, oth3b),
-        (shape(blk, half, dtype=jnp.float32), columns_shape, row_shape),
-        {1: 1, 2: 2},
+        8 * cube,
+        (row, columns, square, partial, oth3a, oth3b),
+        (shape(blk, half, dtype=jnp.float32), columns_shape, row_shape, partial_shape),
+        {1: 1, 2: 2, 3: 3},
     )[0]
 
 

time: 44.5 us -> 43.3 us (0.973)
  waiting for transfers between devices: 10.3 us -> 9.14 us
    ppermute x8, waiting for transfers between devices: 6.71 us -> 0.6 us  [by_depth(): lax.ppermute(v, 'depth', [(i, i ^ m) for i in range(lax.axis_size('depth'...]
    ppermute x3, waiting for transfers between devices: 0.01 us -> 5.82 us  [by_x(): lax.ppermute(v, 'col', [(i, i ^ 1) for i in range(lax.axis_size('col'))])]
    ppermute x8, starting transfers between devices: 7.56 us -> 8.6 us  [by_depth(): lax.ppermute(v, 'depth', [(i, i ^ m) for i in range(lax.axis_size('depth'...]
    ppermute x3, starting transfers between devices: 3.8 us -> 2.91 us  [by_x(): lax.ppermute(v, 'col', [(i, i ^ 1) for i in range(lax.axis_size('col'))])]
    ppermute x3, waiting for transfers between devices: 3.55 us -> 2.73 us  [by_z(): lax.ppermute(v, 'row', [(i, i ^ m) for i in range(lax.axis_size('row'))])]
    pallas_call x4 -> x7, Pallas kernels: 9.92 us -> 9.71 us  [call(): pl.pallas_call(kernel, out_shape=outs, in_specs=[pl.BlockSpec(memory_spac...]
  transfers between devices with their start and end apart: 14 -> 14, of which waited for: 6 -> 7; matrix products, arithmetic and copies ran while one was open for 0% -> 0% of each run, Pallas kernels for 16% -> 17%
where the time goes in v3:
time: 43.3 us; the launch traced here: 43.1 us
  starting transfers between devices  22 us (51%)
  Pallas kernels  9.71 us (22%)
  waiting for transfers between devices  9.14 us (21%)
  local copies, waits for them, and re-layouts  2.17 us (5%)
    ppermute x3, starting transfers between devices, by_z(): lax.ppermute(v, 'row', [(i, i ^ m) for i in range(lax.axis_size('row'))])  10.4 us
    pallas_call x7, Pallas kernels, call(): pl.pallas_call(kernel, out_shape=outs, in_specs=[pl.BlockSpec(memory_spac...  9.71 us
    ppermute x8, starting transfers between devices, by_depth(): lax.ppermute(v, 'depth', [(i, i ^ m) for i in range(lax.axis_size('depth'...  8.6 us
    ppermute x3, waiting for transfers between devices, by_x(): lax.ppermute(v, 'col', [(i, i ^ 1) for i in range(lax.axis_size('col'))])  5.82 us
    ppermute x3, starting transfers between devices, by_x(): lax.ppermute(v, 'col', [(i, i ^ 1) for i in range(lax.axis_size('col'))])  2.91 us
    ppermute x3, waiting for transfers between devices, by_z(): lax.ppermute(v, 'row', [(i, i ^ m) for i in range(lax.axis_size('row'))])  2.73 us
    unnamed x4, local copies, waits for them, and re-layouts  1.23 us
    dynamic_slice x1, local copies, waits for them, and re-layouts, quarter(): lax.dynamic_slice(array, (y * half, k * blk + c * half), (half, half))  0.91 us
  transfers between devices with their start and end apart: 14, of which 7 were waited for; matrix products, arithmetic and copies ran while one was open for 0% of the time, Pallas kernels for 17%

profile of v3, /device:TPU:17, one launch (start us, length us, event | category | flops | bytes accessed | tf_op | source)
XLA Modules:
  0.0 43.1 jit_solution(13773955001385142168)
XLA Ops:
  0.0 0.9 %dynamic_slice.3.before = bf16[256,256]{1,0:T(8,128)(2,1)S(1)} dynamic-slice(bf16[512,1024]{1,0:T(8,128)(2,1)} %own.3, s32[]{:T(128)S(6)} %select_n.14, s32[]{:T(128)S(6)} %select_n.15), dynamic_slice_sizes={256,256} | dynamic-slice | bytes 262148 | tf_op jit(solution)/shard_map/dynamic_slice | solution.py:287
  0.9 0.1 collective-permute-start.2
  1.0 0.0 copy-start
  1.0 1.2 %copy-done = bf16[512,1024]{1,0:T(8,128)(2,1)S(1)} copy-done((bf16[512,1024]{1,0:T(8,128)(2,1)S(1)}, bf16[512,1024]{1,0:T(8,128)(2,1)}, u32[]{:S(2)}) %copy-start) | copy-done | bytes 1048600
  2.3 0.0 copy-start.1
  2.3 1.3 %collective-permute-start = (bf16[256,1024]{1,0:T(8,128)(2,1)S(1)}, bf16[256,1024]{1,0:T(8,128)(2,1)S(1)}, u32[]{:S(2)}, u32[]{:S(2)}) collective-permute-start(bf16[256,1024]{1,0:T(8,128)(2,1)S(1)} %half_row.1.before), channel_id=1, source_target_pairs={{0,4},{4,0},{1,5},{5,1},{2,6},{6,2},{3,7},{7,3},{8,12},{12,8},{9,1... | collective-permute-start | bytes 1572872 | tf_op jit(solution)/shard_map/ppermute | solution.py:281
  3.6 2.5 %collective-permute-start.4 = (bf16[256,256]{1,0:T(8,128)(2,1)S(1)}, bf16[256,256]{1,0:T(8,128)(2,1)S(1)}, u32[]{:S(2)}, u32[]{:S(2)}) collective-permute-start(bf16[256,256]{1,0:T(8,128)(2,1)S(1)} %third.1), channel_id=1, source_target_pairs={{0,24},{8,16},{16,8},{24,0},{1,25},{9,17},{17,9},{25,1},{2,26},{10... | collective-permute-start | bytes 393224 | tf_op jit(solution)/shard_map/ppermute | solution.py:278
  6.1 0.1 collective-permute-done.2.a
  6.3 7.9 %collective-permute-start.3 = (bf16[256,256]{1,0:T(8,128)(2,1)S(1)}, bf16[256,256]{1,0:T(8,128)(2,1)S(1)}, u32[]{:S(2)}, u32[]{:S(2)}) collective-permute-start(bf16[256,256]{1,0:T(8,128)(2,1)S(1)} %broadcast_select_fusion), channel_id=1, source_target_pairs={{0,8},{8,0},{16,24},{24,16},{1,9},{9,1},{17,25},{25,17},{2,10},{10... | collective-permute-start | bytes 393224 | tf_op jit(solution)/shard_map/ppermute | solution.py:278
  14.2 0.7 %own_blocks.1 = (bf16[2,1024,256]{2,1,0:T(8,128)(2,1)S(1)}, f32[2,512,256]{2,1,0:T(8,128)S(1)}) custom-call(bf16[512,1024]{1,0:T(8,128)(2,1)S(1)} %copy-done.1), custom_call_target="tpu_custom_call" | custom-call | flops 1073741824 | tf_op jit(solution)/shard_map/own_blocks/pallas_call | solution.py:254
  15.0 0.8 %collective-permute-done.4.c = bf16[256,256]{1,0:T(8,128)(2,1)S(1)} collective-permute-done((bf16[256,256]{1,0:T(8,128)(2,1)S(1)}, bf16[256,256]{1,0:T(8,128)(2,1)S(1)}, u32[]{:S(2)}, u32[]{:S(2)}) %collective-permute-start.4) | collective-permute-done | bytes 131104 | tf_op jit(solution)/shard_map/ppermute | solution.py:278
  15.7 1.8 %collective-permute-done.3.b = bf16[256,256]{1,0:T(8,128)(2,1)S(1)} collective-permute-done((bf16[256,256]{1,0:T(8,128)(2,1)S(1)}, bf16[256,256]{1,0:T(8,128)(2,1)S(1)}, u32[]{:S(2)}, u32[]{:S(2)}) %collective-permute-start.3) | collective-permute-done | bytes 131104 | tf_op jit(solution)/shard_map/ppermute | solution.py:278
  17.6 1.3 %collective-permute-start.8 = (bf16[3,256,256]{2,1,0:T(8,128)(2,1)S(1)}, bf16[3,256,256]{2,1,0:T(8,128)(2,1)S(1)}, u32[]{:S(2)}, u32[]{:S(2)}) collective-permute-start(bf16[3,256,256]{2,1,0:T(8,128)(2,1)S(1)} %stack.1.own0), channel_id=1, source_target_pairs={{0,4},{4,0},{1,5},{5,1},{2,6},{6,2},{3,7},{7,3},{8,12},{12,8},{9,1... | collective-permute-start | bytes 1179656 | tf_op jit(solution)/shard_map/ppermute | solution.py:281
  18.8 1.2 %collective-permute-start.6 = (bf16[3,256,256]{2,1,0:T(8,128)(2,1)S(1)}, bf16[3,256,256]{2,1,0:T(8,128)(2,1)S(1)}, u32[]{:S(2)}, u32[]{:S(2)}) collective-permute-start(bf16[3,256,256]{2,1,0:T(8,128)(2,1)S(1)} %stack.1.own0), channel_id=1, source_target_pairs={{0,2},{1,3},{2,0},{3,1},{4,6},{5,7},{6,4},{7,5},{8,10},{9,11},{10,... | collective-permute-start | bytes 1179656 | tf_op jit(solution)/shard_map/ppermute | solution.py:284
  20.1 0.0 collective-permute-done.near
  20.1 1.7 %collective-permute-start.1 = (bf16[256,1024]{1,0:T(8,128)(2,1)S(1)}, bf16[256,1024]{1,0:T(8,128)(2,1)S(1)}, u32[]{:S(2)}, u32[]{:S(2)}) collective-permute-start(bf16[256,1024]{1,0:T(8,128)(2,1)S(1)} %collective-permute-done.near), channel_id=1, source_target_pairs={{0,1},{1,0},{2,3},{3,2},{4,5},{5,4},{6,7},{7,6},{8,9},{9,8},{10,11... | collective-permute-start | bytes 1572872 | tf_op jit(solution)/shard_map/ppermute | solution.py:284
  21.8 0.0 collective-permute-start.5
  21.8 5.3 %collective-permute-done.8.oth0 = bf16[3,256,256]{2,1,0:T(8,128)(2,1)S(1)} collective-permute-done((bf16[3,256,256]{2,1,0:T(8,128)(2,1)S(1)}, bf16[3,256,256]{2,1,0:T(8,128)(2,1)S(1)}, u32[]{:S(2)}, u32[]{:S(2)}) %collective-permute-start.8) | collective-permute-done | bytes 393248 | tf_op jit(solution)/shard_map/ppermute | solution.py:281
  27.1 2.1 %collective-permute-start.9 = (bf16[3,256,256]{2,1,0:T(8,128)(2,1)S(1)}, bf16[3,256,256]{2,1,0:T(8,128)(2,1)S(1)}, u32[]{:S(2)}, u32[]{:S(2)}) collective-permute-start(bf16[3,256,256]{2,1,0:T(8,128)(2,1)S(1)} %collective-permute-done.8.oth0), channel_id=1, source_target_pairs={{0,1},{1,0},{2,3},{3,2},{4,5},{5,4},{6,7},{7,6},{8,9},{9,8},{10,11... | collective-permute-start | bytes 1179656 | tf_op jit(solution)/shard_map/ppermute | solution.py:284
  29.2 0.0 collective-permute-done.6.own2
  29.2 1.2 %collective-permute-start.7 = (bf16[3,256,256]{2,1,0:T(8,128)(2,1)S(1)}, bf16[3,256,256]{2,1,0:T(8,128)(2,1)S(1)}, u32[]{:S(2)}, u32[]{:S(2)}) collective-permute-start(bf16[3,256,256]{2,1,0:T(8,128)(2,1)S(1)} %collective-permute-done.6.own2), channel_id=1, source_target_pairs={{0,1},{1,0},{2,3},{3,2},{4,5},{5,4},{6,7},{7,6},{8,9},{9,8},{10,11... | collective-permute-start | bytes 1179656 | tf_op jit(solution)/shard_map/ppermute | solution.py:284
  30.4 1.3 %collective-permute-start.10 = (bf16[3,128,256]{2,1,0:T(8,128)(2,1)S(1)}, bf16[3,128,256]{2,1,0:T(8,128)(2,1)S(1)}, u32[]{:S(2)}, u32[]{:S(2)}) collective-permute-start(bf16[3,128,256]{2,1,0:T(8,128)(2,1)S(1)} %slice.8), channel_id=1, source_target_pairs={{0,2},{1,3},{2,0},{3,1},{4,6},{5,7},{6,4},{7,5},{8,10},{9,11},{10,... | collective-permute-start | bytes 589832 | tf_op jit(solution)/shard_map/ppermute | solution.py:284
  31.7 0.0 collective-permute-done.5.own1
  31.7 0.3 collective-permute-start.11
  32.1 5.4 %middle_blocks.1 = (bf16[512,2048]{1,0:T(8,128)(2,1)S(1)}, bf16[8,2048,256]{2,1,0:T(8,128)(2,1)S(1)}, bf16[512,2048]{1,0:T(8,128)(2,1)S(1)}, f32[4,512,256]{2,1,0:T(8,128)S(1)}) custom-call(bf16[512,1024]{1,0:T(8,128)(2,1)S(1)} %copy-done.1, bf16[2,1024,256]{2,1,0:T(8,128)(2,1)S(1)} %get-tuple-element.17.before.own_turned, ...), custom_call_target="tpu_custom_call" | custom-call | flops 4026531840 | tf_op jit(solution)/shard_map/middle_blocks/pallas_call | solution.py:254
  37.5 0.5 %collective-permute-done.11.oth2b = bf16[3,128,256]{2,1,0:T(8,128)(2,1)S(1)} collective-permute-done((bf16[3,128,256]{2,1,0:T(8,128)(2,1)S(1)}, bf16[3,128,256]{2,1,0:T(8,128)(2,1)S(1)}, u32[]{:S(2)}, u32[]{:S(2)}) %collective-permute-start.11) | collective-permute-done | bytes 196640 | tf_op jit(solution)/shard_map/ppermute | solution.py:281
  38.0 1.1 %collective-permute-start.12 = (bf16[3,128,256]{2,1,0:T(8,128)(2,1)S(1)}, bf16[3,128,256]{2,1,0:T(8,128)(2,1)S(1)}, u32[]{:S(2)}, u32[]{:S(2)}) collective-permute-start(bf16[3,128,256]{2,1,0:T(8,128)(2,1)S(1)} %collective-permute-done.10.oth2a), channel_id=1, source_target_pairs={{0,1},{1,0},{2,3},{3,2},{4,5},{5,4},{6,7},{7,6},{8,9},{9,8},{10,11... | collective-permute-start | bytes 589832 | tf_op jit(solution)/shard_map/ppermute | solution.py:284
  39.1 0.0 collective-permute-start.13
  39.1 0.8 %finish_blocks.1 = (bf16[8,2048,256]{2,1,0:T(8,128)(2,1)S(1)}, f32[4,512,256]{2,1,0:T(8,128)S(1)}) custom-call(bf16[512,2048]{1,0:T(8,128)(2,1)S(1)} %get-tuple-element.19.row, bf16[8,2048,256]{2,1,0:T(8,128)(2,1)S(1)} %get-tuple-element.20.columns_in, ...), custom_call_target="tpu_custom_call", output_to_operand_aliasing={{0}: (1, {}), {1}: (2, {})} | custom-call | flops 536870912 | tf_op jit(solution)/shard_map/finish_blocks/pallas_call | solution.py:254
  40.0 0.2 collective-permute-done.12.oth3a
  40.2 0.4 collective-permute-done.13.oth3b
  40.6 2.6 %last_blocks.1 = (f32[512,256]{1,0:T(8,128)}, bf16[8,2048,256]{2,1,0:T(8,128)(2,1)S(1)}, bf16[512,2048]{1,0:T(8,128)(2,1)S(1)}, f32[4,512,256]{2,1,0:T(8,128)S(1)}) custom-call(bf16[512,2048]{1,0:T(8,128)(2,1)S(1)} %get-tuple-element.19.row, ...), custom_call_target="tpu_custom_call", output_to_operand_aliasing={{1}: (1, {}), {2}: (2, {}), {3}: (3, {})} | custom-call | flops 1073741824 | tf_op jit(solution)/shard_map/last_blocks/pallas_call | solution.py:254
  (11 shorter events, 0.2 us)
Async XLA Ops:
  0.9 5.4 %collective-permute-start.2 = (bf16[256,256]{1,0:T(8,128)(2,1)S(1)}, bf16[256,256]{1,0:T(8,128)(2,1)S(1)}, u32[]{:S(2)}, u32[]{:S(2)}) collective-permute-start(bf16[256,256]{1,0:T(8,128)(2,1)S(1)} %dynamic_slice.3.before), channel_id=1, source_target_pairs={{0,16},{8,24},{16,0},{24,8},{1,17},{9,25},{17,1},{25,9},{2,18},{10... | collective-permute-start | bytes 393224 | tf_op jit(solution)/shard_map/ppermute | solution.py:278
  1.0 1.2 %copy-start = (bf16[512,1024]{1,0:T(8,128)(2,1)S(1)}, bf16[512,1024]{1,0:T(8,128)(2,1)}, u32[]{:S(2)}) copy-start(bf16[512,1024]{1,0:T(8,128)(2,1)} %own.3) | copy-start | bytes 3145732
  2.3 4.0 %copy-start.1 = (bf16[512,1024]{1,0:T(8,128)(2,1)S(1)}, bf16[512,1024]{1,0:T(8,128)(2,1)}, u32[]{:S(2)}) copy-start(bf16[512,1024]{1,0:T(8,128)(2,1)} %own.3) | copy-start | bytes 3145732
  2.3 17.8 %collective-permute-start = (bf16[256,1024]{1,0:T(8,128)(2,1)S(1)}, bf16[256,1024]{1,0:T(8,128)(2,1)S(1)}, u32[]{:S(2)}, u32[]{:S(2)}) collective-permute-start(bf16[256,1024]{1,0:T(8,128)(2,1)S(1)} %half_row.1.before), channel_id=1, source_target_pairs={{0,4},{4,0},{1,5},{5,1},{2,6},{6,2},{3,7},{7,3},{8,12},{12,8},{9,1... | collective-permute-start | bytes 1572872 | tf_op jit(solution)/shard_map/ppermute | solution.py:281
  3.6 12.1 %collective-permute-start.4 = (bf16[256,256]{1,0:T(8,128)(2,1)S(1)}, bf16[256,256]{1,0:T(8,128)(2,1)S(1)}, u32[]{:S(2)}, u32[]{:S(2)}) collective-permute-start(bf16[256,256]{1,0:T(8,128)(2,1)S(1)} %third.1), channel_id=1, source_target_pairs={{0,24},{8,16},{16,8},{24,0},{1,25},{9,17},{17,9},{25,1},{2,26},{10... | collective-permute-start | bytes 393224 | tf_op jit(solution)/shard_map/ppermute | solution.py:278
  6.3 11.2 %collective-permute-start.3 = (bf16[256,256]{1,0:T(8,128)(2,1)S(1)}, bf16[256,256]{1,0:T(8,128)(2,1)S(1)}, u32[]{:S(2)}, u32[]{:S(2)}) collective-permute-start(bf16[256,256]{1,0:T(8,128)(2,1)S(1)} %broadcast_select_fusion), channel_id=1, source_target_pairs={{0,8},{8,0},{16,24},{24,16},{1,9},{9,1},{17,25},{25,17},{2,10},{10... | collective-permute-start | bytes 393224 | tf_op jit(solution)/shard_map/ppermute | solution.py:278
  17.6 9.5 %collective-permute-start.8 = (bf16[3,256,256]{2,1,0:T(8,128)(2,1)S(1)}, bf16[3,256,256]{2,1,0:T(8,128)(2,1)S(1)}, u32[]{:S(2)}, u32[]{:S(2)}) collective-permute-start(bf16[3,256,256]{2,1,0:T(8,128)(2,1)S(1)} %stack.1.own0), channel_id=1, source_target_pairs={{0,4},{4,0},{1,5},{5,1},{2,6},{6,2},{3,7},{7,3},{8,12},{12,8},{9,1... | collective-permute-start | bytes 1179656 | tf_op jit(solution)/shard_map/ppermute | solution.py:281
  18.8 10.3 %collective-permute-start.6 = (bf16[3,256,256]{2,1,0:T(8,128)(2,1)S(1)}, bf16[3,256,256]{2,1,0:T(8,128)(2,1)S(1)}, u32[]{:S(2)}, u32[]{:S(2)}) collective-permute-start(bf16[3,256,256]{2,1,0:T(8,128)(2,1)S(1)} %stack.1.own0), channel_id=1, source_target_pairs={{0,2},{1,3},{2,0},{3,1},{4,6},{5,7},{6,4},{7,5},{8,10},{9,11},{10,... | collective-permute-start | bytes 1179656 | tf_op jit(solution)/shard_map/ppermute | solution.py:284
  20.1 12.0 %collective-permute-start.1 = (bf16[256,1024]{1,0:T(8,128)(2,1)S(1)}, bf16[256,1024]{1,0:T(8,128)(2,1)S(1)}, u32[]{:S(2)}, u32[]{:S(2)}) collective-permute-start(bf16[256,1024]{1,0:T(8,128)(2,1)S(1)} %collective-permute-done.near), channel_id=1, source_target_pairs={{0,1},{1,0},{2,3},{3,2},{4,5},{5,4},{6,7},{7,6},{8,9},{9,8},{10,11... | collective-permute-start | bytes 1572872 | tf_op jit(solution)/shard_map/ppermute | solution.py:284
  21.8 9.9 %collective-permute-start.5 = (bf16[3,256,256]{2,1,0:T(8,128)(2,1)S(1)}, bf16[3,256,256]{2,1,0:T(8,128)(2,1)S(1)}, u32[]{:S(2)}, u32[]{:S(2)}) collective-permute-start(bf16[3,256,256]{2,1,0:T(8,128)(2,1)S(1)} %stack.1.own0), channel_id=1, source_target_pairs={{0,1},{1,0},{2,3},{3,2},{4,5},{5,4},{6,7},{7,6},{8,9},{9,8},{10,11... | collective-permute-start | bytes 1179656 | tf_op jit(solution)/shard_map/ppermute | solution.py:284
  27.1 4.9 %collective-permute-start.9 = (bf16[3,256,256]{2,1,0:T(8,128)(2,1)S(1)}, bf16[3,256,256]{2,1,0:T(8,128)(2,1)S(1)}, u32[]{:S(2)}, u32[]{:S(2)}) collective-permute-start(bf16[3,256,256]{2,1,0:T(8,128)(2,1)S(1)} %collective-permute-done.8.oth0), channel_id=1, source_target_pairs={{0,1},{1,0},{2,3},{3,2},{4,5},{5,4},{6,7},{7,6},{8,9},{9,8},{10,11... | collective-permute-start | bytes 1179656 | tf_op jit(solution)/shard_map/ppermute | solution.py:284
  29.2 2.9 %collective-permute-start.7 = (bf16[3,256,256]{2,1,0:T(8,128)(2,1)S(1)}, bf16[3,256,256]{2,1,0:T(8,128)(2,1)S(1)}, u32[]{:S(2)}, u32[]{:S(2)}) collective-permute-start(bf16[3,256,256]{2,1,0:T(8,128)(2,1)S(1)} %collective-permute-done.6.own2), channel_id=1, source_target_pairs={{0,1},{1,0},{2,3},{3,2},{4,5},{5,4},{6,7},{7,6},{8,9},{9,8},{10,11... | collective-permute-start | bytes 1179656 | tf_op jit(solution)/shard_map/ppermute | solution.py:284
  30.4 7.1 %collective-permute-start.10 = (bf16[3,128,256]{2,1,0:T(8,128)(2,1)S(1)}, bf16[3,128,256]{2,1,0:T(8,128)(2,1)S(1)}, u32[]{:S(2)}, u32[]{:S(2)}) collective-permute-start(bf16[3,128,256]{2,1,0:T(8,128)(2,1)S(1)} %slice.8), channel_id=1, source_target_pairs={{0,2},{1,3},{2,0},{3,1},{4,6},{5,7},{6,4},{7,5},{8,10},{9,11},{10,... | collective-permute-start | bytes 589832 | tf_op jit(solution)/shard_map/ppermute | solution.py:284
  31.7 6.3 %collective-permute-start.11 = (bf16[3,128,256]{2,1,0:T(8,128)(2,1)S(1)}, bf16[3,128,256]{2,1,0:T(8,128)(2,1)S(1)}, u32[]{:S(2)}, u32[]{:S(2)}) collective-permute-start(bf16[3,128,256]{2,1,0:T(8,128)(2,1)S(1)} %slice.9), channel_id=1, source_target_pairs={{0,4},{4,0},{1,5},{5,1},{2,6},{6,2},{3,7},{7,3},{8,12},{12,8},{9,1... | collective-permute-start | bytes 589832 | tf_op jit(solution)/shard_map/ppermute | solution.py:281
  38.0 2.2 %collective-permute-start.12 = (bf16[3,128,256]{2,1,0:T(8,128)(2,1)S(1)}, bf16[3,128,256]{2,1,0:T(8,128)(2,1)S(1)}, u32[]{:S(2)}, u32[]{:S(2)}) collective-permute-start(bf16[3,128,256]{2,1,0:T(8,128)(2,1)S(1)} %collective-permute-done.10.oth2a), channel_id=1, source_target_pairs={{0,1},{1,0},{2,3},{3,2},{4,5},{5,4},{6,7},{7,6},{8,9},{9,8},{10,11... | collective-permute-start | bytes 589832 | tf_op jit(solution)/shard_map/ppermute | solution.py:284
  39.1 1.4 %collective-permute-start.13 = (bf16[3,128,256]{2,1,0:T(8,128)(2,1)S(1)}, bf16[3,128,256]{2,1,0:T(8,128)(2,1)S(1)}, u32[]{:S(2)}, u32[]{:S(2)}) collective-permute-start(bf16[3,128,256]{2,1,0:T(8,128)(2,1)S(1)} %collective-permute-done.11.oth2b), channel_id=1, source_target_pairs={{0,1},{1,0},{2,3},{3,2},{4,5},{5,4},{6,7},{7,6},{8,9},{9,8},{10,11... | collective-permute-start | bytes 589832 | tf_op jit(solution)/shard_map/ppermute | solution.py:284

commit v4 on v3

--- a/solution.py
+++ b/solution.py
@@ -137,8 +137,7 @@
     out[a.shape[0] :] = b[...]
 
 
-def stack_kernel(a, b, c, before, out):
-    del before
+def stack_kernel(a, b, c, out):
     for n, ref in enumerate((a, b, c)):
         out[n] = ref[...]
 
@@ -162,31 +161,41 @@
     fetch(density.at[lanes(y, half), lanes(2 * (1 - picked(z, x)) + c, half)], out, sem)
 
 
-def own_kernel(own, own_turned, own_square):
-    half = own_turned.shape[2]
-    for h in range(2):
-        rows = own[h * half : (h + 1) * half, :]
-        own_square[h] = dot_t(own[...], rows)
-        for s in range(4):
-            own_turned[h, s * half : (s + 1) * half] = turned(rows[:, s * half : (s + 1) * half])
-
-
-def middle_kernel(
-    own, own_turned, own_square, near, far, own0, own1, own2, own3, oth0, oth1, row, columns, square, partial
-):
-    z, x, _, y, c = place()
-    blk, half = near.shape[1] // 2, columns.shape[2]
+def first_kernel(own, own0, own1, row, columns):
+    z, x, _, _, _ = place()
+    blk, half = own.shape[0], columns.shape[2]
     for b in range(2):
         m = (2 * x + b) ^ z
         for h in range(2):
             part = own[:, (2 * b + h) * half : (2 * b + h + 1) * half]
             row[:, lanes(2 * m + h, half)] = part
             columns[2 * m + h, :blk] = part
-            columns[h, pl.ds(pl.multiple_of(m * blk, blk), blk)] = own_turned[h, b * blk : (b + 1) * blk]
+            for g in range(2):
+                columns[g, lanes(2 * m + h, half)] = turned(part[g * half : (g + 1) * half])
+    put_strip(columns, 0, 0, lambda s: own0[s], lambda s: own1[s])
+
+
+def cross_kernel(a, b, before, out):
+    del before
+    _, _, _, _, c = place()
+
+    @pl.when(c == 0)
+    def _():
+        out[...] = a[...]
+
+    @pl.when(c == 1)
+    def _():
+        out[...] = b[...]
+
+
+def middle_kernel(row_in, columns_in, near, far, own2, own3, oth0, oth1, row, columns, square, partial):
+    del row_in, columns_in
+    z, x, _, y, c = place()
+    blk, half = near.shape[1] // 2, columns.shape[2]
+    for b in range(2):
         m = (2 * (1 - x) + b) ^ z
         put_row(row, columns, m, c, near[:, b * blk : (b + 1) * blk])
         put_row(row, columns, m, 1 - c, far[:, b * blk : (b + 1) * blk])
-    put_strip(columns, 0, 0, lambda s: own0[s], lambda s: own1[s])
     put_strip(columns, 0, 1, lambda s: own2[s], lambda s: own3[s])
     put_strip(columns, 1, 0, lambda s: oth0[s], lambda s: oth1[s])
     nothing = jnp.zeros((half, half), columns.dtype)
@@ -199,20 +208,16 @@
             def _(i=i, k=k, h=h):
                 columns[2 * i + 1 - y, lanes(2 * k + h, half)] = nothing
 
-    others = pl.ds(pl.multiple_of(2 * blk * home(), 2 * blk), 2 * blk)
-    for h in range(2):
-        acc = own_square[h] + dot(row[:, others], columns[h, others])
-        square[:, h * half : (h + 1) * half] = acc.astype(square.dtype)
-    for s in early_halves()[2:]:
+    for s in early_halves():
         square[:, lanes(s, half)] = dot(row[...], columns[s]).astype(square.dtype)
     for n, s in enumerate(late_halves()):
         partial[n] = dot(row[...], columns[s])
 
 
-def add_last(row, columns, partial, upper, lower, cc):
+def add_last(row, columns, partial, last, cc):
     _, _, _, y, _ = place()
     half = columns.shape[2]
-    quarters = [jnp.concatenate([upper[slot], lower[slot]], 0) for slot in range(3)]
+    quarters = [last[slot] for slot in range(3)]
     for slot, q in enumerate(quarters):
         i, k = received(slot, 1)
         put(columns, 2 * i + 1 - y, 2 * k + cc, q)
@@ -234,20 +239,34 @@
         partial[3] += dot_t(rows(2 + cc), three)
 
 
-def finish_kernel(row, columns_in, partial_in, oth2a, oth2b, columns, partial):
+def wanted():
+    z, x, _, y, c = place()
+    return 2 * ((2 * x + y) ^ z) + c
+
+
+def finish_kernel(row, columns_in, partial_in, square, oth2, columns, partial, cube):
     del columns_in, partial_in
-    add_last(row, columns, partial, oth2a, oth2b, place()[4])
-
-
-def last_kernel(row, columns_in, square_in, partial_in, oth3a, oth3b, out, columns, square, partial):
+    half = columns.shape[2]
+    add_last(row, columns, partial, oth2, place()[4])
+    s = wanted()
+    acc = None
+    for h in early_halves():
+        term = dot(square[:, lanes(h, half)], columns[s, lanes(h, half)])
+        acc = term if acc is None else acc + term
+    cube[...] = acc
+
+
+def last_kernel(row, columns_in, square_in, partial_in, cube, oth3, out, columns, square, partial):
     del columns_in, square_in, partial_in
-    z, x, _, y, c = place()
     half = columns.shape[2]
-    add_last(row, columns, partial, oth3a, oth3b, 1 - c)
-    for n, s in enumerate(late_halves()):
-        square[:, lanes(s, half)] = partial[n].astype(square.dtype)
-    s = 2 * ((2 * x + y) ^ z) + c
-    out[...] = 3.0 * square[:, lanes(s, half)].astype(jnp.float32) - 2.0 * dot(square[...], columns[s])
+    add_last(row, columns, partial, oth3, 1 - place()[4])
+    s = wanted()
+    acc = cube[...]
+    for n, h in enumerate(late_halves()):
+        part = partial[n].astype(square.dtype)
+        square[:, lanes(h, half)] = part
+        acc += dot(part, columns[s, lanes(h, half)])
+    out[...] = 3.0 * square[:, lanes(s, half)].astype(jnp.float32) - 2.0 * acc
 
 
 def call(kernel, name, flops, args, outs, aliases=None, order_only=0, scratch=()):
@@ -283,6 +302,11 @@
     def by_depth(v, m):
         return lax.ppermute(v, "depth", [(i, i ^ m) for i in range(lax.axis_size("depth"))])
 
+    def crossed(v):
+        n = lax.axis_size("depth")
+        pairs = [(p, p ^ 2 if p % 2 == 0 else p ^ n) for p in range(lax.axis_size("col") * n)]
+        return lax.ppermute(v, ("col", "depth"), pairs)
+
     def quarter(array, k):
         return lax.dynamic_slice(array, (y * half, k * blk + c * half), (half, half))
 
@@ -316,50 +340,49 @@
     three_away = by_z(third, 3)
     one_away = by_z(jnp.where(lax.div(z, 2) == x, sent, two_away), 1)
     far = by_depth(near, 1)
-    own_turned, own_square = call(
-        own_kernel,
-        "own_blocks",
-        8 * cube,
-        (density,),
-        (shape(2, 2 * blk, half), shape(2, blk, half, dtype=jnp.float32)),
-    )
     own0 = call(
         stack_kernel,
         "stack",
         0,
-        (two_away, one_away, three_away, own_turned),
+        (two_away, one_away, three_away),
         (shape(3, half, half),),
-        order_only=1,
     )[0]
     oth0, own2 = by_x(own0), by_depth(own0, 2)
     own1 = by_depth(own0, 1)
-    oth2a = by_depth(oth0[:, : half // 2], 2)
-    oth2b = by_x(own2[:, half // 2 :])
+    row, columns = call(
+        first_kernel, "first_blocks", 2 * cube, (density, own0, own1), (row_shape, columns_shape)
+    )
+    diagonal = call(
+        cross_kernel, "cross", 0, (oth0, own2, row), (shape(3, half, half),), order_only=1
+    )[0]
+    oth2 = crossed(diagonal)
     own3, oth1 = by_depth(own2, 1), by_depth(oth0, 1)
     row, columns, square, partial = call(
         middle_kernel,
         "middle_blocks",
         30 * cube,
-        (density, own_turned, own_square, near, far, own0, own1, own2, own3, oth0, oth1),
+        (row, columns, near, far, own2, own3, oth0, oth1),
         (row_shape, columns_shape, row_shape, shape(4, blk, half, dtype=jnp.float32)),
-    )
-    oth2a, oth2b, partial = lax.optimization_barrier((oth2a, oth2b, partial))
-    oth3a, oth3b = by_depth(oth2a, 1), by_depth(oth2b, 1)
+        {0: 0, 1: 1},
+    )
+    oth2, partial = lax.optimization_barrier((oth2, partial))
+    oth3 = by_depth(oth2, 1)
     partial_shape = shape(4, blk, half, dtype=jnp.float32)
-    columns, partial = call(
+    out_shape = shape(blk, half, dtype=jnp.float32)
+    columns, partial, early = call(
         finish_kernel,
         "finish_blocks",
         4 * cube,
-        (row, columns, partial, oth2a, oth2b),
-        (columns_shape, partial_shape),
+        (row, columns, partial, square, oth2),
+        (columns_shape, partial_shape, out_shape),
         {1: 0, 2: 1},
     )
     return call(
         last_kernel,
         "last_blocks",
         8 * cube,
-        (row, columns, square, partial, oth3a, oth3b),
-        (shape(blk, half, dtype=jnp.float32), columns_shape, row_shape, partial_shape),
+        (row, columns, square, partial, early, oth3),
+        (out_shape, columns_shape, row_shape, partial_shape),
         {1: 1, 2: 2, 3: 3},
     )[0]
 

time: 43.3 us -> 42.7 us (0.986)
  starting transfers between devices: 22 us -> 20.4 us
  waiting for transfers between devices: 9.14 us -> 10.1 us
    ppermute x8 -> x6, starting transfers between devices: 8.6 us -> 7.05 us  [by_depth(): lax.ppermute(v, 'depth', [(i, i ^ m) for i in range(lax.axis_size('depth'...]
    ppermute x0 -> x1, waiting for transfers between devices: none -> 0.87 us  [crossed(): return lax.ppermute(v, ('col', 'depth'), pairs)]
    ppermute x3, waiting for transfers between devices: 2.73 us -> 3.47 us  [by_z(): lax.ppermute(v, 'row', [(i, i ^ m) for i in range(lax.axis_size('row'))])]
    ppermute x3 -> x2, waiting for transfers between devices: 5.82 us -> 5.33 us  [by_x(): lax.ppermute(v, 'col', [(i, i ^ 1) for i in range(lax.axis_size('col'))])]
    ppermute x3 -> x2, starting transfers between devices: 2.91 us -> 2.59 us  [by_x(): lax.ppermute(v, 'col', [(i, i ^ 1) for i in range(lax.axis_size('col'))])]
    pallas_call x7 -> x8, Pallas kernels: 9.71 us -> 9.79 us  [call(): pl.pallas_call(kernel, out_shape=outs, in_specs=[pl.BlockSpec(memory_spac...]
  transfers between devices with their start and end apart: 14 -> 12, of which waited for: 7 -> 7; matrix products, arithmetic and copies ran while one was open for 0% -> 0% of each run, Pallas kernels for 17% -> 18%
where the time goes in v4:
time: 42.7 us; the launch traced here: 42.5 us
  starting transfers between devices  20.4 us (48%)
  waiting for transfers between devices  10.1 us (24%)
  Pallas kernels  9.79 us (23%)
  local copies, waits for them, and re-layouts  2.14 us (5%)
    ppermute x3, starting transfers between devices, by_z(): lax.ppermute(v, 'row', [(i, i ^ m) for i in range(lax.axis_size('row'))])  10.4 us
    pallas_call x8, Pallas kernels, call(): pl.pallas_call(kernel, out_shape=outs, in_specs=[pl.BlockSpec(memory_spac...  9.79 us
    ppermute x6, starting transfers between devices, by_depth(): lax.ppermute(v, 'depth', [(i, i ^ m) for i in range(lax.axis_size('depth'...  7.05 us
    ppermute x2, waiting for transfers between devices, by_x(): lax.ppermute(v, 'col', [(i, i ^ 1) for i in range(lax.axis_size('col'))])  5.33 us
    ppermute x3, waiting for transfers between devices, by_z(): lax.ppermute(v, 'row', [(i, i ^ m) for i in range(lax.axis_size('row'))])  3.47 us
    ppermute x2, starting transfers between devices, by_x(): lax.ppermute(v, 'col', [(i, i ^ 1) for i in range(lax.axis_size('col'))])  2.59 us
    unnamed x4, local copies, waits for them, and re-layouts  1.23 us
    dynamic_slice x1, local copies, waits for them, and re-layouts, quarter(): lax.dynamic_slice(array, (y * half, k * blk + c * half), (half, half))  0.91 us
  transfers between devices with their start and end apart: 12, of which 7 were waited for; matrix products, arithmetic and copies ran while one was open for 0% of the time, Pallas kernels for 18%

profile of v4, /device:TPU:17, one launch (start us, length us, event | category | flops | bytes accessed | tf_op | source)
XLA Modules:
  0.0 42.5 jit_solution(2508041347385656432)
XLA Ops:
  0.0 0.9 %dynamic_slice.3.before = bf16[256,256]{1,0:T(8,128)(2,1)S(1)} dynamic-slice(bf16[512,1024]{1,0:T(8,128)(2,1)} %own.1, s32[]{:T(128)S(6)} %select_n.14, s32[]{:T(128)S(6)} %select_n.15), dynamic_slice_sizes={256,256} | dynamic-slice | bytes 262148 | tf_op jit(solution)/shard_map/dynamic_slice | solution.py:311
  0.9 0.1 collective-permute-start
  1.0 0.0 copy-start
  1.0 1.2 %copy-done = bf16[512,1024]{1,0:T(8,128)(2,1)S(1)} copy-done((bf16[512,1024]{1,0:T(8,128)(2,1)S(1)}, bf16[512,1024]{1,0:T(8,128)(2,1)}, u32[]{:S(2)}) %copy-start) | copy-done | bytes 1048600
  2.3 0.0 copy-start.1
  2.3 1.3 %collective-permute-start.4 = (bf16[256,1024]{1,0:T(8,128)(2,1)S(1)}, bf16[256,1024]{1,0:T(8,128)(2,1)S(1)}, u32[]{:S(2)}, u32[]{:S(2)}) collective-permute-start(bf16[256,1024]{1,0:T(8,128)(2,1)S(1)} %half_row.1.before), channel_id=1, source_target_pairs={{0,4},{4,0},{1,5},{5,1},{2,6},{6,2},{3,7},{7,3},{8,12},{12,8},{9,1... | collective-permute-start | bytes 1572872 | tf_op jit(solution)/shard_map/ppermute | solution.py:300
  3.6 2.5 %collective-permute-start.2 = (bf16[256,256]{1,0:T(8,128)(2,1)S(1)}, bf16[256,256]{1,0:T(8,128)(2,1)S(1)}, u32[]{:S(2)}, u32[]{:S(2)}) collective-permute-start(bf16[256,256]{1,0:T(8,128)(2,1)S(1)} %third.1), channel_id=1, source_target_pairs={{0,24},{8,16},{16,8},{24,0},{1,25},{9,17},{17,9},{25,1},{2,26},{10... | collective-permute-start | bytes 393224 | tf_op jit(solution)/shard_map/ppermute | solution.py:297
  6.1 0.1 collective-permute-done.a
  6.3 7.9 %collective-permute-start.1 = (bf16[256,256]{1,0:T(8,128)(2,1)S(1)}, bf16[256,256]{1,0:T(8,128)(2,1)S(1)}, u32[]{:S(2)}, u32[]{:S(2)}) collective-permute-start(bf16[256,256]{1,0:T(8,128)(2,1)S(1)} %broadcast_select_fusion), channel_id=1, source_target_pairs={{0,8},{8,0},{16,24},{24,16},{1,9},{9,1},{17,25},{25,17},{2,10},{10... | collective-permute-start | bytes 393224 | tf_op jit(solution)/shard_map/ppermute | solution.py:297
  14.2 1.5 %collective-permute-done.2.c = bf16[256,256]{1,0:T(8,128)(2,1)S(1)} collective-permute-done((bf16[256,256]{1,0:T(8,128)(2,1)S(1)}, bf16[256,256]{1,0:T(8,128)(2,1)S(1)}, u32[]{:S(2)}, u32[]{:S(2)}) %collective-permute-start.2) | collective-permute-done | bytes 131104 | tf_op jit(solution)/shard_map/ppermute | solution.py:297
  15.7 1.8 %collective-permute-done.1.b = bf16[256,256]{1,0:T(8,128)(2,1)S(1)} collective-permute-done((bf16[256,256]{1,0:T(8,128)(2,1)S(1)}, bf16[256,256]{1,0:T(8,128)(2,1)S(1)}, u32[]{:S(2)}, u32[]{:S(2)}) %collective-permute-start.1) | collective-permute-done | bytes 131104 | tf_op jit(solution)/shard_map/ppermute | solution.py:297
  17.6 1.3 %collective-permute-start.8 = (bf16[3,256,256]{2,1,0:T(8,128)(2,1)S(1)}, bf16[3,256,256]{2,1,0:T(8,128)(2,1)S(1)}, u32[]{:S(2)}, u32[]{:S(2)}) collective-permute-start(bf16[3,256,256]{2,1,0:T(8,128)(2,1)S(1)} %stack.1.own0), channel_id=1, source_target_pairs={{0,4},{4,0},{1,5},{5,1},{2,6},{6,2},{3,7},{7,3},{8,12},{12,8},{9,1... | collective-permute-start | bytes 1179656 | tf_op jit(solution)/shard_map/ppermute | solution.py:300
  18.8 1.2 %collective-permute-start.6 = (bf16[3,256,256]{2,1,0:T(8,128)(2,1)S(1)}, bf16[3,256,256]{2,1,0:T(8,128)(2,1)S(1)}, u32[]{:S(2)}, u32[]{:S(2)}) collective-permute-start(bf16[3,256,256]{2,1,0:T(8,128)(2,1)S(1)} %stack.1.own0), channel_id=1, source_target_pairs={{0,2},{1,3},{2,0},{3,1},{4,6},{5,7},{6,4},{7,5},{8,10},{9,11},{10,... | collective-permute-start | bytes 1179656 | tf_op jit(solution)/shard_map/ppermute | solution.py:303
  20.1 0.0 collective-permute-done.4.near
  20.1 1.7 %collective-permute-start.5 = (bf16[256,1024]{1,0:T(8,128)(2,1)S(1)}, bf16[256,1024]{1,0:T(8,128)(2,1)S(1)}, u32[]{:S(2)}, u32[]{:S(2)}) collective-permute-start(bf16[256,1024]{1,0:T(8,128)(2,1)S(1)} %collective-permute-done.4.near), channel_id=1, source_target_pairs={{0,1},{1,0},{2,3},{3,2},{4,5},{5,4},{6,7},{7,6},{8,9},{9,8},{10,11... | collective-permute-start | bytes 1572872 | tf_op jit(solution)/shard_map/ppermute | solution.py:303
  21.8 0.0 collective-permute-start.3
  21.8 5.3 %collective-permute-done.8.oth0.a = bf16[3,256,256]{2,1,0:T(8,128)(2,1)S(1)} collective-permute-done((bf16[3,256,256]{2,1,0:T(8,128)(2,1)S(1)}, bf16[3,256,256]{2,1,0:T(8,128)(2,1)S(1)}, u32[]{:S(2)}, u32[]{:S(2)}) %collective-permute-start.8) | collective-permute-done | bytes 393248 | tf_op jit(solution)/shard_map/ppermute | solution.py:300
  27.1 2.1 %collective-permute-start.9 = (bf16[3,256,256]{2,1,0:T(8,128)(2,1)S(1)}, bf16[3,256,256]{2,1,0:T(8,128)(2,1)S(1)}, u32[]{:S(2)}, u32[]{:S(2)}) collective-permute-start(bf16[3,256,256]{2,1,0:T(8,128)(2,1)S(1)} %collective-permute-done.8.oth0.a), channel_id=1, source_target_pairs={{0,1},{1,0},{2,3},{3,2},{4,5},{5,4},{6,7},{7,6},{8,9},{9,8},{10,11... | collective-permute-start | bytes 1179656 | tf_op jit(solution)/shard_map/ppermute | solution.py:303
  29.2 0.0 collective-permute-done.6.own2.b
  29.2 1.2 %collective-permute-start.7 = (bf16[3,256,256]{2,1,0:T(8,128)(2,1)S(1)}, bf16[3,256,256]{2,1,0:T(8,128)(2,1)S(1)}, u32[]{:S(2)}, u32[]{:S(2)}) collective-permute-start(bf16[3,256,256]{2,1,0:T(8,128)(2,1)S(1)} %collective-permute-done.6.own2.b), channel_id=1, source_target_pairs={{0,1},{1,0},{2,3},{3,2},{4,5},{5,4},{6,7},{7,6},{8,9},{9,8},{10,11... | collective-permute-start | bytes 1179656 | tf_op jit(solution)/shard_map/ppermute | solution.py:303
  30.4 0.0 collective-permute-done.3.own1
  30.4 0.6 %first_blocks.1 = (bf16[512,2048]{1,0:T(8,128)(2,1)S(1)}, bf16[8,2048,256]{2,1,0:T(8,128)(2,1)S(1)}) custom-call(bf16[512,1024]{1,0:T(8,128)(2,1)S(1)} %copy-done.1, bf16[3,256,256]{2,1,0:T(8,128)(2,1)S(1)} %stack.1.own0, bf16[3,256,256]{2,1,0:T(8,128)(2,1)S(1)} %collective-permute-done.3.own1), custom_call_target="tpu_custom_call" | custom-call | flops 268435456 | tf_op jit(solution)/shard_map/first_blocks/pallas_call | solution.py:273
  31.1 0.3 collective-permute-start.10
  31.4 0.0 collective-permute-done.9.oth1
  31.4 0.3 collective-permute-done.7.own3
  31.7 0.0 collective-permute-done.5.far
  31.7 5.5 %middle_blocks.1 = (bf16[512,2048]{1,0:T(8,128)(2,1)S(1)}, bf16[8,2048,256]{2,1,0:T(8,128)(2,1)S(1)}, bf16[512,2048]{1,0:T(8,128)(2,1)S(1)}, f32[4,512,256]{2,1,0:T(8,128)S(1)}) custom-call(bf16[512,2048]{1,0:T(8,128)(2,1)S(1)} %get-tuple-element.17.row_in.before, ...), custom_call_target="tpu_custom_call", output_to_operand_aliasing={{0}: (0, {}), {1}: (1, {})} | custom-call | flops 4026531840 | tf_op jit(solution)/shard_map/middle_blocks/pallas_call | solution.py:273
  37.2 0.9 %collective-permute-done.10.oth2 = bf16[3,256,256]{2,1,0:T(8,128)(2,1)S(1)} collective-permute-done((bf16[3,256,256]{2,1,0:T(8,128)(2,1)S(1)}, bf16[3,256,256]{2,1,0:T(8,128)(2,1)S(1)}, u32[]{:S(2)}, u32[]{:S(2)}) %collective-permute-start.10) | collective-permute-done | bytes 393248 | tf_op jit(solution)/shard_map/ppermute | solution.py:308
  38.1 0.9 %collective-permute-start.11 = (bf16[3,256,256]{2,1,0:T(8,128)(2,1)S(1)}, bf16[3,256,256]{2,1,0:T(8,128)(2,1)S(1)}, u32[]{:S(2)}, u32[]{:S(2)}) collective-permute-start(bf16[3,256,256]{2,1,0:T(8,128)(2,1)S(1)} %collective-permute-done.10.oth2), channel_id=1, source_target_pairs={{0,1},{1,0},{2,3},{3,2},{4,5},{5,4},{6,7},{7,6},{8,9},{9,8},{10,11... | collective-permute-start | bytes 1179656 | tf_op jit(solution)/shard_map/ppermute | solution.py:303
  38.9 1.3 %finish_blocks.1 = (bf16[8,2048,256]{2,1,0:T(8,128)(2,1)S(1)}, f32[4,512,256]{2,1,0:T(8,128)S(1)}, f32[512,256]{1,0:T(8,128)S(1)}) custom-call(bf16[512,2048]{1,0:T(8,128)(2,1)S(1)} %get-tuple-element.19.row, bf16[8,2048,256]{2,1,0:T(8,128)(2,1)S(1)} %get-tuple-element.20.columns_in, ...), custom_call_target="tpu_custom_call", output_to_operand_aliasing={{0}: (1, {}), {1}: (2, {})} | custom-call | flops 536870912 | tf_op jit(solution)/shard_map/finish_blocks/pallas_call | solution.py:273
  40.2 0.1 collective-permute-done.11.oth3
  40.3 2.3 %last_blocks.1 = (f32[512,256]{1,0:T(8,128)}, bf16[8,2048,256]{2,1,0:T(8,128)(2,1)S(1)}, bf16[512,2048]{1,0:T(8,128)(2,1)S(1)}, f32[4,512,256]{2,1,0:T(8,128)S(1)}) custom-call(bf16[512,2048]{1,0:T(8,128)(2,1)S(1)} %get-tuple-element.19.row, ...), custom_call_target="tpu_custom_call", output_to_operand_aliasing={{1}: (1, {}), {2}: (2, {}), {3}: (3, {})} | custom-call | flops 1073741824 | tf_op jit(solution)/shard_map/last_blocks/pallas_call | solution.py:273
  (6 shorter events, 0.2 us)
Async XLA Ops:
  0.9 5.4 %collective-permute-start = (bf16[256,256]{1,0:T(8,128)(2,1)S(1)}, bf16[256,256]{1,0:T(8,128)(2,1)S(1)}, u32[]{:S(2)}, u32[]{:S(2)}) collective-permute-start(bf16[256,256]{1,0:T(8,128)(2,1)S(1)} %dynamic_slice.3.before), channel_id=1, source_target_pairs={{0,16},{8,24},{16,0},{24,8},{1,17},{9,25},{17,1},{25,9},{2,18},{10... | collective-permute-start | bytes 393224 | tf_op jit(solution)/shard_map/ppermute | solution.py:297
  1.0 1.2 %copy-start = (bf16[512,1024]{1,0:T(8,128)(2,1)S(1)}, bf16[512,1024]{1,0:T(8,128)(2,1)}, u32[]{:S(2)}) copy-start(bf16[512,1024]{1,0:T(8,128)(2,1)} %own.1) | copy-start | bytes 3145732
  2.3 4.0 %copy-start.1 = (bf16[512,1024]{1,0:T(8,128)(2,1)S(1)}, bf16[512,1024]{1,0:T(8,128)(2,1)}, u32[]{:S(2)}) copy-start(bf16[512,1024]{1,0:T(8,128)(2,1)} %own.1) | copy-start | bytes 3145732
  2.3 17.8 %collective-permute-start.4 = (bf16[256,1024]{1,0:T(8,128)(2,1)S(1)}, bf16[256,1024]{1,0:T(8,128)(2,1)S(1)}, u32[]{:S(2)}, u32[]{:S(2)}) collective-permute-start(bf16[256,1024]{1,0:T(8,128)(2,1)S(1)} %half_row.1.before), channel_id=1, source_target_pairs={{0,4},{4,0},{1,5},{5,1},{2,6},{6,2},{3,7},{7,3},{8,12},{12,8},{9,1... | collective-permute-start | bytes 1572872 | tf_op jit(solution)/shard_map/ppermute | solution.py:300
  3.6 12.1 %collective-permute-start.2 = (bf16[256,256]{1,0:T(8,128)(2,1)S(1)}, bf16[256,256]{1,0:T(8,128)(2,1)S(1)}, u32[]{:S(2)}, u32[]{:S(2)}) collective-permute-start(bf16[256,256]{1,0:T(8,128)(2,1)S(1)} %third.1), channel_id=1, source_target_pairs={{0,24},{8,16},{16,8},{24,0},{1,25},{9,17},{17,9},{25,1},{2,26},{10... | collective-permute-start | bytes 393224 | tf_op jit(solution)/shard_map/ppermute | solution.py:297
  6.3 11.2 %collective-permute-start.1 = (bf16[256,256]{1,0:T(8,128)(2,1)S(1)}, bf16[256,256]{1,0:T(8,128)(2,1)S(1)}, u32[]{:S(2)}, u32[]{:S(2)}) collective-permute-start(bf16[256,256]{1,0:T(8,128)(2,1)S(1)} %broadcast_select_fusion), channel_id=1, source_target_pairs={{0,8},{8,0},{16,24},{24,16},{1,9},{9,1},{17,25},{25,17},{2,10},{10... | collective-permute-start | bytes 393224 | tf_op jit(solution)/shard_map/ppermute | solution.py:297
  17.6 9.5 %collective-permute-start.8 = (bf16[3,256,256]{2,1,0:T(8,128)(2,1)S(1)}, bf16[3,256,256]{2,1,0:T(8,128)(2,1)S(1)}, u32[]{:S(2)}, u32[]{:S(2)}) collective-permute-start(bf16[3,256,256]{2,1,0:T(8,128)(2,1)S(1)} %stack.1.own0), channel_id=1, source_target_pairs={{0,4},{4,0},{1,5},{5,1},{2,6},{6,2},{3,7},{7,3},{8,12},{12,8},{9,1... | collective-permute-start | bytes 1179656 | tf_op jit(solution)/shard_map/ppermute | solution.py:300
  18.8 10.3 %collective-permute-start.6 = (bf16[3,256,256]{2,1,0:T(8,128)(2,1)S(1)}, bf16[3,256,256]{2,1,0:T(8,128)(2,1)S(1)}, u32[]{:S(2)}, u32[]{:S(2)}) collective-permute-start(bf16[3,256,256]{2,1,0:T(8,128)(2,1)S(1)} %stack.1.own0), channel_id=1, source_target_pairs={{0,2},{1,3},{2,0},{3,1},{4,6},{5,7},{6,4},{7,5},{8,10},{9,11},{10,... | collective-permute-start | bytes 1179656 | tf_op jit(solution)/shard_map/ppermute | solution.py:303
  20.1 11.6 %collective-permute-start.5 = (bf16[256,1024]{1,0:T(8,128)(2,1)S(1)}, bf16[256,1024]{1,0:T(8,128)(2,1)S(1)}, u32[]{:S(2)}, u32[]{:S(2)}) collective-permute-start(bf16[256,1024]{1,0:T(8,128)(2,1)S(1)} %collective-permute-done.4.near), channel_id=1, source_target_pairs={{0,1},{1,0},{2,3},{3,2},{4,5},{5,4},{6,7},{7,6},{8,9},{9,8},{10,11... | collective-permute-start | bytes 1572872 | tf_op jit(solution)/shard_map/ppermute | solution.py:303
  21.8 8.6 %collective-permute-start.3 = (bf16[3,256,256]{2,1,0:T(8,128)(2,1)S(1)}, bf16[3,256,256]{2,1,0:T(8,128)(2,1)S(1)}, u32[]{:S(2)}, u32[]{:S(2)}) collective-permute-start(bf16[3,256,256]{2,1,0:T(8,128)(2,1)S(1)} %stack.1.own0), channel_id=1, source_target_pairs={{0,1},{1,0},{2,3},{3,2},{4,5},{5,4},{6,7},{7,6},{8,9},{9,8},{10,11... | collective-permute-start | bytes 1179656 | tf_op jit(solution)/shard_map/ppermute | solution.py:303
  27.1 4.3 %collective-permute-start.9 = (bf16[3,256,256]{2,1,0:T(8,128)(2,1)S(1)}, bf16[3,256,256]{2,1,0:T(8,128)(2,1)S(1)}, u32[]{:S(2)}, u32[]{:S(2)}) collective-permute-start(bf16[3,256,256]{2,1,0:T(8,128)(2,1)S(1)} %collective-permute-done.8.oth0.a), channel_id=1, source_target_pairs={{0,1},{1,0},{2,3},{3,2},{4,5},{5,4},{6,7},{7,6},{8,9},{9,8},{10,11... | collective-permute-start | bytes 1179656 | tf_op jit(solution)/shard_map/ppermute | solution.py:303
  29.2 2.6 %collective-permute-start.7 = (bf16[3,256,256]{2,1,0:T(8,128)(2,1)S(1)}, bf16[3,256,256]{2,1,0:T(8,128)(2,1)S(1)}, u32[]{:S(2)}, u32[]{:S(2)}) collective-permute-start(bf16[3,256,256]{2,1,0:T(8,128)(2,1)S(1)} %collective-permute-done.6.own2.b), channel_id=1, source_target_pairs={{0,1},{1,0},{2,3},{3,2},{4,5},{5,4},{6,7},{7,6},{8,9},{9,8},{10,11... | collective-permute-start | bytes 1179656 | tf_op jit(solution)/shard_map/ppermute | solution.py:303
  31.1 7.0 %collective-permute-start.10 = (bf16[3,256,256]{2,1,0:T(8,128)(2,1)S(1)}, bf16[3,256,256]{2,1,0:T(8,128)(2,1)S(1)}, u32[]{:S(2)}, u32[]{:S(2)}) collective-permute-start(bf16[3,256,256]{2,1,0:T(8,128)(2,1)S(1)} %cross.1), channel_id=1, source_target_pairs={{0,2},{1,5},{2,0},{3,7},{4,6},{5,1},{6,4},{7,3},{8,10},{9,13},{10,... | collective-permute-start | bytes 1179656 | tf_op jit(solution)/shard_map/ppermute | solution.py:308
  38.1 2.2 %collective-permute-start.11 = (bf16[3,256,256]{2,1,0:T(8,128)(2,1)S(1)}, bf16[3,256,256]{2,1,0:T(8,128)(2,1)S(1)}, u32[]{:S(2)}, u32[]{:S(2)}) collective-permute-start(bf16[3,256,256]{2,1,0:T(8,128)(2,1)S(1)} %collective-permute-done.10.oth2), channel_id=1, source_target_pairs={{0,1},{1,0},{2,3},{3,2},{4,5},{5,4},{6,7},{7,6},{8,9},{9,8},{10,11... | collective-permute-start | bytes 1179656 | tf_op jit(solution)/shard_map/ppermute | solution.py:303

commit v5 on v4

--- a/solution.py
+++ b/solution.py
@@ -161,8 +161,8 @@
     fetch(density.at[lanes(y, half), lanes(2 * (1 - picked(z, x)) + c, half)], out, sem)
 
 
-def first_kernel(own, own0, own1, row, columns):
-    z, x, _, _, _ = place()
+def first_kernel(own, own0, row, columns):
+    z, x, _, y, c = place()
     blk, half = own.shape[0], columns.shape[2]
     for b in range(2):
         m = (2 * x + b) ^ z
@@ -172,7 +172,14 @@
             columns[2 * m + h, :blk] = part
             for g in range(2):
                 columns[g, lanes(2 * m + h, half)] = turned(part[g * half : (g + 1) * half])
-    put_strip(columns, 0, 0, lambda s: own0[s], lambda s: own1[s])
+    for slot in range(3):
+        i, k = received(slot, 0)
+        put(columns, 2 * i + y, 2 * k + c, own0[slot])
+
+
+def pass_kernel(a, before, out):
+    del before
+    out[...] = a[...]
 
 
 def cross_kernel(a, b, before, out):
@@ -188,7 +195,7 @@
         out[...] = b[...]
 
 
-def middle_kernel(row_in, columns_in, near, far, own2, own3, oth0, oth1, row, columns, square, partial):
+def middle_kernel(row_in, columns_in, near, far, own1, own2, own3, oth0, oth1, row, columns, square, partial):
     del row_in, columns_in
     z, x, _, y, c = place()
     blk, half = near.shape[1] // 2, columns.shape[2]
@@ -196,6 +203,9 @@
         m = (2 * (1 - x) + b) ^ z
         put_row(row, columns, m, c, near[:, b * blk : (b + 1) * blk])
         put_row(row, columns, m, 1 - c, far[:, b * blk : (b + 1) * blk])
+    for slot in range(3):
+        i, k = received(slot, 0)
+        put(columns, 2 * i + y, 2 * k + 1 - c, own1[slot])
     put_strip(columns, 0, 1, lambda s: own2[s], lambda s: own3[s])
     put_strip(columns, 1, 0, lambda s: oth0[s], lambda s: oth1[s])
     nothing = jnp.zeros((half, half), columns.dtype)
@@ -350,18 +360,20 @@
     oth0, own2 = by_x(own0), by_depth(own0, 2)
     own1 = by_depth(own0, 1)
     row, columns = call(
-        first_kernel, "first_blocks", 2 * cube, (density, own0, own1), (row_shape, columns_shape)
-    )
+        first_kernel, "first_blocks", 2 * cube, (density, own0), (row_shape, columns_shape)
+    )
+    quarters = shape(3, half, half)
+    oth1 = by_depth(call(pass_kernel, "oth0", 0, (oth0, row), (quarters,), order_only=1)[0], 1)
+    own3 = by_depth(call(pass_kernel, "own2", 0, (own2, row), (quarters,), order_only=1)[0], 1)
     diagonal = call(
         cross_kernel, "cross", 0, (oth0, own2, row), (shape(3, half, half),), order_only=1
     )[0]
     oth2 = crossed(diagonal)
-    own3, oth1 = by_depth(own2, 1), by_depth(oth0, 1)
     row, columns, square, partial = call(
         middle_kernel,
         "middle_blocks",
         30 * cube,
-        (row, columns, near, far, own2, own3, oth0, oth1),
+        (row, columns, near, far, own1, own2, own3, oth0, oth1),
         (row_shape, columns_shape, row_shape, shape(4, blk, half, dtype=jnp.float32)),
         {0: 0, 1: 1},
     )

time: 42.7 us -> 42.2 us (0.988)
  waiting for transfers between devices: 10.1 us -> 8.47 us
  starting transfers between devices: 20.4 us -> 21.5 us
    ppermute x2, waiting for transfers between devices: 5.33 us -> 0.01 us  [by_x(): lax.ppermute(v, 'col', [(i, i ^ 1) for i in range(lax.axis_size('col'))])]
    ppermute x6, waiting for transfers between devices: 0.4 us -> 4.88 us  [by_depth(): lax.ppermute(v, 'depth', [(i, i ^ m) for i in range(lax.axis_size('depth'...]
    ppermute x1, starting transfers between devices: 0.32 us -> 1.28 us  [crossed(): return lax.ppermute(v, ('col', 'depth'), pairs)]
    ppermute x1, waiting for transfers between devices: 0.87 us -> 0.11 us  [crossed(): return lax.ppermute(v, ('col', 'depth'), pairs)]
    pallas_call x8 -> x10, Pallas kernels: 9.79 us -> 9.82 us  [call(): pl.pallas_call(kernel, out_shape=outs, in_specs=[pl.BlockSpec(memory_spac...]
  transfers between devices with their start and end apart: 12 -> 12, of which waited for: 7 -> 6; matrix products, arithmetic and copies ran while one was open for 0% -> 0% of each run, Pallas kernels for 18% -> 18%
where the time goes in v5:
time: 42.2 us; the launch traced here: 42 us
  starting transfers between devices  21.5 us (51%)
  Pallas kernels  9.82 us (23%)
  waiting for transfers between devices  8.47 us (20%)
  local copies, waits for them, and re-layouts  2.14 us (5%)
    ppermute x3, starting transfers between devices, by_z(): lax.ppermute(v, 'row', [(i, i ^ m) for i in range(lax.axis_size('row'))])  10.4 us
    pallas_call x10, Pallas kernels, call(): pl.pallas_call(kernel, out_shape=outs, in_specs=[pl.BlockSpec(memory_spac...  9.82 us
    ppermute x6, starting transfers between devices, by_depth(): lax.ppermute(v, 'depth', [(i, i ^ m) for i in range(lax.axis_size('depth'...  7.21 us
    ppermute x6, waiting for transfers between devices, by_depth(): lax.ppermute(v, 'depth', [(i, i ^ m) for i in range(lax.axis_size('depth'...  4.88 us
    ppermute x3, waiting for transfers between devices, by_z(): lax.ppermute(v, 'row', [(i, i ^ m) for i in range(lax.axis_size('row'))])  3.47 us
    ppermute x2, starting transfers between devices, by_x(): lax.ppermute(v, 'col', [(i, i ^ 1) for i in range(lax.axis_size('col'))])  2.53 us
    ppermute x1, starting transfers between devices, crossed(): return lax.ppermute(v, ('col', 'depth'), pairs)  1.28 us
    unnamed x4, local copies, waits for them, and re-layouts  1.23 us
  transfers between devices with their start and end apart: 12, of which 6 were waited for; matrix products, arithmetic and copies ran while one was open for 0% of the time, Pallas kernels for 18%

profile of v5, /device:TPU:17, one launch (start us, length us, event | category | flops | bytes accessed | tf_op | source)
XLA Modules:
  0.0 42.0 jit_solution(7829291439295588008)
XLA Ops:
  0.0 0.9 %dynamic_slice.3.before = bf16[256,256]{1,0:T(8,128)(2,1)S(1)} dynamic-slice(bf16[512,1024]{1,0:T(8,128)(2,1)} %own.1, s32[]{:T(128)S(6)} %select_n.14, s32[]{:T(128)S(6)} %select_n.15), dynamic_slice_sizes={256,256} | dynamic-slice | bytes 262148 | tf_op jit(solution)/shard_map/dynamic_slice | solution.py:321
  0.9 0.1 collective-permute-start
  1.0 0.0 copy-start
  1.0 1.2 %copy-done = bf16[512,1024]{1,0:T(8,128)(2,1)S(1)} copy-done((bf16[512,1024]{1,0:T(8,128)(2,1)S(1)}, bf16[512,1024]{1,0:T(8,128)(2,1)}, u32[]{:S(2)}) %copy-start) | copy-done | bytes 1048600
  2.3 0.0 copy-start.1
  2.3 1.3 %collective-permute-start.3 = (bf16[256,1024]{1,0:T(8,128)(2,1)S(1)}, bf16[256,1024]{1,0:T(8,128)(2,1)S(1)}, u32[]{:S(2)}, u32[]{:S(2)}) collective-permute-start(bf16[256,1024]{1,0:T(8,128)(2,1)S(1)} %half_row.1.before), channel_id=1, source_target_pairs={{0,4},{4,0},{1,5},{5,1},{2,6},{6,2},{3,7},{7,3},{8,12},{12,8},{9,1... | collective-permute-start | bytes 1572872 | tf_op jit(solution)/shard_map/ppermute | solution.py:310
  3.6 2.5 %collective-permute-start.2 = (bf16[256,256]{1,0:T(8,128)(2,1)S(1)}, bf16[256,256]{1,0:T(8,128)(2,1)S(1)}, u32[]{:S(2)}, u32[]{:S(2)}) collective-permute-start(bf16[256,256]{1,0:T(8,128)(2,1)S(1)} %third.1), channel_id=1, source_target_pairs={{0,24},{8,16},{16,8},{24,0},{1,25},{9,17},{17,9},{25,1},{2,26},{10... | collective-permute-start | bytes 393224 | tf_op jit(solution)/shard_map/ppermute | solution.py:307
  6.1 0.1 collective-permute-done.a
  6.3 7.9 %collective-permute-start.1 = (bf16[256,256]{1,0:T(8,128)(2,1)S(1)}, bf16[256,256]{1,0:T(8,128)(2,1)S(1)}, u32[]{:S(2)}, u32[]{:S(2)}) collective-permute-start(bf16[256,256]{1,0:T(8,128)(2,1)S(1)} %broadcast_select_fusion), channel_id=1, source_target_pairs={{0,8},{8,0},{16,24},{24,16},{1,9},{9,1},{17,25},{25,17},{2,10},{10... | collective-permute-start | bytes 393224 | tf_op jit(solution)/shard_map/ppermute | solution.py:307
  14.2 1.5 %collective-permute-done.2.c = bf16[256,256]{1,0:T(8,128)(2,1)S(1)} collective-permute-done((bf16[256,256]{1,0:T(8,128)(2,1)S(1)}, bf16[256,256]{1,0:T(8,128)(2,1)S(1)}, u32[]{:S(2)}, u32[]{:S(2)}) %collective-permute-start.2) | collective-permute-done | bytes 131104 | tf_op jit(solution)/shard_map/ppermute | solution.py:307
  15.7 1.8 %collective-permute-done.1.b = bf16[256,256]{1,0:T(8,128)(2,1)S(1)} collective-permute-done((bf16[256,256]{1,0:T(8,128)(2,1)S(1)}, bf16[256,256]{1,0:T(8,128)(2,1)S(1)}, u32[]{:S(2)}, u32[]{:S(2)}) %collective-permute-start.1) | collective-permute-done | bytes 131104 | tf_op jit(solution)/shard_map/ppermute | solution.py:307
  17.6 1.3 %collective-permute-start.6 = (bf16[3,256,256]{2,1,0:T(8,128)(2,1)S(1)}, bf16[3,256,256]{2,1,0:T(8,128)(2,1)S(1)}, u32[]{:S(2)}, u32[]{:S(2)}) collective-permute-start(bf16[3,256,256]{2,1,0:T(8,128)(2,1)S(1)} %stack.1.own0), channel_id=1, source_target_pairs={{0,2},{1,3},{2,0},{3,1},{4,6},{5,7},{6,4},{7,5},{8,10},{9,11},{10,... | collective-permute-start | bytes 1179656 | tf_op jit(solution)/shard_map/ppermute | solution.py:313
  18.9 1.2 %collective-permute-start.8 = (bf16[3,256,256]{2,1,0:T(8,128)(2,1)S(1)}, bf16[3,256,256]{2,1,0:T(8,128)(2,1)S(1)}, u32[]{:S(2)}, u32[]{:S(2)}) collective-permute-start(bf16[3,256,256]{2,1,0:T(8,128)(2,1)S(1)} %stack.1.own0), channel_id=1, source_target_pairs={{0,4},{4,0},{1,5},{5,1},{2,6},{6,2},{3,7},{7,3},{8,12},{12,8},{9,1... | collective-permute-start | bytes 1179656 | tf_op jit(solution)/shard_map/ppermute | solution.py:310
  20.1 0.0 collective-permute-done.3.near
  20.1 1.7 %collective-permute-start.4 = (bf16[256,1024]{1,0:T(8,128)(2,1)S(1)}, bf16[256,1024]{1,0:T(8,128)(2,1)S(1)}, u32[]{:S(2)}, u32[]{:S(2)}) collective-permute-start(bf16[256,1024]{1,0:T(8,128)(2,1)S(1)} %collective-permute-done.3.near), channel_id=1, source_target_pairs={{0,1},{1,0},{2,3},{3,2},{4,5},{5,4},{6,7},{7,6},{8,9},{9,8},{10,11... | collective-permute-start | bytes 1572872 | tf_op jit(solution)/shard_map/ppermute | solution.py:313
  21.8 0.0 collective-permute-start.5
  21.8 0.5 %first_blocks.1 = (bf16[512,2048]{1,0:T(8,128)(2,1)S(1)}, bf16[8,2048,256]{2,1,0:T(8,128)(2,1)S(1)}) custom-call(bf16[512,1024]{1,0:T(8,128)(2,1)S(1)} %copy-done.1, bf16[3,256,256]{2,1,0:T(8,128)(2,1)S(1)} %stack.1.own0), custom_call_target="tpu_custom_call" | custom-call | flops 268435456 | tf_op jit(solution)/shard_map/first_blocks/pallas_call | solution.py:283
  22.3 4.8 %collective-permute-done.6.a.own2.b = bf16[3,256,256]{2,1,0:T(8,128)(2,1)S(1)} collective-permute-done((bf16[3,256,256]{2,1,0:T(8,128)(2,1)S(1)}, bf16[3,256,256]{2,1,0:T(8,128)(2,1)S(1)}, u32[]{:S(2)}, u32[]{:S(2)}) %collective-permute-start.6) | collective-permute-done | bytes 393248 | tf_op jit(solution)/shard_map/ppermute | solution.py:313
  27.1 2.1 %collective-permute-start.7 = (bf16[3,256,256]{2,1,0:T(8,128)(2,1)S(1)}, bf16[3,256,256]{2,1,0:T(8,128)(2,1)S(1)}, u32[]{:S(2)}, u32[]{:S(2)}) collective-permute-start(bf16[3,256,256]{2,1,0:T(8,128)(2,1)S(1)} %own2.1), channel_id=1, source_target_pairs={{0,1},{1,0},{2,3},{3,2},{4,5},{5,4},{6,7},{7,6},{8,9},{9,8},{10,11... | collective-permute-start | bytes 1179656 | tf_op jit(solution)/shard_map/ppermute | solution.py:313
  29.3 0.0 collective-permute-done.8.a.oth0
  29.3 1.2 %collective-permute-start.9 = (bf16[3,256,256]{2,1,0:T(8,128)(2,1)S(1)}, bf16[3,256,256]{2,1,0:T(8,128)(2,1)S(1)}, u32[]{:S(2)}, u32[]{:S(2)}) collective-permute-start(bf16[3,256,256]{2,1,0:T(8,128)(2,1)S(1)} %oth0.1), channel_id=1, source_target_pairs={{0,1},{1,0},{2,3},{3,2},{4,5},{5,4},{6,7},{7,6},{8,9},{9,8},{10,11... | collective-permute-start | bytes 1179656 | tf_op jit(solution)/shard_map/ppermute | solution.py:313
  30.5 1.3 %collective-permute-start.10 = (bf16[3,256,256]{2,1,0:T(8,128)(2,1)S(1)}, bf16[3,256,256]{2,1,0:T(8,128)(2,1)S(1)}, u32[]{:S(2)}, u32[]{:S(2)}) collective-permute-start(bf16[3,256,256]{2,1,0:T(8,128)(2,1)S(1)} %cross.1), channel_id=1, source_target_pairs={{0,2},{1,5},{2,0},{3,7},{4,6},{5,1},{6,4},{7,3},{8,10},{9,13},{10,... | collective-permute-start | bytes 1179656 | tf_op jit(solution)/shard_map/ppermute | solution.py:318
  31.8 0.0 collective-permute-done.5.own1
  31.8 0.0 collective-permute-done.4.far
  31.8 0.0 collective-permute-done.7.own3
  31.8 0.0 collective-permute-done.9.oth1
  31.9 5.5 %middle_blocks.1 = (bf16[512,2048]{1,0:T(8,128)(2,1)S(1)}, bf16[8,2048,256]{2,1,0:T(8,128)(2,1)S(1)}, bf16[512,2048]{1,0:T(8,128)(2,1)S(1)}, f32[4,512,256]{2,1,0:T(8,128)S(1)}) custom-call(bf16[512,2048]{1,0:T(8,128)(2,1)S(1)} %get-tuple-element.17.before.row_in, ...), custom_call_target="tpu_custom_call", output_to_operand_aliasing={{0}: (0, {}), {1}: (1, {})} | custom-call | flops 4026531840 | tf_op jit(solution)/shard_map/middle_blocks/pallas_call | solution.py:283
  37.4 0.1 collective-permute-done.10.oth2
  37.5 0.9 %collective-permute-start.11 = (bf16[3,256,256]{2,1,0:T(8,128)(2,1)S(1)}, bf16[3,256,256]{2,1,0:T(8,128)(2,1)S(1)}, u32[]{:S(2)}, u32[]{:S(2)}) collective-permute-start(bf16[3,256,256]{2,1,0:T(8,128)(2,1)S(1)} %collective-permute-done.10.oth2), channel_id=1, source_target_pairs={{0,1},{1,0},{2,3},{3,2},{4,5},{5,4},{6,7},{7,6},{8,9},{9,8},{10,11... | collective-permute-start | bytes 1179656 | tf_op jit(solution)/shard_map/ppermute | solution.py:313
  38.4 1.3 %finish_blocks.1 = (bf16[8,2048,256]{2,1,0:T(8,128)(2,1)S(1)}, f32[4,512,256]{2,1,0:T(8,128)S(1)}, f32[512,256]{1,0:T(8,128)S(1)}) custom-call(bf16[512,2048]{1,0:T(8,128)(2,1)S(1)} %get-tuple-element.19.row, bf16[8,2048,256]{2,1,0:T(8,128)(2,1)S(1)} %get-tuple-element.20.columns_in, ...), custom_call_target="tpu_custom_call", output_to_operand_aliasing={{0}: (1, {}), {1}: (2, {})} | custom-call | flops 536870912 | tf_op jit(solution)/shard_map/finish_blocks/pallas_call | solution.py:283
  39.7 0.1 collective-permute-done.11.oth3
  39.8 2.3 %last_blocks.1 = (f32[512,256]{1,0:T(8,128)}, bf16[8,2048,256]{2,1,0:T(8,128)(2,1)S(1)}, bf16[512,2048]{1,0:T(8,128)(2,1)S(1)}, f32[4,512,256]{2,1,0:T(8,128)S(1)}) custom-call(bf16[512,2048]{1,0:T(8,128)(2,1)S(1)} %get-tuple-element.19.row, ...), custom_call_target="tpu_custom_call", output_to_operand_aliasing={{1}: (1, {}), {2}: (2, {}), {3}: (3, {})} | custom-call | flops 1073741824 | tf_op jit(solution)/shard_map/last_blocks/pallas_call | solution.py:283
  (8 shorter events, 0.2 us)
Async XLA Ops:
  0.9 5.4 %collective-permute-start = (bf16[256,256]{1,0:T(8,128)(2,1)S(1)}, bf16[256,256]{1,0:T(8,128)(2,1)S(1)}, u32[]{:S(2)}, u32[]{:S(2)}) collective-permute-start(bf16[256,256]{1,0:T(8,128)(2,1)S(1)} %dynamic_slice.3.before), channel_id=1, source_target_pairs={{0,16},{8,24},{16,0},{24,8},{1,17},{9,25},{17,1},{25,9},{2,18},{10... | collective-permute-start | bytes 393224 | tf_op jit(solution)/shard_map/ppermute | solution.py:307
  1.0 1.2 %copy-start = (bf16[512,1024]{1,0:T(8,128)(2,1)S(1)}, bf16[512,1024]{1,0:T(8,128)(2,1)}, u32[]{:S(2)}) copy-start(bf16[512,1024]{1,0:T(8,128)(2,1)} %own.1) | copy-start | bytes 3145732
  2.3 4.0 %copy-start.1 = (bf16[512,1024]{1,0:T(8,128)(2,1)S(1)}, bf16[512,1024]{1,0:T(8,128)(2,1)}, u32[]{:S(2)}) copy-start(bf16[512,1024]{1,0:T(8,128)(2,1)} %own.1) | copy-start | bytes 3145732
  2.3 17.8 %collective-permute-start.3 = (bf16[256,1024]{1,0:T(8,128)(2,1)S(1)}, bf16[256,1024]{1,0:T(8,128)(2,1)S(1)}, u32[]{:S(2)}, u32[]{:S(2)}) collective-permute-start(bf16[256,1024]{1,0:T(8,128)(2,1)S(1)} %half_row.1.before), channel_id=1, source_target_pairs={{0,4},{4,0},{1,5},{5,1},{2,6},{6,2},{3,7},{7,3},{8,12},{12,8},{9,1... | collective-permute-start | bytes 1572872 | tf_op jit(solution)/shard_map/ppermute | solution.py:310
  3.6 12.1 %collective-permute-start.2 = (bf16[256,256]{1,0:T(8,128)(2,1)S(1)}, bf16[256,256]{1,0:T(8,128)(2,1)S(1)}, u32[]{:S(2)}, u32[]{:S(2)}) collective-permute-start(bf16[256,256]{1,0:T(8,128)(2,1)S(1)} %third.1), channel_id=1, source_target_pairs={{0,24},{8,16},{16,8},{24,0},{1,25},{9,17},{17,9},{25,1},{2,26},{10... | collective-permute-start | bytes 393224 | tf_op jit(solution)/shard_map/ppermute | solution.py:307
  6.3 11.2 %collective-permute-start.1 = (bf16[256,256]{1,0:T(8,128)(2,1)S(1)}, bf16[256,256]{1,0:T(8,128)(2,1)S(1)}, u32[]{:S(2)}, u32[]{:S(2)}) collective-permute-start(bf16[256,256]{1,0:T(8,128)(2,1)S(1)} %broadcast_select_fusion), channel_id=1, source_target_pairs={{0,8},{8,0},{16,24},{24,16},{1,9},{9,1},{17,25},{25,17},{2,10},{10... | collective-permute-start | bytes 393224 | tf_op jit(solution)/shard_map/ppermute | solution.py:307
  17.6 9.5 %collective-permute-start.6 = (bf16[3,256,256]{2,1,0:T(8,128)(2,1)S(1)}, bf16[3,256,256]{2,1,0:T(8,128)(2,1)S(1)}, u32[]{:S(2)}, u32[]{:S(2)}) collective-permute-start(bf16[3,256,256]{2,1,0:T(8,128)(2,1)S(1)} %stack.1.own0), channel_id=1, source_target_pairs={{0,2},{1,3},{2,0},{3,1},{4,6},{5,7},{6,4},{7,5},{8,10},{9,11},{10,... | collective-permute-start | bytes 1179656 | tf_op jit(solution)/shard_map/ppermute | solution.py:313
  18.9 10.4 %collective-permute-start.8 = (bf16[3,256,256]{2,1,0:T(8,128)(2,1)S(1)}, bf16[3,256,256]{2,1,0:T(8,128)(2,1)S(1)}, u32[]{:S(2)}, u32[]{:S(2)}) collective-permute-start(bf16[3,256,256]{2,1,0:T(8,128)(2,1)S(1)} %stack.1.own0), channel_id=1, source_target_pairs={{0,4},{4,0},{1,5},{5,1},{2,6},{6,2},{3,7},{7,3},{8,12},{12,8},{9,1... | collective-permute-start | bytes 1179656 | tf_op jit(solution)/shard_map/ppermute | solution.py:310
  20.1 11.7 %collective-permute-start.4 = (bf16[256,1024]{1,0:T(8,128)(2,1)S(1)}, bf16[256,1024]{1,0:T(8,128)(2,1)S(1)}, u32[]{:S(2)}, u32[]{:S(2)}) collective-permute-start(bf16[256,1024]{1,0:T(8,128)(2,1)S(1)} %collective-permute-done.3.near), channel_id=1, source_target_pairs={{0,1},{1,0},{2,3},{3,2},{4,5},{5,4},{6,7},{7,6},{8,9},{9,8},{10,11... | collective-permute-start | bytes 1572872 | tf_op jit(solution)/shard_map/ppermute | solution.py:313
  21.8 10.0 %collective-permute-start.5 = (bf16[3,256,256]{2,1,0:T(8,128)(2,1)S(1)}, bf16[3,256,256]{2,1,0:T(8,128)(2,1)S(1)}, u32[]{:S(2)}, u32[]{:S(2)}) collective-permute-start(bf16[3,256,256]{2,1,0:T(8,128)(2,1)S(1)} %stack.1.own0), channel_id=1, source_target_pairs={{0,1},{1,0},{2,3},{3,2},{4,5},{5,4},{6,7},{7,6},{8,9},{9,8},{10,11... | collective-permute-start | bytes 1179656 | tf_op jit(solution)/shard_map/ppermute | solution.py:313
  27.1 4.7 %collective-permute-start.7 = (bf16[3,256,256]{2,1,0:T(8,128)(2,1)S(1)}, bf16[3,256,256]{2,1,0:T(8,128)(2,1)S(1)}, u32[]{:S(2)}, u32[]{:S(2)}) collective-permute-start(bf16[3,256,256]{2,1,0:T(8,128)(2,1)S(1)} %own2.1), channel_id=1, source_target_pairs={{0,1},{1,0},{2,3},{3,2},{4,5},{5,4},{6,7},{7,6},{8,9},{9,8},{10,11... | collective-permute-start | bytes 1179656 | tf_op jit(solution)/shard_map/ppermute | solution.py:313
  29.3 2.6 %collective-permute-start.9 = (bf16[3,256,256]{2,1,0:T(8,128)(2,1)S(1)}, bf16[3,256,256]{2,1,0:T(8,128)(2,1)S(1)}, u32[]{:S(2)}, u32[]{:S(2)}) collective-permute-start(bf16[3,256,256]{2,1,0:T(8,128)(2,1)S(1)} %oth0.1), channel_id=1, source_target_pairs={{0,1},{1,0},{2,3},{3,2},{4,5},{5,4},{6,7},{7,6},{8,9},{9,8},{10,11... | collective-permute-start | bytes 1179656 | tf_op jit(solution)/shard_map/ppermute | solution.py:313
  30.5 7.0 %collective-permute-start.10 = (bf16[3,256,256]{2,1,0:T(8,128)(2,1)S(1)}, bf16[3,256,256]{2,1,0:T(8,128)(2,1)S(1)}, u32[]{:S(2)}, u32[]{:S(2)}) collective-permute-start(bf16[3,256,256]{2,1,0:T(8,128)(2,1)S(1)} %cross.1), channel_id=1, source_target_pairs={{0,2},{1,5},{2,0},{3,7},{4,6},{5,1},{6,4},{7,3},{8,10},{9,13},{10,... | collective-permute-start | bytes 1179656 | tf_op jit(solution)/shard_map/ppermute | solution.py:318
  37.5 2.2 %collective-permute-start.11 = (bf16[3,256,256]{2,1,0:T(8,128)(2,1)S(1)}, bf16[3,256,256]{2,1,0:T(8,128)(2,1)S(1)}, u32[]{:S(2)}, u32[]{:S(2)}) collective-permute-start(bf16[3,256,256]{2,1,0:T(8,128)(2,1)S(1)} %collective-permute-done.10.oth2), channel_id=1, source_target_pairs={{0,1},{1,0},{2,3},{3,2},{4,5},{5,4},{6,7},{7,6},{8,9},{9,8},{10,11... | collective-permute-start | bytes 1179656 | tf_op jit(solution)/shard_map/ppermute | solution.py:313

commit v6 on v5

--- a/solution.py
+++ b/solution.py
@@ -226,15 +226,24 @@
 
 def add_last(row, columns, partial, last, cc):
     _, _, _, y, _ = place()
-    half = columns.shape[2]
+    half, s = columns.shape[2], wanted()
     quarters = [last[slot] for slot in range(3)]
     for slot, q in enumerate(quarters):
         i, k = received(slot, 1)
-        put(columns, 2 * i + 1 - y, 2 * k + cc, q)
+        there, across = 2 * i + 1 - y, 2 * k + cc
+
+        @pl.when(across == s)
+        def _(there=there, q=q):
+            columns[s, lanes(there, half)] = q
+
+        @pl.when(there == s)
+        def _(across=across, q=q):
+            columns[s, lanes(across, half)] = turned(q)
+
     two, one, three = quarters
 
-    def rows(s):
-        return row[:, lanes(s, half)]
+    def rows(h):
+        return row[:, lanes(h, half)]
 
     @pl.when(home() == 1)
     def _():
@@ -266,17 +275,17 @@
     cube[...] = acc
 
 
-def last_kernel(row, columns_in, square_in, partial_in, cube, oth3, out, columns, square, partial):
-    del columns_in, square_in, partial_in
+def last_kernel(row, columns_in, square, partial_in, cube, oth3, out, columns, partial):
+    del columns_in, partial_in
     half = columns.shape[2]
     add_last(row, columns, partial, oth3, 1 - place()[4])
     s = wanted()
-    acc = cube[...]
+    acc, own = cube[...], square[:, lanes(s, half)].astype(jnp.float32)
     for n, h in enumerate(late_halves()):
         part = partial[n].astype(square.dtype)
-        square[:, lanes(h, half)] = part
+        own = jnp.where(h == s, part.astype(jnp.float32), own)
         acc += dot(part, columns[s, lanes(h, half)])
-    out[...] = 3.0 * square[:, lanes(s, half)].astype(jnp.float32) - 2.0 * acc
+    out[...] = 3.0 * own - 2.0 * acc
 
 
 def call(kernel, name, flops, args, outs, aliases=None, order_only=0, scratch=()):
@@ -394,8 +403,8 @@
         "last_blocks",
         8 * cube,
         (row, columns, square, partial, early, oth3),
-        (out_shape, columns_shape, row_shape, partial_shape),
-        {1: 1, 2: 2, 3: 3},
+        (out_shape, columns_shape, partial_shape),
+        {1: 1, 3: 2},
     )[0]
 
 

time: 42.2 us -> 42.1 us (level)
  no operation moved by 1% of the time
where the time goes in v6:
time: 42.1 us; the launch traced here: 42 us
  starting transfers between devices  21.5 us (51%)
  Pallas kernels  9.73 us (23%)
  waiting for transfers between devices  8.49 us (20%)
  local copies, waits for them, and re-layouts  2.14 us (5%)
    ppermute x3, starting transfers between devices, by_z(): lax.ppermute(v, 'row', [(i, i ^ m) for i in range(lax.axis_size('row'))])  10.4 us
    pallas_call x10, Pallas kernels, call(): pl.pallas_call(kernel, out_shape=outs, in_specs=[pl.BlockSpec(memory_spac...  9.73 us
    ppermute x6, starting transfers between devices, by_depth(): lax.ppermute(v, 'depth', [(i, i ^ m) for i in range(lax.axis_size('depth'...  7.21 us
    ppermute x6, waiting for transfers between devices, by_depth(): lax.ppermute(v, 'depth', [(i, i ^ m) for i in range(lax.axis_size('depth'...  4.9 us
    ppermute x3, waiting for transfers between devices, by_z(): lax.ppermute(v, 'row', [(i, i ^ m) for i in range(lax.axis_size('row'))])  3.47 us
    ppermute x2, starting transfers between devices, by_x(): lax.ppermute(v, 'col', [(i, i ^ 1) for i in range(lax.axis_size('col'))])  2.53 us
    ppermute x1, starting transfers between devices, crossed(): return lax.ppermute(v, ('col', 'depth'), pairs)  1.28 us
    unnamed x4, local copies, waits for them, and re-layouts  1.23 us
  transfers between devices with their start and end apart: 12, of which 6 were waited for; matrix products, arithmetic and copies ran while one was open for 0% of the time, Pallas kernels for 18%

profile of v6, /device:TPU:17, one launch (start us, length us, event | category | flops | bytes accessed | tf_op | source)
XLA Modules:
  0.0 42.0 jit_solution(10211195608888076743)
XLA Ops:
  0.0 0.9 %dynamic_slice.3.before = bf16[256,256]{1,0:T(8,128)(2,1)S(1)} dynamic-slice(bf16[512,1024]{1,0:T(8,128)(2,1)} %own.1, s32[]{:T(128)S(6)} %select_n.14, s32[]{:T(128)S(6)} %select_n.15), dynamic_slice_sizes={256,256} | dynamic-slice | bytes 262148 | tf_op jit(solution)/shard_map/dynamic_slice | solution.py:330
  0.9 0.1 collective-permute-start
  1.0 0.0 copy-start
  1.0 1.2 %copy-done = bf16[512,1024]{1,0:T(8,128)(2,1)S(1)} copy-done((bf16[512,1024]{1,0:T(8,128)(2,1)S(1)}, bf16[512,1024]{1,0:T(8,128)(2,1)}, u32[]{:S(2)}) %copy-start) | copy-done | bytes 1048600
  2.3 0.0 copy-start.1
  2.3 1.3 %collective-permute-start.3 = (bf16[256,1024]{1,0:T(8,128)(2,1)S(1)}, bf16[256,1024]{1,0:T(8,128)(2,1)S(1)}, u32[]{:S(2)}, u32[]{:S(2)}) collective-permute-start(bf16[256,1024]{1,0:T(8,128)(2,1)S(1)} %half_row.1.before), channel_id=1, source_target_pairs={{0,4},{4,0},{1,5},{5,1},{2,6},{6,2},{3,7},{7,3},{8,12},{12,8},{9,1... | collective-permute-start | bytes 1572872 | tf_op jit(solution)/shard_map/ppermute | solution.py:319
  3.6 2.5 %collective-permute-start.2 = (bf16[256,256]{1,0:T(8,128)(2,1)S(1)}, bf16[256,256]{1,0:T(8,128)(2,1)S(1)}, u32[]{:S(2)}, u32[]{:S(2)}) collective-permute-start(bf16[256,256]{1,0:T(8,128)(2,1)S(1)} %third.1), channel_id=1, source_target_pairs={{0,24},{8,16},{16,8},{24,0},{1,25},{9,17},{17,9},{25,1},{2,26},{10... | collective-permute-start | bytes 393224 | tf_op jit(solution)/shard_map/ppermute | solution.py:316
  6.1 0.1 collective-permute-done.a
  6.3 7.9 %collective-permute-start.1 = (bf16[256,256]{1,0:T(8,128)(2,1)S(1)}, bf16[256,256]{1,0:T(8,128)(2,1)S(1)}, u32[]{:S(2)}, u32[]{:S(2)}) collective-permute-start(bf16[256,256]{1,0:T(8,128)(2,1)S(1)} %broadcast_select_fusion), channel_id=1, source_target_pairs={{0,8},{8,0},{16,24},{24,16},{1,9},{9,1},{17,25},{25,17},{2,10},{10... | collective-permute-start | bytes 393224 | tf_op jit(solution)/shard_map/ppermute | solution.py:316
  14.2 1.5 %collective-permute-done.2.c = bf16[256,256]{1,0:T(8,128)(2,1)S(1)} collective-permute-done((bf16[256,256]{1,0:T(8,128)(2,1)S(1)}, bf16[256,256]{1,0:T(8,128)(2,1)S(1)}, u32[]{:S(2)}, u32[]{:S(2)}) %collective-permute-start.2) | collective-permute-done | bytes 131104 | tf_op jit(solution)/shard_map/ppermute | solution.py:316
  15.7 1.8 %collective-permute-done.1.b = bf16[256,256]{1,0:T(8,128)(2,1)S(1)} collective-permute-done((bf16[256,256]{1,0:T(8,128)(2,1)S(1)}, bf16[256,256]{1,0:T(8,128)(2,1)S(1)}, u32[]{:S(2)}, u32[]{:S(2)}) %collective-permute-start.1) | collective-permute-done | bytes 131104 | tf_op jit(solution)/shard_map/ppermute | solution.py:316
  17.6 1.3 %collective-permute-start.6 = (bf16[3,256,256]{2,1,0:T(8,128)(2,1)S(1)}, bf16[3,256,256]{2,1,0:T(8,128)(2,1)S(1)}, u32[]{:S(2)}, u32[]{:S(2)}) collective-permute-start(bf16[3,256,256]{2,1,0:T(8,128)(2,1)S(1)} %stack.1.own0), channel_id=1, source_target_pairs={{0,2},{1,3},{2,0},{3,1},{4,6},{5,7},{6,4},{7,5},{8,10},{9,11},{10,... | collective-permute-start | bytes 1179656 | tf_op jit(solution)/shard_map/ppermute | solution.py:322
  18.9 1.2 %collective-permute-start.8 = (bf16[3,256,256]{2,1,0:T(8,128)(2,1)S(1)}, bf16[3,256,256]{2,1,0:T(8,128)(2,1)S(1)}, u32[]{:S(2)}, u32[]{:S(2)}) collective-permute-start(bf16[3,256,256]{2,1,0:T(8,128)(2,1)S(1)} %stack.1.own0), channel_id=1, source_target_pairs={{0,4},{4,0},{1,5},{5,1},{2,6},{6,2},{3,7},{7,3},{8,12},{12,8},{9,1... | collective-permute-start | bytes 1179656 | tf_op jit(solution)/shard_map/ppermute | solution.py:319
  20.1 0.0 collective-permute-done.3.near
  20.1 1.7 %collective-permute-start.4 = (bf16[256,1024]{1,0:T(8,128)(2,1)S(1)}, bf16[256,1024]{1,0:T(8,128)(2,1)S(1)}, u32[]{:S(2)}, u32[]{:S(2)}) collective-permute-start(bf16[256,1024]{1,0:T(8,128)(2,1)S(1)} %collective-permute-done.3.near), channel_id=1, source_target_pairs={{0,1},{1,0},{2,3},{3,2},{4,5},{5,4},{6,7},{7,6},{8,9},{9,8},{10,11... | collective-permute-start | bytes 1572872 | tf_op jit(solution)/shard_map/ppermute | solution.py:322
  21.8 0.0 collective-permute-start.5
  21.8 0.5 %first_blocks.1 = (bf16[512,2048]{1,0:T(8,128)(2,1)S(1)}, bf16[8,2048,256]{2,1,0:T(8,128)(2,1)S(1)}) custom-call(bf16[512,1024]{1,0:T(8,128)(2,1)S(1)} %copy-done.1, bf16[3,256,256]{2,1,0:T(8,128)(2,1)S(1)} %stack.1.own0), custom_call_target="tpu_custom_call" | custom-call | flops 268435456 | tf_op jit(solution)/shard_map/first_blocks/pallas_call | solution.py:292
  22.3 4.8 %collective-permute-done.6.a.own2.b = bf16[3,256,256]{2,1,0:T(8,128)(2,1)S(1)} collective-permute-done((bf16[3,256,256]{2,1,0:T(8,128)(2,1)S(1)}, bf16[3,256,256]{2,1,0:T(8,128)(2,1)S(1)}, u32[]{:S(2)}, u32[]{:S(2)}) %collective-permute-start.6) | collective-permute-done | bytes 393248 | tf_op jit(solution)/shard_map/ppermute | solution.py:322
  27.1 2.1 %collective-permute-start.7 = (bf16[3,256,256]{2,1,0:T(8,128)(2,1)S(1)}, bf16[3,256,256]{2,1,0:T(8,128)(2,1)S(1)}, u32[]{:S(2)}, u32[]{:S(2)}) collective-permute-start(bf16[3,256,256]{2,1,0:T(8,128)(2,1)S(1)} %own2.1), channel_id=1, source_target_pairs={{0,1},{1,0},{2,3},{3,2},{4,5},{5,4},{6,7},{7,6},{8,9},{9,8},{10,11... | collective-permute-start | bytes 1179656 | tf_op jit(solution)/shard_map/ppermute | solution.py:322
  29.3 0.0 collective-permute-done.8.a.oth0
  29.3 1.2 %collective-permute-start.9 = (bf16[3,256,256]{2,1,0:T(8,128)(2,1)S(1)}, bf16[3,256,256]{2,1,0:T(8,128)(2,1)S(1)}, u32[]{:S(2)}, u32[]{:S(2)}) collective-permute-start(bf16[3,256,256]{2,1,0:T(8,128)(2,1)S(1)} %oth0.1), channel_id=1, source_target_pairs={{0,1},{1,0},{2,3},{3,2},{4,5},{5,4},{6,7},{7,6},{8,9},{9,8},{10,11... | collective-permute-start | bytes 1179656 | tf_op jit(solution)/shard_map/ppermute | solution.py:322
  30.5 1.3 %collective-permute-start.10 = (bf16[3,256,256]{2,1,0:T(8,128)(2,1)S(1)}, bf16[3,256,256]{2,1,0:T(8,128)(2,1)S(1)}, u32[]{:S(2)}, u32[]{:S(2)}) collective-permute-start(bf16[3,256,256]{2,1,0:T(8,128)(2,1)S(1)} %cross.1), channel_id=1, source_target_pairs={{0,2},{1,5},{2,0},{3,7},{4,6},{5,1},{6,4},{7,3},{8,10},{9,13},{10,... | collective-permute-start | bytes 1179656 | tf_op jit(solution)/shard_map/ppermute | solution.py:327
  31.8 0.0 collective-permute-done.5.own1
  31.8 0.0 collective-permute-done.4.far
  31.8 0.0 collective-permute-done.7.own3
  31.8 0.0 collective-permute-done.9.oth1
  31.9 5.5 %middle_blocks.1 = (bf16[512,2048]{1,0:T(8,128)(2,1)S(1)}, bf16[8,2048,256]{2,1,0:T(8,128)(2,1)S(1)}, bf16[512,2048]{1,0:T(8,128)(2,1)S(1)}, f32[4,512,256]{2,1,0:T(8,128)S(1)}) custom-call(bf16[512,2048]{1,0:T(8,128)(2,1)S(1)} %get-tuple-element.17.before.row_in, ...), custom_call_target="tpu_custom_call", output_to_operand_aliasing={{0}: (0, {}), {1}: (1, {})} | custom-call | flops 4026531840 | tf_op jit(solution)/shard_map/middle_blocks/pallas_call | solution.py:292
  37.4 0.1 collective-permute-done.10.oth2
  37.5 0.9 %collective-permute-start.11 = (bf16[3,256,256]{2,1,0:T(8,128)(2,1)S(1)}, bf16[3,256,256]{2,1,0:T(8,128)(2,1)S(1)}, u32[]{:S(2)}, u32[]{:S(2)}) collective-permute-start(bf16[3,256,256]{2,1,0:T(8,128)(2,1)S(1)} %collective-permute-done.10.oth2), channel_id=1, source_target_pairs={{0,1},{1,0},{2,3},{3,2},{4,5},{5,4},{6,7},{7,6},{8,9},{9,8},{10,11... | collective-permute-start | bytes 1179656 | tf_op jit(solution)/shard_map/ppermute | solution.py:322
  38.4 1.3 %finish_blocks.1 = (bf16[8,2048,256]{2,1,0:T(8,128)(2,1)S(1)}, f32[4,512,256]{2,1,0:T(8,128)S(1)}, f32[512,256]{1,0:T(8,128)S(1)}) custom-call(bf16[512,2048]{1,0:T(8,128)(2,1)S(1)} %get-tuple-element.19.row, bf16[8,2048,256]{2,1,0:T(8,128)(2,1)S(1)} %get-tuple-element.20.columns_in, ...), custom_call_target="tpu_custom_call", output_to_operand_aliasing={{0}: (1, {}), {1}: (2, {})} | custom-call | flops 536870912 | tf_op jit(solution)/shard_map/finish_blocks/pallas_call | solution.py:292
  39.7 0.1 collective-permute-done.11.oth3
  39.8 2.2 %last_blocks.1 = (f32[512,256]{1,0:T(8,128)}, bf16[8,2048,256]{2,1,0:T(8,128)(2,1)S(1)}, f32[4,512,256]{2,1,0:T(8,128)S(1)}) custom-call(bf16[512,2048]{1,0:T(8,128)(2,1)S(1)} %get-tuple-element.19.row, bf16[8,2048,256]{2,1,0:T(8,128)(2,1)S(1)} %get-tuple-element.25.columns_in, ...), custom_call_target="tpu_custom_call", output_to_operand_aliasing={{1}: (1, {}), {2}: (3, {})} | custom-call | flops 1073741824 | tf_op jit(solution)/shard_map/last_blocks/pallas_call | solution.py:292
  (8 shorter events, 0.2 us)
Async XLA Ops:
  0.9 5.4 %collective-permute-start = (bf16[256,256]{1,0:T(8,128)(2,1)S(1)}, bf16[256,256]{1,0:T(8,128)(2,1)S(1)}, u32[]{:S(2)}, u32[]{:S(2)}) collective-permute-start(bf16[256,256]{1,0:T(8,128)(2,1)S(1)} %dynamic_slice.3.before), channel_id=1, source_target_pairs={{0,16},{8,24},{16,0},{24,8},{1,17},{9,25},{17,1},{25,9},{2,18},{10... | collective-permute-start | bytes 393224 | tf_op jit(solution)/shard_map/ppermute | solution.py:316
  1.0 1.2 %copy-start = (bf16[512,1024]{1,0:T(8,128)(2,1)S(1)}, bf16[512,1024]{1,0:T(8,128)(2,1)}, u32[]{:S(2)}) copy-start(bf16[512,1024]{1,0:T(8,128)(2,1)} %own.1) | copy-start | bytes 3145732
  2.3 4.0 %copy-start.1 = (bf16[512,1024]{1,0:T(8,128)(2,1)S(1)}, bf16[512,1024]{1,0:T(8,128)(2,1)}, u32[]{:S(2)}) copy-start(bf16[512,1024]{1,0:T(8,128)(2,1)} %own.1) | copy-start | bytes 3145732
  2.3 17.8 %collective-permute-start.3 = (bf16[256,1024]{1,0:T(8,128)(2,1)S(1)}, bf16[256,1024]{1,0:T(8,128)(2,1)S(1)}, u32[]{:S(2)}, u32[]{:S(2)}) collective-permute-start(bf16[256,1024]{1,0:T(8,128)(2,1)S(1)} %half_row.1.before), channel_id=1, source_target_pairs={{0,4},{4,0},{1,5},{5,1},{2,6},{6,2},{3,7},{7,3},{8,12},{12,8},{9,1... | collective-permute-start | bytes 1572872 | tf_op jit(solution)/shard_map/ppermute | solution.py:319
  3.6 12.1 %collective-permute-start.2 = (bf16[256,256]{1,0:T(8,128)(2,1)S(1)}, bf16[256,256]{1,0:T(8,128)(2,1)S(1)}, u32[]{:S(2)}, u32[]{:S(2)}) collective-permute-start(bf16[256,256]{1,0:T(8,128)(2,1)S(1)} %third.1), channel_id=1, source_target_pairs={{0,24},{8,16},{16,8},{24,0},{1,25},{9,17},{17,9},{25,1},{2,26},{10... | collective-permute-start | bytes 393224 | tf_op jit(solution)/shard_map/ppermute | solution.py:316
  6.3 11.2 %collective-permute-start.1 = (bf16[256,256]{1,0:T(8,128)(2,1)S(1)}, bf16[256,256]{1,0:T(8,128)(2,1)S(1)}, u32[]{:S(2)}, u32[]{:S(2)}) collective-permute-start(bf16[256,256]{1,0:T(8,128)(2,1)S(1)} %broadcast_select_fusion), channel_id=1, source_target_pairs={{0,8},{8,0},{16,24},{24,16},{1,9},{9,1},{17,25},{25,17},{2,10},{10... | collective-permute-start | bytes 393224 | tf_op jit(solution)/shard_map/ppermute | solution.py:316
  17.6 9.5 %collective-permute-start.6 = (bf16[3,256,256]{2,1,0:T(8,128)(2,1)S(1)}, bf16[3,256,256]{2,1,0:T(8,128)(2,1)S(1)}, u32[]{:S(2)}, u32[]{:S(2)}) collective-permute-start(bf16[3,256,256]{2,1,0:T(8,128)(2,1)S(1)} %stack.1.own0), channel_id=1, source_target_pairs={{0,2},{1,3},{2,0},{3,1},{4,6},{5,7},{6,4},{7,5},{8,10},{9,11},{10,... | collective-permute-start | bytes 1179656 | tf_op jit(solution)/shard_map/ppermute | solution.py:322
  18.9 10.4 %collective-permute-start.8 = (bf16[3,256,256]{2,1,0:T(8,128)(2,1)S(1)}, bf16[3,256,256]{2,1,0:T(8,128)(2,1)S(1)}, u32[]{:S(2)}, u32[]{:S(2)}) collective-permute-start(bf16[3,256,256]{2,1,0:T(8,128)(2,1)S(1)} %stack.1.own0), channel_id=1, source_target_pairs={{0,4},{4,0},{1,5},{5,1},{2,6},{6,2},{3,7},{7,3},{8,12},{12,8},{9,1... | collective-permute-start | bytes 1179656 | tf_op jit(solution)/shard_map/ppermute | solution.py:319
  20.1 11.7 %collective-permute-start.4 = (bf16[256,1024]{1,0:T(8,128)(2,1)S(1)}, bf16[256,1024]{1,0:T(8,128)(2,1)S(1)}, u32[]{:S(2)}, u32[]{:S(2)}) collective-permute-start(bf16[256,1024]{1,0:T(8,128)(2,1)S(1)} %collective-permute-done.3.near), channel_id=1, source_target_pairs={{0,1},{1,0},{2,3},{3,2},{4,5},{5,4},{6,7},{7,6},{8,9},{9,8},{10,11... | collective-permute-start | bytes 1572872 | tf_op jit(solution)/shard_map/ppermute | solution.py:322
  21.8 10.0 %collective-permute-start.5 = (bf16[3,256,256]{2,1,0:T(8,128)(2,1)S(1)}, bf16[3,256,256]{2,1,0:T(8,128)(2,1)S(1)}, u32[]{:S(2)}, u32[]{:S(2)}) collective-permute-start(bf16[3,256,256]{2,1,0:T(8,128)(2,1)S(1)} %stack.1.own0), channel_id=1, source_target_pairs={{0,1},{1,0},{2,3},{3,2},{4,5},{5,4},{6,7},{7,6},{8,9},{9,8},{10,11... | collective-permute-start | bytes 1179656 | tf_op jit(solution)/shard_map/ppermute | solution.py:322
  27.1 4.7 %collective-permute-start.7 = (bf16[3,256,256]{2,1,0:T(8,128)(2,1)S(1)}, bf16[3,256,256]{2,1,0:T(8,128)(2,1)S(1)}, u32[]{:S(2)}, u32[]{:S(2)}) collective-permute-start(bf16[3,256,256]{2,1,0:T(8,128)(2,1)S(1)} %own2.1), channel_id=1, source_target_pairs={{0,1},{1,0},{2,3},{3,2},{4,5},{5,4},{6,7},{7,6},{8,9},{9,8},{10,11... | collective-permute-start | bytes 1179656 | tf_op jit(solution)/shard_map/ppermute | solution.py:322
  29.3 2.6 %collective-permute-start.9 = (bf16[3,256,256]{2,1,0:T(8,128)(2,1)S(1)}, bf16[3,256,256]{2,1,0:T(8,128)(2,1)S(1)}, u32[]{:S(2)}, u32[]{:S(2)}) collective-permute-start(bf16[3,256,256]{2,1,0:T(8,128)(2,1)S(1)} %oth0.1), channel_id=1, source_target_pairs={{0,1},{1,0},{2,3},{3,2},{4,5},{5,4},{6,7},{7,6},{8,9},{9,8},{10,11... | collective-permute-start | bytes 1179656 | tf_op jit(solution)/shard_map/ppermute | solution.py:322
  30.5 7.0 %collective-permute-start.10 = (bf16[3,256,256]{2,1,0:T(8,128)(2,1)S(1)}, bf16[3,256,256]{2,1,0:T(8,128)(2,1)S(1)}, u32[]{:S(2)}, u32[]{:S(2)}) collective-permute-start(bf16[3,256,256]{2,1,0:T(8,128)(2,1)S(1)} %cross.1), channel_id=1, source_target_pairs={{0,2},{1,5},{2,0},{3,7},{4,6},{5,1},{6,4},{7,3},{8,10},{9,13},{10,... | collective-permute-start | bytes 1179656 | tf_op jit(solution)/shard_map/ppermute | solution.py:327
  37.5 2.2 %collective-permute-start.11 = (bf16[3,256,256]{2,1,0:T(8,128)(2,1)S(1)}, bf16[3,256,256]{2,1,0:T(8,128)(2,1)S(1)}, u32[]{:S(2)}, u32[]{:S(2)}) collective-permute-start(bf16[3,256,256]{2,1,0:T(8,128)(2,1)S(1)} %collective-permute-done.10.oth2), channel_id=1, source_target_pairs={{0,1},{1,0},{2,3},{3,2},{4,5},{5,4},{6,7},{7,6},{8,9},{9,8},{10,11... | collective-permute-start | bytes 1179656 | tf_op jit(solution)/shard_map/ppermute | solution.py:322

commit v7 on v6

--- a/solution.py
+++ b/solution.py
@@ -272,7 +272,9 @@
     for h in early_halves():
         term = dot(square[:, lanes(h, half)], columns[s, lanes(h, half)])
         acc = term if acc is None else acc + term
-    cube[...] = acc
+    c = place()[4]
+    h = late_halves()[0] + c
+    cube[...] = acc + dot(partial[c].astype(square.dtype), columns[s, lanes(h, half)])
 
 
 def last_kernel(row, columns_in, square, partial_in, cube, oth3, out, columns, partial):
@@ -281,7 +283,9 @@
     add_last(row, columns, partial, oth3, 1 - place()[4])
     s = wanted()
     acc, own = cube[...], square[:, lanes(s, half)].astype(jnp.float32)
-    for n, h in enumerate(late_halves()):
+    c, late = place()[4], late_halves()
+    own = jnp.where(late[0] + c == s, partial[c].astype(square.dtype).astype(jnp.float32), own)
+    for n, h in ((1 - c, late[0] + 1 - c), (2, late[2]), (3, late[3])):
         part = partial[n].astype(square.dtype)
         own = jnp.where(h == s, part.astype(jnp.float32), own)
         acc += dot(part, columns[s, lanes(h, half)])

time: 42.1 us -> 42.1 us (level)
  transfers between devices with their start and end apart: 12 -> 12, of which waited for: 6 -> 5; matrix products, arithmetic and copies ran while one was open for 0% -> 0% of each run, Pallas kernels for 18% -> 18%
where the time goes in v7:
time: 42.1 us; the launch traced here: 41.9 us
  starting transfers between devices  21.5 us (51%)
  Pallas kernels  9.73 us (23%)
  waiting for transfers between devices  8.42 us (20%)
  local copies, waits for them, and re-layouts  2.14 us (5%)
    ppermute x3, starting transfers between devices, by_z(): lax.ppermute(v, 'row', [(i, i ^ m) for i in range(lax.axis_size('row'))])  10.4 us
    pallas_call x10, Pallas kernels, call(): pl.pallas_call(kernel, out_shape=outs, in_specs=[pl.BlockSpec(memory_spac...  9.73 us
    ppermute x6, starting transfers between devices, by_depth(): lax.ppermute(v, 'depth', [(i, i ^ m) for i in range(lax.axis_size('depth'...  7.21 us
    ppermute x6, waiting for transfers between devices, by_depth(): lax.ppermute(v, 'depth', [(i, i ^ m) for i in range(lax.axis_size('depth'...  4.83 us
    ppermute x3, waiting for transfers between devices, by_z(): lax.ppermute(v, 'row', [(i, i ^ m) for i in range(lax.axis_size('row'))])  3.47 us
    ppermute x2, starting transfers between devices, by_x(): lax.ppermute(v, 'col', [(i, i ^ 1) for i in range(lax.axis_size('col'))])  2.53 us
    ppermute x1, starting transfers between devices, crossed(): return lax.ppermute(v, ('col', 'depth'), pairs)  1.28 us
    unnamed x4, local copies, waits for them, and re-layouts  1.23 us
  transfers between devices with their start and end apart: 12, of which 5 were waited for; matrix products, arithmetic and copies ran while one was open for 0% of the time, Pallas kernels for 18%

profile of v7, /device:TPU:17, one launch (start us, length us, event | category | flops | bytes accessed | tf_op | source)
XLA Modules:
  0.0 41.9 jit_solution(5678109665491428928)
XLA Ops:
  0.0 0.9 %dynamic_slice.3.before = bf16[256,256]{1,0:T(8,128)(2,1)S(1)} dynamic-slice(bf16[512,1024]{1,0:T(8,128)(2,1)} %own.1, s32[]{:T(128)S(6)} %select_n.14, s32[]{:T(128)S(6)} %select_n.15), dynamic_slice_sizes={256,256} | dynamic-slice | bytes 262148 | tf_op jit(solution)/shard_map/dynamic_slice | solution.py:334
  0.9 0.1 collective-permute-start
  1.0 0.0 copy-start
  1.0 1.2 %copy-done = bf16[512,1024]{1,0:T(8,128)(2,1)S(1)} copy-done((bf16[512,1024]{1,0:T(8,128)(2,1)S(1)}, bf16[512,1024]{1,0:T(8,128)(2,1)}, u32[]{:S(2)}) %copy-start) | copy-done | bytes 1048600
  2.3 0.0 copy-start.1
  2.3 1.3 %collective-permute-start.3 = (bf16[256,1024]{1,0:T(8,128)(2,1)S(1)}, bf16[256,1024]{1,0:T(8,128)(2,1)S(1)}, u32[]{:S(2)}, u32[]{:S(2)}) collective-permute-start(bf16[256,1024]{1,0:T(8,128)(2,1)S(1)} %half_row.1.before), channel_id=1, source_target_pairs={{0,4},{4,0},{1,5},{5,1},{2,6},{6,2},{3,7},{7,3},{8,12},{12,8},{9,1... | collective-permute-start | bytes 1572872 | tf_op jit(solution)/shard_map/ppermute | solution.py:323
  3.6 2.5 %collective-permute-start.2 = (bf16[256,256]{1,0:T(8,128)(2,1)S(1)}, bf16[256,256]{1,0:T(8,128)(2,1)S(1)}, u32[]{:S(2)}, u32[]{:S(2)}) collective-permute-start(bf16[256,256]{1,0:T(8,128)(2,1)S(1)} %third.1), channel_id=1, source_target_pairs={{0,24},{8,16},{16,8},{24,0},{1,25},{9,17},{17,9},{25,1},{2,26},{10... | collective-permute-start | bytes 393224 | tf_op jit(solution)/shard_map/ppermute | solution.py:320
  6.1 0.1 collective-permute-done.a
  6.3 7.9 %collective-permute-start.1 = (bf16[256,256]{1,0:T(8,128)(2,1)S(1)}, bf16[256,256]{1,0:T(8,128)(2,1)S(1)}, u32[]{:S(2)}, u32[]{:S(2)}) collective-permute-start(bf16[256,256]{1,0:T(8,128)(2,1)S(1)} %broadcast_select_fusion), channel_id=1, source_target_pairs={{0,8},{8,0},{16,24},{24,16},{1,9},{9,1},{17,25},{25,17},{2,10},{10... | collective-permute-start | bytes 393224 | tf_op jit(solution)/shard_map/ppermute | solution.py:320
  14.2 1.5 %collective-permute-done.2.c = bf16[256,256]{1,0:T(8,128)(2,1)S(1)} collective-permute-done((bf16[256,256]{1,0:T(8,128)(2,1)S(1)}, bf16[256,256]{1,0:T(8,128)(2,1)S(1)}, u32[]{:S(2)}, u32[]{:S(2)}) %collective-permute-start.2) | collective-permute-done | bytes 131104 | tf_op jit(solution)/shard_map/ppermute | solution.py:320
  15.7 1.8 %collective-permute-done.1.b = bf16[256,256]{1,0:T(8,128)(2,1)S(1)} collective-permute-done((bf16[256,256]{1,0:T(8,128)(2,1)S(1)}, bf16[256,256]{1,0:T(8,128)(2,1)S(1)}, u32[]{:S(2)}, u32[]{:S(2)}) %collective-permute-start.1) | collective-permute-done | bytes 131104 | tf_op jit(solution)/shard_map/ppermute | solution.py:320
  17.6 1.3 %collective-permute-start.6 = (bf16[3,256,256]{2,1,0:T(8,128)(2,1)S(1)}, bf16[3,256,256]{2,1,0:T(8,128)(2,1)S(1)}, u32[]{:S(2)}, u32[]{:S(2)}) collective-permute-start(bf16[3,256,256]{2,1,0:T(8,128)(2,1)S(1)} %stack.1.own0), channel_id=1, source_target_pairs={{0,2},{1,3},{2,0},{3,1},{4,6},{5,7},{6,4},{7,5},{8,10},{9,11},{10,... | collective-permute-start | bytes 1179656 | tf_op jit(solution)/shard_map/ppermute | solution.py:326
  18.9 1.2 %collective-permute-start.8 = (bf16[3,256,256]{2,1,0:T(8,128)(2,1)S(1)}, bf16[3,256,256]{2,1,0:T(8,128)(2,1)S(1)}, u32[]{:S(2)}, u32[]{:S(2)}) collective-permute-start(bf16[3,256,256]{2,1,0:T(8,128)(2,1)S(1)} %stack.1.own0), channel_id=1, source_target_pairs={{0,4},{4,0},{1,5},{5,1},{2,6},{6,2},{3,7},{7,3},{8,12},{12,8},{9,1... | collective-permute-start | bytes 1179656 | tf_op jit(solution)/shard_map/ppermute | solution.py:323
  20.1 0.0 collective-permute-done.3.near
  20.1 1.7 %collective-permute-start.4 = (bf16[256,1024]{1,0:T(8,128)(2,1)S(1)}, bf16[256,1024]{1,0:T(8,128)(2,1)S(1)}, u32[]{:S(2)}, u32[]{:S(2)}) collective-permute-start(bf16[256,1024]{1,0:T(8,128)(2,1)S(1)} %collective-permute-done.3.near), channel_id=1, source_target_pairs={{0,1},{1,0},{2,3},{3,2},{4,5},{5,4},{6,7},{7,6},{8,9},{9,8},{10,11... | collective-permute-start | bytes 1572872 | tf_op jit(solution)/shard_map/ppermute | solution.py:326
  21.8 0.0 collective-permute-start.5
  21.8 0.5 %first_blocks.1 = (bf16[512,2048]{1,0:T(8,128)(2,1)S(1)}, bf16[8,2048,256]{2,1,0:T(8,128)(2,1)S(1)}) custom-call(bf16[512,1024]{1,0:T(8,128)(2,1)S(1)} %copy-done.1, bf16[3,256,256]{2,1,0:T(8,128)(2,1)S(1)} %stack.1.own0), custom_call_target="tpu_custom_call" | custom-call | flops 268435456 | tf_op jit(solution)/shard_map/first_blocks/pallas_call | solution.py:296
  22.3 4.8 %collective-permute-done.6.a.own2.b = bf16[3,256,256]{2,1,0:T(8,128)(2,1)S(1)} collective-permute-done((bf16[3,256,256]{2,1,0:T(8,128)(2,1)S(1)}, bf16[3,256,256]{2,1,0:T(8,128)(2,1)S(1)}, u32[]{:S(2)}, u32[]{:S(2)}) %collective-permute-start.6) | collective-permute-done | bytes 393248 | tf_op jit(solution)/shard_map/ppermute | solution.py:326
  27.1 2.1 %collective-permute-start.7 = (bf16[3,256,256]{2,1,0:T(8,128)(2,1)S(1)}, bf16[3,256,256]{2,1,0:T(8,128)(2,1)S(1)}, u32[]{:S(2)}, u32[]{:S(2)}) collective-permute-start(bf16[3,256,256]{2,1,0:T(8,128)(2,1)S(1)} %own2.1), channel_id=1, source_target_pairs={{0,1},{1,0},{2,3},{3,2},{4,5},{5,4},{6,7},{7,6},{8,9},{9,8},{10,11... | collective-permute-start | bytes 1179656 | tf_op jit(solution)/shard_map/ppermute | solution.py:326
  29.3 0.0 collective-permute-done.8.a.oth0
  29.3 1.2 %collective-permute-start.9 = (bf16[3,256,256]{2,1,0:T(8,128)(2,1)S(1)}, bf16[3,256,256]{2,1,0:T(8,128)(2,1)S(1)}, u32[]{:S(2)}, u32[]{:S(2)}) collective-permute-start(bf16[3,256,256]{2,1,0:T(8,128)(2,1)S(1)} %oth0.1), channel_id=1, source_target_pairs={{0,1},{1,0},{2,3},{3,2},{4,5},{5,4},{6,7},{7,6},{8,9},{9,8},{10,11... | collective-permute-start | bytes 1179656 | tf_op jit(solution)/shard_map/ppermute | solution.py:326
  30.5 1.3 %collective-permute-start.10 = (bf16[3,256,256]{2,1,0:T(8,128)(2,1)S(1)}, bf16[3,256,256]{2,1,0:T(8,128)(2,1)S(1)}, u32[]{:S(2)}, u32[]{:S(2)}) collective-permute-start(bf16[3,256,256]{2,1,0:T(8,128)(2,1)S(1)} %cross.1), channel_id=1, source_target_pairs={{0,2},{1,5},{2,0},{3,7},{4,6},{5,1},{6,4},{7,3},{8,10},{9,13},{10,... | collective-permute-start | bytes 1179656 | tf_op jit(solution)/shard_map/ppermute | solution.py:331
  31.8 0.0 collective-permute-done.5.own1
  31.8 0.0 collective-permute-done.4.far
  31.8 0.0 collective-permute-done.7.own3
  31.8 0.0 collective-permute-done.9.oth1
  31.9 5.5 %middle_blocks.1 = (bf16[512,2048]{1,0:T(8,128)(2,1)S(1)}, bf16[8,2048,256]{2,1,0:T(8,128)(2,1)S(1)}, bf16[512,2048]{1,0:T(8,128)(2,1)S(1)}, f32[4,512,256]{2,1,0:T(8,128)S(1)}) custom-call(bf16[512,2048]{1,0:T(8,128)(2,1)S(1)} %get-tuple-element.17.before.row_in, ...), custom_call_target="tpu_custom_call", output_to_operand_aliasing={{0}: (0, {}), {1}: (1, {})} | custom-call | flops 4026531840 | tf_op jit(solution)/shard_map/middle_blocks/pallas_call | solution.py:296
  37.4 0.1 collective-permute-done.10.oth2
  37.5 0.9 %collective-permute-start.11 = (bf16[3,256,256]{2,1,0:T(8,128)(2,1)S(1)}, bf16[3,256,256]{2,1,0:T(8,128)(2,1)S(1)}, u32[]{:S(2)}, u32[]{:S(2)}) collective-permute-start(bf16[3,256,256]{2,1,0:T(8,128)(2,1)S(1)} %collective-permute-done.10.oth2), channel_id=1, source_target_pairs={{0,1},{1,0},{2,3},{3,2},{4,5},{5,4},{6,7},{7,6},{8,9},{9,8},{10,11... | collective-permute-start | bytes 1179656 | tf_op jit(solution)/shard_map/ppermute | solution.py:326
  38.4 1.3 %finish_blocks.1 = (bf16[8,2048,256]{2,1,0:T(8,128)(2,1)S(1)}, f32[4,512,256]{2,1,0:T(8,128)S(1)}, f32[512,256]{1,0:T(8,128)S(1)}) custom-call(bf16[512,2048]{1,0:T(8,128)(2,1)S(1)} %get-tuple-element.19.row, bf16[8,2048,256]{2,1,0:T(8,128)(2,1)S(1)} %get-tuple-element.20.columns_in, ...), custom_call_target="tpu_custom_call", output_to_operand_aliasing={{0}: (1, {}), {1}: (2, {})} | custom-call | flops 536870912 | tf_op jit(solution)/shard_map/finish_blocks/pallas_call | solution.py:296
  39.8 0.0 collective-permute-done.11.oth3
  39.8 2.1 %last_blocks.1 = (f32[512,256]{1,0:T(8,128)}, bf16[8,2048,256]{2,1,0:T(8,128)(2,1)S(1)}, f32[4,512,256]{2,1,0:T(8,128)S(1)}) custom-call(bf16[512,2048]{1,0:T(8,128)(2,1)S(1)} %get-tuple-element.19.row, bf16[8,2048,256]{2,1,0:T(8,128)(2,1)S(1)} %get-tuple-element.25.columns_in, ...), custom_call_target="tpu_custom_call", output_to_operand_aliasing={{1}: (1, {}), {2}: (3, {})} | custom-call | flops 1073741824 | tf_op jit(solution)/shard_map/last_blocks/pallas_call | solution.py:296
  (8 shorter events, 0.2 us)
Async XLA Ops:
  0.9 5.4 %collective-permute-start = (bf16[256,256]{1,0:T(8,128)(2,1)S(1)}, bf16[256,256]{1,0:T(8,128)(2,1)S(1)}, u32[]{:S(2)}, u32[]{:S(2)}) collective-permute-start(bf16[256,256]{1,0:T(8,128)(2,1)S(1)} %dynamic_slice.3.before), channel_id=1, source_target_pairs={{0,16},{8,24},{16,0},{24,8},{1,17},{9,25},{17,1},{25,9},{2,18},{10... | collective-permute-start | bytes 393224 | tf_op jit(solution)/shard_map/ppermute | solution.py:320
  1.0 1.2 %copy-start = (bf16[512,1024]{1,0:T(8,128)(2,1)S(1)}, bf16[512,1024]{1,0:T(8,128)(2,1)}, u32[]{:S(2)}) copy-start(bf16[512,1024]{1,0:T(8,128)(2,1)} %own.1) | copy-start | bytes 3145732
  2.3 4.0 %copy-start.1 = (bf16[512,1024]{1,0:T(8,128)(2,1)S(1)}, bf16[512,1024]{1,0:T(8,128)(2,1)}, u32[]{:S(2)}) copy-start(bf16[512,1024]{1,0:T(8,128)(2,1)} %own.1) | copy-start | bytes 3145732
  2.3 17.8 %collective-permute-start.3 = (bf16[256,1024]{1,0:T(8,128)(2,1)S(1)}, bf16[256,1024]{1,0:T(8,128)(2,1)S(1)}, u32[]{:S(2)}, u32[]{:S(2)}) collective-permute-start(bf16[256,1024]{1,0:T(8,128)(2,1)S(1)} %half_row.1.before), channel_id=1, source_target_pairs={{0,4},{4,0},{1,5},{5,1},{2,6},{6,2},{3,7},{7,3},{8,12},{12,8},{9,1... | collective-permute-start | bytes 1572872 | tf_op jit(solution)/shard_map/ppermute | solution.py:323
  3.6 12.1 %collective-permute-start.2 = (bf16[256,256]{1,0:T(8,128)(2,1)S(1)}, bf16[256,256]{1,0:T(8,128)(2,1)S(1)}, u32[]{:S(2)}, u32[]{:S(2)}) collective-permute-start(bf16[256,256]{1,0:T(8,128)(2,1)S(1)} %third.1), channel_id=1, source_target_pairs={{0,24},{8,16},{16,8},{24,0},{1,25},{9,17},{17,9},{25,1},{2,26},{10... | collective-permute-start | bytes 393224 | tf_op jit(solution)/shard_map/ppermute | solution.py:320
  6.3 11.2 %collective-permute-start.1 = (bf16[256,256]{1,0:T(8,128)(2,1)S(1)}, bf16[256,256]{1,0:T(8,128)(2,1)S(1)}, u32[]{:S(2)}, u32[]{:S(2)}) collective-permute-start(bf16[256,256]{1,0:T(8,128)(2,1)S(1)} %broadcast_select_fusion), channel_id=1, source_target_pairs={{0,8},{8,0},{16,24},{24,16},{1,9},{9,1},{17,25},{25,17},{2,10},{10... | collective-permute-start | bytes 393224 | tf_op jit(solution)/shard_map/ppermute | solution.py:320
  17.6 9.5 %collective-permute-start.6 = (bf16[3,256,256]{2,1,0:T(8,128)(2,1)S(1)}, bf16[3,256,256]{2,1,0:T(8,128)(2,1)S(1)}, u32[]{:S(2)}, u32[]{:S(2)}) collective-permute-start(bf16[3,256,256]{2,1,0:T(8,128)(2,1)S(1)} %stack.1.own0), channel_id=1, source_target_pairs={{0,2},{1,3},{2,0},{3,1},{4,6},{5,7},{6,4},{7,5},{8,10},{9,11},{10,... | collective-permute-start | bytes 1179656 | tf_op jit(solution)/shard_map/ppermute | solution.py:326
  18.9 10.4 %collective-permute-start.8 = (bf16[3,256,256]{2,1,0:T(8,128)(2,1)S(1)}, bf16[3,256,256]{2,1,0:T(8,128)(2,1)S(1)}, u32[]{:S(2)}, u32[]{:S(2)}) collective-permute-start(bf16[3,256,256]{2,1,0:T(8,128)(2,1)S(1)} %stack.1.own0), channel_id=1, source_target_pairs={{0,4},{4,0},{1,5},{5,1},{2,6},{6,2},{3,7},{7,3},{8,12},{12,8},{9,1... | collective-permute-start | bytes 1179656 | tf_op jit(solution)/shard_map/ppermute | solution.py:323
  20.1 11.7 %collective-permute-start.4 = (bf16[256,1024]{1,0:T(8,128)(2,1)S(1)}, bf16[256,1024]{1,0:T(8,128)(2,1)S(1)}, u32[]{:S(2)}, u32[]{:S(2)}) collective-permute-start(bf16[256,1024]{1,0:T(8,128)(2,1)S(1)} %collective-permute-done.3.near), channel_id=1, source_target_pairs={{0,1},{1,0},{2,3},{3,2},{4,5},{5,4},{6,7},{7,6},{8,9},{9,8},{10,11... | collective-permute-start | bytes 1572872 | tf_op jit(solution)/shard_map/ppermute | solution.py:326
  21.8 10.0 %collective-permute-start.5 = (bf16[3,256,256]{2,1,0:T(8,128)(2,1)S(1)}, bf16[3,256,256]{2,1,0:T(8,128)(2,1)S(1)}, u32[]{:S(2)}, u32[]{:S(2)}) collective-permute-start(bf16[3,256,256]{2,1,0:T(8,128)(2,1)S(1)} %stack.1.own0), channel_id=1, source_target_pairs={{0,1},{1,0},{2,3},{3,2},{4,5},{5,4},{6,7},{7,6},{8,9},{9,8},{10,11... | collective-permute-start | bytes 1179656 | tf_op jit(solution)/shard_map/ppermute | solution.py:326
  27.1 4.7 %collective-permute-start.7 = (bf16[3,256,256]{2,1,0:T(8,128)(2,1)S(1)}, bf16[3,256,256]{2,1,0:T(8,128)(2,1)S(1)}, u32[]{:S(2)}, u32[]{:S(2)}) collective-permute-start(bf16[3,256,256]{2,1,0:T(8,128)(2,1)S(1)} %own2.1), channel_id=1, source_target_pairs={{0,1},{1,0},{2,3},{3,2},{4,5},{5,4},{6,7},{7,6},{8,9},{9,8},{10,11... | collective-permute-start | bytes 1179656 | tf_op jit(solution)/shard_map/ppermute | solution.py:326
  29.3 2.6 %collective-permute-start.9 = (bf16[3,256,256]{2,1,0:T(8,128)(2,1)S(1)}, bf16[3,256,256]{2,1,0:T(8,128)(2,1)S(1)}, u32[]{:S(2)}, u32[]{:S(2)}) collective-permute-start(bf16[3,256,256]{2,1,0:T(8,128)(2,1)S(1)} %oth0.1), channel_id=1, source_target_pairs={{0,1},{1,0},{2,3},{3,2},{4,5},{5,4},{6,7},{7,6},{8,9},{9,8},{10,11... | collective-permute-start | bytes 1179656 | tf_op jit(solution)/shard_map/ppermute | solution.py:326
  30.5 7.0 %collective-permute-start.10 = (bf16[3,256,256]{2,1,0:T(8,128)(2,1)S(1)}, bf16[3,256,256]{2,1,0:T(8,128)(2,1)S(1)}, u32[]{:S(2)}, u32[]{:S(2)}) collective-permute-start(bf16[3,256,256]{2,1,0:T(8,128)(2,1)S(1)} %cross.1), channel_id=1, source_target_pairs={{0,2},{1,5},{2,0},{3,7},{4,6},{5,1},{6,4},{7,3},{8,10},{9,13},{10,... | collective-permute-start | bytes 1179656 | tf_op jit(solution)/shard_map/ppermute | solution.py:331
  37.5 2.2 %collective-permute-start.11 = (bf16[3,256,256]{2,1,0:T(8,128)(2,1)S(1)}, bf16[3,256,256]{2,1,0:T(8,128)(2,1)S(1)}, u32[]{:S(2)}, u32[]{:S(2)}) collective-permute-start(bf16[3,256,256]{2,1,0:T(8,128)(2,1)S(1)} %collective-permute-done.10.oth2), channel_id=1, source_target_pairs={{0,1},{1,0},{2,3},{3,2},{4,5},{5,4},{6,7},{7,6},{8,9},{9,8},{10,11... | collective-permute-start | bytes 1179656 | tf_op jit(solution)/shard_map/ppermute | solution.py:326

commit v8 on v6

--- a/solution.py
+++ b/solution.py
@@ -161,7 +161,7 @@
     fetch(density.at[lanes(y, half), lanes(2 * (1 - picked(z, x)) + c, half)], out, sem)
 
 
-def first_kernel(own, own0, row, columns):
+def first_kernel(own, own0, near, row, columns):
     z, x, _, y, c = place()
     blk, half = own.shape[0], columns.shape[2]
     for b in range(2):
@@ -172,6 +172,8 @@
             columns[2 * m + h, :blk] = part
             for g in range(2):
                 columns[g, lanes(2 * m + h, half)] = turned(part[g * half : (g + 1) * half])
+    for b in range(2):
+        put_row(row, columns, (2 * (1 - x) + b) ^ z, c, near[:, b * blk : (b + 1) * blk])
     for slot in range(3):
         i, k = received(slot, 0)
         put(columns, 2 * i + y, 2 * k + c, own0[slot])
@@ -195,13 +197,12 @@
         out[...] = b[...]
 
 
-def middle_kernel(row_in, columns_in, near, far, own1, own2, own3, oth0, oth1, row, columns, square, partial):
+def middle_kernel(row_in, columns_in, far, own1, own2, own3, oth0, oth1, row, columns, square, partial):
     del row_in, columns_in
     z, x, _, y, c = place()
-    blk, half = near.shape[1] // 2, columns.shape[2]
+    blk, half = far.shape[1] // 2, columns.shape[2]
     for b in range(2):
         m = (2 * (1 - x) + b) ^ z
-        put_row(row, columns, m, c, near[:, b * blk : (b + 1) * blk])
         put_row(row, columns, m, 1 - c, far[:, b * blk : (b + 1) * blk])
     for slot in range(3):
         i, k = received(slot, 0)
@@ -369,7 +370,7 @@
     oth0, own2 = by_x(own0), by_depth(own0, 2)
     own1 = by_depth(own0, 1)
     row, columns = call(
-        first_kernel, "first_blocks", 2 * cube, (density, own0), (row_shape, columns_shape)
+        first_kernel, "first_blocks", 2 * cube, (density, own0, near), (row_shape, columns_shape)
     )
     quarters = shape(3, half, half)
     oth1 = by_depth(call(pass_kernel, "oth0", 0, (oth0, row), (quarters,), order_only=1)[0], 1)
@@ -382,7 +383,7 @@
         middle_kernel,
         "middle_blocks",
         30 * cube,
-        (row, columns, near, far, own1, own2, own3, oth0, oth1),
+        (row, columns, far, own1, own2, own3, oth0, oth1),
         (row_shape, columns_shape, row_shape, shape(4, blk, half, dtype=jnp.float32)),
         {0: 0, 1: 1},
     )

time: 42.1 us -> 42.1 us (level)
  no operation moved by 1% of the time
where the time goes in v8:
time: 42.1 us; the launch traced here: 42 us
  starting transfers between devices  21.5 us (51%)
  Pallas kernels  9.72 us (23%)
  waiting for transfers between devices  8.5 us (20%)
  local copies, waits for them, and re-layouts  2.14 us (5%)
    ppermute x3, starting transfers between devices, by_z(): lax.ppermute(v, 'row', [(i, i ^ m) for i in range(lax.axis_size('row'))])  10.4 us
    pallas_call x10, Pallas kernels, call(): pl.pallas_call(kernel, out_shape=outs, in_specs=[pl.BlockSpec(memory_spac...  9.72 us
    ppermute x6, starting transfers between devices, by_depth(): lax.ppermute(v, 'depth', [(i, i ^ m) for i in range(lax.axis_size('depth'...  7.21 us
    ppermute x6, waiting for transfers between devices, by_depth(): lax.ppermute(v, 'depth', [(i, i ^ m) for i in range(lax.axis_size('depth'...  4.74 us
    ppermute x3, waiting for transfers between devices, by_z(): lax.ppermute(v, 'row', [(i, i ^ m) for i in range(lax.axis_size('row'))])  3.47 us
    ppermute x2, starting transfers between devices, by_x(): lax.ppermute(v, 'col', [(i, i ^ 1) for i in range(lax.axis_size('col'))])  2.53 us
    ppermute x1, starting transfers between devices, crossed(): return lax.ppermute(v, ('col', 'depth'), pairs)  1.28 us
    unnamed x4, local copies, waits for them, and re-layouts  1.23 us
  transfers between devices with their start and end apart: 12, of which 6 were waited for; matrix products, arithmetic and copies ran while one was open for 0% of the time, Pallas kernels for 18%

profile of v8, /device:TPU:17, one launch (start us, length us, event | category | flops | bytes accessed | tf_op | source)
XLA Modules:
  0.0 42.0 jit_solution(7507665621183665836)
XLA Ops:
  0.0 0.9 %dynamic_slice.3.before = bf16[256,256]{1,0:T(8,128)(2,1)S(1)} dynamic-slice(bf16[512,1024]{1,0:T(8,128)(2,1)} %own.1, s32[]{:T(128)S(6)} %select_n.14, s32[]{:T(128)S(6)} %select_n.15), dynamic_slice_sizes={256,256} | dynamic-slice | bytes 262148 | tf_op jit(solution)/shard_map/dynamic_slice | solution.py:331
  0.9 0.1 collective-permute-start
  1.0 0.0 copy-start
  1.0 1.2 %copy-done = bf16[512,1024]{1,0:T(8,128)(2,1)S(1)} copy-done((bf16[512,1024]{1,0:T(8,128)(2,1)S(1)}, bf16[512,1024]{1,0:T(8,128)(2,1)}, u32[]{:S(2)}) %copy-start) | copy-done | bytes 1048600
  2.3 0.0 copy-start.1
  2.3 1.3 %collective-permute-start.3 = (bf16[256,1024]{1,0:T(8,128)(2,1)S(1)}, bf16[256,1024]{1,0:T(8,128)(2,1)S(1)}, u32[]{:S(2)}, u32[]{:S(2)}) collective-permute-start(bf16[256,1024]{1,0:T(8,128)(2,1)S(1)} %half_row.1.before), channel_id=1, source_target_pairs={{0,4},{4,0},{1,5},{5,1},{2,6},{6,2},{3,7},{7,3},{8,12},{12,8},{9,1... | collective-permute-start | bytes 1572872 | tf_op jit(solution)/shard_map/ppermute | solution.py:320
  3.6 2.5 %collective-permute-start.2 = (bf16[256,256]{1,0:T(8,128)(2,1)S(1)}, bf16[256,256]{1,0:T(8,128)(2,1)S(1)}, u32[]{:S(2)}, u32[]{:S(2)}) collective-permute-start(bf16[256,256]{1,0:T(8,128)(2,1)S(1)} %third.1), channel_id=1, source_target_pairs={{0,24},{8,16},{16,8},{24,0},{1,25},{9,17},{17,9},{25,1},{2,26},{10... | collective-permute-start | bytes 393224 | tf_op jit(solution)/shard_map/ppermute | solution.py:317
  6.1 0.1 collective-permute-done.a
  6.3 7.9 %collective-permute-start.1 = (bf16[256,256]{1,0:T(8,128)(2,1)S(1)}, bf16[256,256]{1,0:T(8,128)(2,1)S(1)}, u32[]{:S(2)}, u32[]{:S(2)}) collective-permute-start(bf16[256,256]{1,0:T(8,128)(2,1)S(1)} %broadcast_select_fusion), channel_id=1, source_target_pairs={{0,8},{8,0},{16,24},{24,16},{1,9},{9,1},{17,25},{25,17},{2,10},{10... | collective-permute-start | bytes 393224 | tf_op jit(solution)/shard_map/ppermute | solution.py:317
  14.2 1.5 %collective-permute-done.2.c = bf16[256,256]{1,0:T(8,128)(2,1)S(1)} collective-permute-done((bf16[256,256]{1,0:T(8,128)(2,1)S(1)}, bf16[256,256]{1,0:T(8,128)(2,1)S(1)}, u32[]{:S(2)}, u32[]{:S(2)}) %collective-permute-start.2) | collective-permute-done | bytes 131104 | tf_op jit(solution)/shard_map/ppermute | solution.py:317
  15.7 1.8 %collective-permute-done.1.b = bf16[256,256]{1,0:T(8,128)(2,1)S(1)} collective-permute-done((bf16[256,256]{1,0:T(8,128)(2,1)S(1)}, bf16[256,256]{1,0:T(8,128)(2,1)S(1)}, u32[]{:S(2)}, u32[]{:S(2)}) %collective-permute-start.1) | collective-permute-done | bytes 131104 | tf_op jit(solution)/shard_map/ppermute | solution.py:317
  17.6 1.3 %collective-permute-start.6 = (bf16[3,256,256]{2,1,0:T(8,128)(2,1)S(1)}, bf16[3,256,256]{2,1,0:T(8,128)(2,1)S(1)}, u32[]{:S(2)}, u32[]{:S(2)}) collective-permute-start(bf16[3,256,256]{2,1,0:T(8,128)(2,1)S(1)} %stack.1.own0), channel_id=1, source_target_pairs={{0,2},{1,3},{2,0},{3,1},{4,6},{5,7},{6,4},{7,5},{8,10},{9,11},{10,... | collective-permute-start | bytes 1179656 | tf_op jit(solution)/shard_map/ppermute | solution.py:323
  18.9 1.2 %collective-permute-start.8 = (bf16[3,256,256]{2,1,0:T(8,128)(2,1)S(1)}, bf16[3,256,256]{2,1,0:T(8,128)(2,1)S(1)}, u32[]{:S(2)}, u32[]{:S(2)}) collective-permute-start(bf16[3,256,256]{2,1,0:T(8,128)(2,1)S(1)} %stack.1.own0), channel_id=1, source_target_pairs={{0,4},{4,0},{1,5},{5,1},{2,6},{6,2},{3,7},{7,3},{8,12},{12,8},{9,1... | collective-permute-start | bytes 1179656 | tf_op jit(solution)/shard_map/ppermute | solution.py:320
  20.1 0.0 collective-permute-done.3.near
  20.1 1.7 %collective-permute-start.4 = (bf16[256,1024]{1,0:T(8,128)(2,1)S(1)}, bf16[256,1024]{1,0:T(8,128)(2,1)S(1)}, u32[]{:S(2)}, u32[]{:S(2)}) collective-permute-start(bf16[256,1024]{1,0:T(8,128)(2,1)S(1)} %collective-permute-done.3.near), channel_id=1, source_target_pairs={{0,1},{1,0},{2,3},{3,2},{4,5},{5,4},{6,7},{7,6},{8,9},{9,8},{10,11... | collective-permute-start | bytes 1572872 | tf_op jit(solution)/shard_map/ppermute | solution.py:323
  21.8 0.0 collective-permute-start.5
  21.8 0.7 %first_blocks.1 = (bf16[512,2048]{1,0:T(8,128)(2,1)S(1)}, bf16[8,2048,256]{2,1,0:T(8,128)(2,1)S(1)}) custom-call(bf16[512,1024]{1,0:T(8,128)(2,1)S(1)} %copy-done.1, bf16[3,256,256]{2,1,0:T(8,128)(2,1)S(1)} %stack.1.own0, bf16[256,1024]{1,0:T(8,128)(2,1)S(1)} %collective-permute-done.3.near), custom_call_target="tpu_custom_call" | custom-call | flops 268435456 | tf_op jit(solution)/shard_map/first_blocks/pallas_call | solution.py:293
  22.5 4.6 %collective-permute-done.6.a.own2.b = bf16[3,256,256]{2,1,0:T(8,128)(2,1)S(1)} collective-permute-done((bf16[3,256,256]{2,1,0:T(8,128)(2,1)S(1)}, bf16[3,256,256]{2,1,0:T(8,128)(2,1)S(1)}, u32[]{:S(2)}, u32[]{:S(2)}) %collective-permute-start.6) | collective-permute-done | bytes 393248 | tf_op jit(solution)/shard_map/ppermute | solution.py:323
  27.1 2.1 %collective-permute-start.7 = (bf16[3,256,256]{2,1,0:T(8,128)(2,1)S(1)}, bf16[3,256,256]{2,1,0:T(8,128)(2,1)S(1)}, u32[]{:S(2)}, u32[]{:S(2)}) collective-permute-start(bf16[3,256,256]{2,1,0:T(8,128)(2,1)S(1)} %own2.1), channel_id=1, source_target_pairs={{0,1},{1,0},{2,3},{3,2},{4,5},{5,4},{6,7},{7,6},{8,9},{9,8},{10,11... | collective-permute-start | bytes 1179656 | tf_op jit(solution)/shard_map/ppermute | solution.py:323
  29.3 0.0 collective-permute-done.8.a.oth0
  29.3 1.2 %collective-permute-start.9 = (bf16[3,256,256]{2,1,0:T(8,128)(2,1)S(1)}, bf16[3,256,256]{2,1,0:T(8,128)(2,1)S(1)}, u32[]{:S(2)}, u32[]{:S(2)}) collective-permute-start(bf16[3,256,256]{2,1,0:T(8,128)(2,1)S(1)} %oth0.1), channel_id=1, source_target_pairs={{0,1},{1,0},{2,3},{3,2},{4,5},{5,4},{6,7},{7,6},{8,9},{9,8},{10,11... | collective-permute-start | bytes 1179656 | tf_op jit(solution)/shard_map/ppermute | solution.py:323
  30.5 1.3 %collective-permute-start.10 = (bf16[3,256,256]{2,1,0:T(8,128)(2,1)S(1)}, bf16[3,256,256]{2,1,0:T(8,128)(2,1)S(1)}, u32[]{:S(2)}, u32[]{:S(2)}) collective-permute-start(bf16[3,256,256]{2,1,0:T(8,128)(2,1)S(1)} %cross.1), channel_id=1, source_target_pairs={{0,2},{1,5},{2,0},{3,7},{4,6},{5,1},{6,4},{7,3},{8,10},{9,13},{10,... | collective-permute-start | bytes 1179656 | tf_op jit(solution)/shard_map/ppermute | solution.py:328
  31.8 0.0 collective-permute-done.5.own1
  31.8 0.0 collective-permute-done.4.far
  31.8 0.0 collective-permute-done.7.own3
  31.8 0.0 collective-permute-done.9.oth1
  31.9 5.4 %middle_blocks.1 = (bf16[512,2048]{1,0:T(8,128)(2,1)S(1)}, bf16[8,2048,256]{2,1,0:T(8,128)(2,1)S(1)}, bf16[512,2048]{1,0:T(8,128)(2,1)S(1)}, f32[4,512,256]{2,1,0:T(8,128)S(1)}) custom-call(bf16[512,2048]{1,0:T(8,128)(2,1)S(1)} %get-tuple-element.17.before.row_in, ...), custom_call_target="tpu_custom_call", output_to_operand_aliasing={{0}: (0, {}), {1}: (1, {})} | custom-call | flops 4026531840 | tf_op jit(solution)/shard_map/middle_blocks/pallas_call | solution.py:293
  37.2 0.3 collective-permute-done.10.oth2
  37.5 0.9 %collective-permute-start.11 = (bf16[3,256,256]{2,1,0:T(8,128)(2,1)S(1)}, bf16[3,256,256]{2,1,0:T(8,128)(2,1)S(1)}, u32[]{:S(2)}, u32[]{:S(2)}) collective-permute-start(bf16[3,256,256]{2,1,0:T(8,128)(2,1)S(1)} %collective-permute-done.10.oth2), channel_id=1, source_target_pairs={{0,1},{1,0},{2,3},{3,2},{4,5},{5,4},{6,7},{7,6},{8,9},{9,8},{10,11... | collective-permute-start | bytes 1179656 | tf_op jit(solution)/shard_map/ppermute | solution.py:323
  38.4 1.3 %finish_blocks.1 = (bf16[8,2048,256]{2,1,0:T(8,128)(2,1)S(1)}, f32[4,512,256]{2,1,0:T(8,128)S(1)}, f32[512,256]{1,0:T(8,128)S(1)}) custom-call(bf16[512,2048]{1,0:T(8,128)(2,1)S(1)} %get-tuple-element.19.row, bf16[8,2048,256]{2,1,0:T(8,128)(2,1)S(1)} %get-tuple-element.20.columns_in, ...), custom_call_target="tpu_custom_call", output_to_operand_aliasing={{0}: (1, {}), {1}: (2, {})} | custom-call | flops 536870912 | tf_op jit(solution)/shard_map/finish_blocks/pallas_call | solution.py:293
  39.7 0.1 collective-permute-done.11.oth3
  39.8 2.2 %last_blocks.1 = (f32[512,256]{1,0:T(8,128)}, bf16[8,2048,256]{2,1,0:T(8,128)(2,1)S(1)}, f32[4,512,256]{2,1,0:T(8,128)S(1)}) custom-call(bf16[512,2048]{1,0:T(8,128)(2,1)S(1)} %get-tuple-element.19.row, bf16[8,2048,256]{2,1,0:T(8,128)(2,1)S(1)} %get-tuple-element.25.columns_in, ...), custom_call_target="tpu_custom_call", output_to_operand_aliasing={{1}: (1, {}), {2}: (3, {})} | custom-call | flops 1073741824 | tf_op jit(solution)/shard_map/last_blocks/pallas_call | solution.py:293
  (8 shorter events, 0.2 us)
Async XLA Ops:
  0.9 5.4 %collective-permute-start = (bf16[256,256]{1,0:T(8,128)(2,1)S(1)}, bf16[256,256]{1,0:T(8,128)(2,1)S(1)}, u32[]{:S(2)}, u32[]{:S(2)}) collective-permute-start(bf16[256,256]{1,0:T(8,128)(2,1)S(1)} %dynamic_slice.3.before), channel_id=1, source_target_pairs={{0,16},{8,24},{16,0},{24,8},{1,17},{9,25},{17,1},{25,9},{2,18},{10... | collective-permute-start | bytes 393224 | tf_op jit(solution)/shard_map/ppermute | solution.py:317
  1.0 1.2 %copy-start = (bf16[512,1024]{1,0:T(8,128)(2,1)S(1)}, bf16[512,1024]{1,0:T(8,128)(2,1)}, u32[]{:S(2)}) copy-start(bf16[512,1024]{1,0:T(8,128)(2,1)} %own.1) | copy-start | bytes 3145732
  2.3 4.0 %copy-start.1 = (bf16[512,1024]{1,0:T(8,128)(2,1)S(1)}, bf16[512,1024]{1,0:T(8,128)(2,1)}, u32[]{:S(2)}) copy-start(bf16[512,1024]{1,0:T(8,128)(2,1)} %own.1) | copy-start | bytes 3145732
  2.3 17.8 %collective-permute-start.3 = (bf16[256,1024]{1,0:T(8,128)(2,1)S(1)}, bf16[256,1024]{1,0:T(8,128)(2,1)S(1)}, u32[]{:S(2)}, u32[]{:S(2)}) collective-permute-start(bf16[256,1024]{1,0:T(8,128)(2,1)S(1)} %half_row.1.before), channel_id=1, source_target_pairs={{0,4},{4,0},{1,5},{5,1},{2,6},{6,2},{3,7},{7,3},{8,12},{12,8},{9,1... | collective-permute-start | bytes 1572872 | tf_op jit(solution)/shard_map/ppermute | solution.py:320
  3.6 12.1 %collective-permute-start.2 = (bf16[256,256]{1,0:T(8,128)(2,1)S(1)}, bf16[256,256]{1,0:T(8,128)(2,1)S(1)}, u32[]{:S(2)}, u32[]{:S(2)}) collective-permute-start(bf16[256,256]{1,0:T(8,128)(2,1)S(1)} %third.1), channel_id=1, source_target_pairs={{0,24},{8,16},{16,8},{24,0},{1,25},{9,17},{17,9},{25,1},{2,26},{10... | collective-permute-start | bytes 393224 | tf_op jit(solution)/shard_map/ppermute | solution.py:317
  6.3 11.2 %collective-permute-start.1 = (bf16[256,256]{1,0:T(8,128)(2,1)S(1)}, bf16[256,256]{1,0:T(8,128)(2,1)S(1)}, u32[]{:S(2)}, u32[]{:S(2)}) collective-permute-start(bf16[256,256]{1,0:T(8,128)(2,1)S(1)} %broadcast_select_fusion), channel_id=1, source_target_pairs={{0,8},{8,0},{16,24},{24,16},{1,9},{9,1},{17,25},{25,17},{2,10},{10... | collective-permute-start | bytes 393224 | tf_op jit(solution)/shard_map/ppermute | solution.py:317
  17.6 9.5 %collective-permute-start.6 = (bf16[3,256,256]{2,1,0:T(8,128)(2,1)S(1)}, bf16[3,256,256]{2,1,0:T(8,128)(2,1)S(1)}, u32[]{:S(2)}, u32[]{:S(2)}) collective-permute-start(bf16[3,256,256]{2,1,0:T(8,128)(2,1)S(1)} %stack.1.own0), channel_id=1, source_target_pairs={{0,2},{1,3},{2,0},{3,1},{4,6},{5,7},{6,4},{7,5},{8,10},{9,11},{10,... | collective-permute-start | bytes 1179656 | tf_op jit(solution)/shard_map/ppermute | solution.py:323
  18.9 10.4 %collective-permute-start.8 = (bf16[3,256,256]{2,1,0:T(8,128)(2,1)S(1)}, bf16[3,256,256]{2,1,0:T(8,128)(2,1)S(1)}, u32[]{:S(2)}, u32[]{:S(2)}) collective-permute-start(bf16[3,256,256]{2,1,0:T(8,128)(2,1)S(1)} %stack.1.own0), channel_id=1, source_target_pairs={{0,4},{4,0},{1,5},{5,1},{2,6},{6,2},{3,7},{7,3},{8,12},{12,8},{9,1... | collective-permute-start | bytes 1179656 | tf_op jit(solution)/shard_map/ppermute | solution.py:320
  20.1 11.7 %collective-permute-start.4 = (bf16[256,1024]{1,0:T(8,128)(2,1)S(1)}, bf16[256,1024]{1,0:T(8,128)(2,1)S(1)}, u32[]{:S(2)}, u32[]{:S(2)}) collective-permute-start(bf16[256,1024]{1,0:T(8,128)(2,1)S(1)} %collective-permute-done.3.near), channel_id=1, source_target_pairs={{0,1},{1,0},{2,3},{3,2},{4,5},{5,4},{6,7},{7,6},{8,9},{9,8},{10,11... | collective-permute-start | bytes 1572872 | tf_op jit(solution)/shard_map/ppermute | solution.py:323
  21.8 10.0 %collective-permute-start.5 = (bf16[3,256,256]{2,1,0:T(8,128)(2,1)S(1)}, bf16[3,256,256]{2,1,0:T(8,128)(2,1)S(1)}, u32[]{:S(2)}, u32[]{:S(2)}) collective-permute-start(bf16[3,256,256]{2,1,0:T(8,128)(2,1)S(1)} %stack.1.own0), channel_id=1, source_target_pairs={{0,1},{1,0},{2,3},{3,2},{4,5},{5,4},{6,7},{7,6},{8,9},{9,8},{10,11... | collective-permute-start | bytes 1179656 | tf_op jit(solution)/shard_map/ppermute | solution.py:323
  27.1 4.7 %collective-permute-start.7 = (bf16[3,256,256]{2,1,0:T(8,128)(2,1)S(1)}, bf16[3,256,256]{2,1,0:T(8,128)(2,1)S(1)}, u32[]{:S(2)}, u32[]{:S(2)}) collective-permute-start(bf16[3,256,256]{2,1,0:T(8,128)(2,1)S(1)} %own2.1), channel_id=1, source_target_pairs={{0,1},{1,0},{2,3},{3,2},{4,5},{5,4},{6,7},{7,6},{8,9},{9,8},{10,11... | collective-permute-start | bytes 1179656 | tf_op jit(solution)/shard_map/ppermute | solution.py:323
  29.3 2.6 %collective-permute-start.9 = (bf16[3,256,256]{2,1,0:T(8,128)(2,1)S(1)}, bf16[3,256,256]{2,1,0:T(8,128)(2,1)S(1)}, u32[]{:S(2)}, u32[]{:S(2)}) collective-permute-start(bf16[3,256,256]{2,1,0:T(8,128)(2,1)S(1)} %oth0.1), channel_id=1, source_target_pairs={{0,1},{1,0},{2,3},{3,2},{4,5},{5,4},{6,7},{7,6},{8,9},{9,8},{10,11... | collective-permute-start | bytes 1179656 | tf_op jit(solution)/shard_map/ppermute | solution.py:323
  30.5 7.0 %collective-permute-start.10 = (bf16[3,256,256]{2,1,0:T(8,128)(2,1)S(1)}, bf16[3,256,256]{2,1,0:T(8,128)(2,1)S(1)}, u32[]{:S(2)}, u32[]{:S(2)}) collective-permute-start(bf16[3,256,256]{2,1,0:T(8,128)(2,1)S(1)} %cross.1), channel_id=1, source_target_pairs={{0,2},{1,5},{2,0},{3,7},{4,6},{5,1},{6,4},{7,3},{8,10},{9,13},{10,... | collective-permute-start | bytes 1179656 | tf_op jit(solution)/shard_map/ppermute | solution.py:328
  37.5 2.2 %collective-permute-start.11 = (bf16[3,256,256]{2,1,0:T(8,128)(2,1)S(1)}, bf16[3,256,256]{2,1,0:T(8,128)(2,1)S(1)}, u32[]{:S(2)}, u32[]{:S(2)}) collective-permute-start(bf16[3,256,256]{2,1,0:T(8,128)(2,1)S(1)} %collective-permute-done.10.oth2), channel_id=1, source_target_pairs={{0,1},{1,0},{2,3},{3,2},{4,5},{5,4},{6,7},{7,6},{8,9},{9,8},{10,11... | collective-permute-start | bytes 1179656 | tf_op jit(solution)/shard_map/ppermute | solution.py:323
